TPU v7x, 32 devices: a whole 2x2x4 slice. The times are simulated.
32 devices in a mesh: dp: 8 (over z, core), tensor: 4 (over y, x).
Axes of the slice: x: 2, y: 2, z: 4, core: 2. Of those that a mesh axis runs over, the one named last changes fastest.
Arguments:
- block_in: bfloat16 [16384, 1536], P(('dp', 'tensor')), may hold values from -6 to 6
- cond_tokens: bfloat16 [16, 130, 768], P('dp'), may hold values from -6 to 6
- cond_count: int32 [16], P('dp'), may hold values from 65 to 130, as said below
- norm1_gain: bfloat16 [1536], P('dp'), may hold values from 0.25 to 1.75
- norm2_gain: bfloat16 [1536], P('dp'), may hold values from 0.25 to 1.75
- norm3_gain: bfloat16 [1536], P('dp'), may hold values from 0.25 to 1.75
- qkv_weight: bfloat16 [1536, 3, 1536], P('dp', None, 'tensor'), may hold values from -0.15625 to 0.15625
- attn_out_weight: bfloat16 [1536, 1536], P('tensor', 'dp'), may hold values from -0.625 to 0.625
- cross_q_weight: bfloat16 [1536, 1536], P('dp', 'tensor'), may hold values from -0.15625 to 0.15625
- cross_kv_weight: bfloat16 [768, 2, 1536], P('dp', None, 'tensor'), may hold values from -0.21875 to 0.21875
- cross_out_weight: bfloat16 [1536, 1536], P('tensor', 'dp'), may hold values from -0.4375 to 0.4375
- gate_up_weight: bfloat16 [1536, 2, 6144], P('dp', None, 'tensor'), may hold values from -0.15625 to 0.15625
- down_weight: bfloat16 [6144, 1536], P('tensor', 'dp'), may hold values from -0.15625 to 0.15625
- out_cotangent: bfloat16 [16384, 1536], P(('dp', 'tensor')), may hold values from -6 to 6
Outputs:
- block_out: bfloat16 [16384, 1536], P(('dp', 'tensor'))
- grad_in: float32 [16384, 1536], P(('dp', 'tensor'))
- grad_cond: float32 [16, 130, 768], P('dp', None, 'tensor')
- grad_norm1: float32 [1536], P('dp')
- grad_norm2: float32 [1536], P('dp')
- grad_norm3: float32 [1536], P('dp')
- grad_qkv: float32 [1536, 3, 1536], P('dp', None, 'tensor')
- grad_attn_out: float32 [1536, 1536], P('tensor', 'dp')
- grad_cross_q: float32 [1536, 1536], P('dp', 'tensor')
- grad_cross_kv: float32 [768, 2, 1536], P('dp', None, 'tensor')
- grad_cross_out: float32 [1536, 1536], P('tensor', 'dp')
- grad_gate_up: float32 [1536, 2, 6144], P('dp', None, 'tensor')
- grad_down: float32 [6144, 1536], P('tensor', 'dp')
Inputs may be any that keep to these rules, and one draw needn't show every extreme that they name: `cond_count`: in every draw one sequence has all 130 slots valid and another exactly 65.
All inputs are finite; a program needn't handle non-finite values.
Results may differ from a plain program's by a relative error of at most 0.024.
Values may be sent and summed in bfloat16 or wider, within the bound.
A program may use at most 320 MiB of HBM per device.

v0:
```python
import jax
import jax.numpy as jnp
from jax import lax
from jax.sharding import PartitionSpec as P

HD = 64


EPSILON = 1e-05
MASKED_SCORE = -1e30


def layer_norm(values, gain):
    centre = values - jnp.mean(values, axis=-1, keepdims=True)
    spread = jnp.mean(centre * centre, axis=-1, keepdims=True)
    return centre * lax.rsqrt(spread + EPSILON) * gain


def rotate(values, cosine, sine):
    quarter = cosine.shape[-1]
    first_part = values[..., :quarter]
    second_part = values[..., quarter : 2 * quarter]
    rest_part = values[..., 2 * quarter :]
    return jnp.concatenate(
        [
            first_part * cosine - second_part * sine,
            first_part * sine + second_part * cosine,
            rest_part,
        ],
        axis=-1,
    )


def rotate_back(grads, cosine, sine):
    quarter = cosine.shape[-1]
    first_part = grads[..., :quarter]
    second_part = grads[..., quarter : 2 * quarter]
    rest_part = grads[..., 2 * quarter :]
    return jnp.concatenate(
        [
            first_part * cosine + second_part * sine,
            second_part * cosine - first_part * sine,
            rest_part,
        ],
        axis=-1,
    )


def gated(gate_vals, up_vals):
    return jax.nn.silu(gate_vals) * up_vals


def rows_by_rows(left, right):
    return lax.dot_general(
        left, right, (((0,), (0,)), ((), ())), preferred_element_type=jnp.float32
    )


def times_transposed(left, right):
    return lax.dot_general(
        left, right, (((1,), (1,)), ((), ())), preferred_element_type=jnp.float32
    )


def attend_forward(query_rows, key_rows, value_rows, allowed):
    scores = jnp.einsum("qhd,khd->hqk", query_rows, key_rows, preferred_element_type=jnp.float32)
    scores = jnp.where(allowed[None, None, :], scores, MASKED_SCORE)
    top_score = jnp.max(scores, axis=-1, keepdims=True)
    weights = jnp.exp(scores - top_score)
    totals = jnp.sum(weights, axis=-1, keepdims=True)
    probs = weights / totals
    mixed = jnp.einsum(
        "hqk,khd->qhd", probs.astype(jnp.bfloat16), value_rows, preferred_element_type=jnp.float32
    )
    return (mixed.astype(jnp.bfloat16), top_score + jnp.log(totals))


def attend_backward(query_rows, key_rows, value_rows, allowed, log_total, grad_mixed):
    scores = jnp.einsum("qhd,khd->hqk", query_rows, key_rows, preferred_element_type=jnp.float32)
    scores = jnp.where(allowed[None, None, :], scores, MASKED_SCORE)
    probs = jnp.exp(scores - log_total)
    grad_probs = jnp.einsum(
        "qhd,khd->hqk", grad_mixed, value_rows, preferred_element_type=jnp.float32
    )
    grad_values = jnp.einsum(
        "hqk,qhd->khd", probs.astype(jnp.bfloat16), grad_mixed, preferred_element_type=jnp.float32
    )
    grad_scores = probs * (grad_probs - jnp.sum(probs * grad_probs, axis=-1, keepdims=True))
    grad_scores = grad_scores.astype(jnp.bfloat16)
    grad_query = jnp.einsum(
        "hqk,khd->qhd", grad_scores, key_rows, preferred_element_type=jnp.float32
    )
    grad_keys = jnp.einsum(
        "hqk,qhd->khd", grad_scores, query_rows, preferred_element_type=jnp.float32
    )
    return (grad_query, grad_keys, grad_values)


def body(
    block_in,
    cond_tokens,
    cond_count,
    norm1_gain,
    norm2_gain,
    norm3_gain,
    qkv_weight,
    attn_out_weight,
    cross_q_weight,
    cross_kv_weight,
    cross_out_weight,
    gate_up_weight,
    down_weight,
    out_cotangent,
):
    local_rows = block_in.shape[0]
    model_width = block_in.shape[1]
    group_rows = local_rows * lax.axis_size("tensor")
    seq_here = cond_tokens.shape[0]
    seq_length = group_rows // seq_here
    cond_slots = cond_tokens.shape[1]
    cond_width = cond_tokens.shape[2]
    head_cols = attn_out_weight.shape[0]
    heads_here = head_cols // HD
    hidden_here = down_weight.shape[0]
    gain_one, gain_two, gain_three, w_qkv, w_out, w_cq, w_ckv, w_co, w_gu, w_down = (
        lax.all_gather(norm1_gain, "dp", axis=0, tiled=True),
        lax.all_gather(norm2_gain, "dp", axis=0, tiled=True),
        lax.all_gather(norm3_gain, "dp", axis=0, tiled=True),
        lax.all_gather(qkv_weight, "dp", axis=0, tiled=True),
        lax.all_gather(attn_out_weight, "dp", axis=1, tiled=True),
        lax.all_gather(cross_q_weight, "dp", axis=0, tiled=True),
        lax.all_gather(cross_kv_weight, "dp", axis=0, tiled=True),
        lax.all_gather(cross_out_weight, "dp", axis=1, tiled=True),
        lax.all_gather(gate_up_weight, "dp", axis=0, tiled=True),
        lax.all_gather(down_weight, "dp", axis=1, tiled=True),
    )
    quarter = HD // 4
    positions = (jnp.arange(group_rows) % seq_length).astype(jnp.float32)
    inverse = 10000.0 ** (-jnp.arange(quarter).astype(jnp.float32) / quarter)
    angle_grid = positions[:, None] * inverse[None, :]
    cosine = jnp.cos(angle_grid)[:, None, :]
    sine = jnp.sin(angle_grid)[:, None, :]
    every_key = jnp.ones((seq_length,), dtype=jnp.bool_)
    valid_slots = jnp.arange(cond_slots)[None, :] < cond_count[:, None]

    def by_sequence(array):
        return array.reshape((seq_here, seq_length) + array.shape[1:])

    def spread_rows(local_part):
        return lax.all_gather(local_part, "tensor", axis=0, tiled=True)

    def project_out(mixed_all, weight):
        return lax.psum_scatter(
            jnp.dot(mixed_all, weight, preferred_element_type=jnp.float32),
            "tensor",
            scatter_dimension=0,
            tiled=True,
        )

    def spread_grads(local_part):
        return lax.all_gather(local_part, "tensor", axis=0, tiled=True)

    def gather_back(grad_all, weight):
        return lax.psum_scatter(
            times_transposed(grad_all, weight), "tensor", scatter_dimension=0, tiled=True
        )

    def self_forward(seq_parts):
        return attend_forward(seq_parts[0], seq_parts[1], seq_parts[2], every_key)

    def cross_forward(seq_parts):
        return attend_forward(seq_parts[0], seq_parts[1][:, 0], seq_parts[1][:, 1], seq_parts[2])

    def self_backward(seq_parts):
        return attend_backward(
            seq_parts[0], seq_parts[1], seq_parts[2], every_key, seq_parts[3], seq_parts[4]
        )

    def cross_backward(seq_parts):
        return attend_backward(
            seq_parts[0],
            seq_parts[1][:, 0],
            seq_parts[1][:, 1],
            seq_parts[2],
            seq_parts[3],
            seq_parts[4],
        )

    gain_first = gain_one.astype(jnp.float32)
    gain_second = gain_two.astype(jnp.float32)
    gain_third = gain_three.astype(jnp.float32)
    input_rows = block_in.astype(jnp.float32)
    first_all = spread_rows(layer_norm(input_rows, gain_first).astype(jnp.bfloat16))
    qkv_all = jnp.dot(
        first_all, w_qkv.reshape(model_width, 3 * head_cols), preferred_element_type=jnp.float32
    )
    qkv_all = qkv_all.reshape(group_rows, 3, heads_here, HD)
    query_rot = (rotate(qkv_all[:, 0], cosine, sine) * 0.125).astype(jnp.bfloat16)
    key_rot = rotate(qkv_all[:, 1], cosine, sine).astype(jnp.bfloat16)
    value_rows = qkv_all[:, 2].astype(jnp.bfloat16)
    self_mixed, self_lse = lax.map(
        self_forward, (by_sequence(query_rot), by_sequence(key_rot), by_sequence(value_rows))
    )
    self_flat = self_mixed.reshape(group_rows, head_cols)
    after_self = input_rows + project_out(self_flat, w_out)
    second_all = spread_rows(layer_norm(after_self, gain_second).astype(jnp.bfloat16))
    cross_query = (jnp.dot(second_all, w_cq, preferred_element_type=jnp.float32) * 0.125).astype(
        jnp.bfloat16
    )
    cross_query = cross_query.reshape(group_rows, heads_here, HD)
    cond_flat = cond_tokens.reshape(seq_here * cond_slots, cond_width)
    cross_kv = jnp.dot(
        cond_flat, w_ckv.reshape(cond_width, 2 * head_cols), preferred_element_type=jnp.float32
    )
    cross_kv = cross_kv.astype(jnp.bfloat16).reshape(seq_here, cond_slots, 2, heads_here, HD)
    cross_mixed, cross_lse = lax.map(
        cross_forward, (by_sequence(cross_query), cross_kv, valid_slots)
    )
    cross_flat = cross_mixed.reshape(group_rows, head_cols)
    after_cross = after_self + project_out(cross_flat, w_co)
    third_all = spread_rows(layer_norm(after_cross, gain_third).astype(jnp.bfloat16))
    gate_up = jnp.dot(
        third_all, w_gu.reshape(model_width, 2 * hidden_here), preferred_element_type=jnp.float32
    )
    gate_up = gate_up.reshape(group_rows, 2, hidden_here)
    gate_vals = gate_up[:, 0]
    up_vals = gate_up[:, 1]
    hidden = gated(gate_vals, up_vals).astype(jnp.bfloat16)
    block_out = (after_cross + project_out(hidden, w_down)).astype(jnp.bfloat16)
    gain_one, gain_two, gain_three, w_qkv, w_out, w_cq, w_ckv, w_co, w_gu, w_down = (
        lax.all_gather(norm1_gain, "dp", axis=0, tiled=True),
        lax.all_gather(norm2_gain, "dp", axis=0, tiled=True),
        lax.all_gather(norm3_gain, "dp", axis=0, tiled=True),
        lax.all_gather(qkv_weight, "dp", axis=0, tiled=True),
        lax.all_gather(attn_out_weight, "dp", axis=1, tiled=True),
        lax.all_gather(cross_q_weight, "dp", axis=0, tiled=True),
        lax.all_gather(cross_kv_weight, "dp", axis=0, tiled=True),
        lax.all_gather(cross_out_weight, "dp", axis=1, tiled=True),
        lax.all_gather(gate_up_weight, "dp", axis=0, tiled=True),
        lax.all_gather(down_weight, "dp", axis=1, tiled=True),
    )
    gain_first = gain_one.astype(jnp.float32)
    gain_second = gain_two.astype(jnp.float32)
    gain_third = gain_three.astype(jnp.float32)
    grad_top = out_cotangent.astype(jnp.float32)
    third_grads = spread_grads(out_cotangent)
    grad_hidden = times_transposed(third_grads, w_down)
    grad_down = rows_by_rows(hidden, third_grads)
    gated_out, gated_pull = jax.vjp(gated, gate_vals, up_vals)
    grad_gate, grad_up = gated_pull(grad_hidden)
    grad_gate_up = (
        jnp.stack([grad_gate, grad_up], axis=1)
        .astype(jnp.bfloat16)
        .reshape(group_rows, 2 * hidden_here)
    )
    grad_gu_weight = rows_by_rows(third_all, grad_gate_up).reshape(model_width, 2, hidden_here)
    grad_third = gather_back(grad_gate_up, w_gu.reshape(model_width, 2 * hidden_here))
    norm_out, norm_pull = jax.vjp(layer_norm, after_cross, gain_third)
    part_rows, grad_gain_third = norm_pull(grad_third)
    grad_cross_rows = grad_top + part_rows
    second_grads = spread_grads(grad_cross_rows.astype(jnp.bfloat16))
    grad_cross_mixed = times_transposed(second_grads, w_co).astype(jnp.bfloat16)
    grad_co_weight = rows_by_rows(cross_flat, second_grads)
    cross_gq, cross_gk, cross_gv = lax.map(
        cross_backward,
        (
            by_sequence(cross_query),
            cross_kv,
            valid_slots,
            cross_lse,
            by_sequence(grad_cross_mixed.reshape(group_rows, heads_here, HD)),
        ),
    )
    grad_cross_query = (cross_gq * 0.125).astype(jnp.bfloat16).reshape(group_rows, head_cols)
    grad_cross_kv = (
        jnp.stack([cross_gk, cross_gv], axis=2)
        .astype(jnp.bfloat16)
        .reshape(seq_here * cond_slots, 2 * head_cols)
    )
    grad_cq_weight = rows_by_rows(second_all, grad_cross_query)
    grad_ckv_weight = rows_by_rows(cond_flat, grad_cross_kv).reshape(cond_width, 2, head_cols)
    cond_partial = times_transposed(
        grad_cross_kv, w_ckv.reshape(cond_width, 2 * head_cols)
    ).reshape(seq_here, cond_slots, cond_width)
    grad_cond = lax.psum_scatter(cond_partial, "tensor", scatter_dimension=2, tiled=True)
    grad_second = gather_back(grad_cross_query, w_cq)
    norm_out, norm_pull = jax.vjp(layer_norm, after_self, gain_second)
    part_rows, grad_gain_second = norm_pull(grad_second)
    grad_self_rows = grad_cross_rows + part_rows
    first_grads = spread_grads(grad_self_rows.astype(jnp.bfloat16))
    grad_self_mixed = times_transposed(first_grads, w_out).astype(jnp.bfloat16)
    grad_out_weight = rows_by_rows(self_flat, first_grads)
    self_gq, self_gk, self_gv = lax.map(
        self_backward,
        (
            by_sequence(query_rot),
            by_sequence(key_rot),
            by_sequence(value_rows),
            self_lse,
            by_sequence(grad_self_mixed.reshape(group_rows, heads_here, HD)),
        ),
    )
    grad_query = rotate_back(self_gq.reshape(group_rows, heads_here, HD) * 0.125, cosine, sine)
    grad_keys = rotate_back(self_gk.reshape(group_rows, heads_here, HD), cosine, sine)
    grad_values = self_gv.reshape(group_rows, heads_here, HD)
    grad_qkv_all = (
        jnp.stack([grad_query, grad_keys, grad_values], axis=1)
        .astype(jnp.bfloat16)
        .reshape(group_rows, 3 * head_cols)
    )
    grad_qkv_weight = rows_by_rows(first_all, grad_qkv_all).reshape(model_width, 3, head_cols)
    grad_first = gather_back(grad_qkv_all, w_qkv.reshape(model_width, 3 * head_cols))
    norm_out, norm_pull = jax.vjp(layer_norm, input_rows, gain_first)
    part_rows, grad_gain_first = norm_pull(grad_first)
    grad_input = grad_self_rows + part_rows
    owned = (
        lax.psum_scatter(grad_gain_first, "dp", scatter_dimension=0, tiled=True),
        lax.psum_scatter(grad_gain_second, "dp", scatter_dimension=0, tiled=True),
        lax.psum_scatter(grad_gain_third, "dp", scatter_dimension=0, tiled=True),
        lax.psum_scatter(grad_qkv_weight, "dp", scatter_dimension=0, tiled=True),
        lax.psum_scatter(grad_out_weight, "dp", scatter_dimension=1, tiled=True),
        lax.psum_scatter(grad_cq_weight, "dp", scatter_dimension=0, tiled=True),
        lax.psum_scatter(grad_ckv_weight, "dp", scatter_dimension=0, tiled=True),
        lax.psum_scatter(grad_co_weight, "dp", scatter_dimension=1, tiled=True),
        lax.psum_scatter(grad_gu_weight, "dp", scatter_dimension=0, tiled=True),
        lax.psum_scatter(grad_down, "dp", scatter_dimension=1, tiled=True),
    )
    gain_grads = lax.psum((owned[0], owned[1], owned[2]), "tensor")
    return (
        block_out,
        grad_input,
        grad_cond,
        gain_grads[0],
        gain_grads[1],
        gain_grads[2],
        owned[3],
        owned[4],
        owned[5],
        owned[6],
        owned[7],
        owned[8],
        owned[9],
    )


def solution(mesh):
    return jax.shard_map(
        body,
        mesh=mesh,
        in_specs=(
            P(("dp", "tensor"), None),
            P("dp", None, None),
            P("dp"),
            P("dp"),
            P("dp"),
            P("dp"),
            P("dp", None, "tensor"),
            P("tensor", "dp"),
            P("dp", "tensor"),
            P("dp", None, "tensor"),
            P("tensor", "dp"),
            P("dp", None, "tensor"),
            P("tensor", "dp"),
            P(("dp", "tensor"), None),
        ),
        out_specs=(
            P(("dp", "tensor"), None),
            P(("dp", "tensor"), None),
            P("dp", None, "tensor"),
            P("dp"),
            P("dp"),
            P("dp"),
            P("dp", None, "tensor"),
            P("tensor", "dp"),
            P("dp", "tensor"),
            P("dp", None, "tensor"),
            P("tensor", "dp"),
            P("dp", None, "tensor"),
            P("tensor", "dp"),
        ),
        check_vma=False,
    )
```

profile of v0, /device:TPU:0, one launch (start us, length us, event | category | flops | bytes accessed | tf_op | source)
XLA Modules:
  0.0 2242.6 jit_solution(11685545461042360764)
XLA Ops:
  12.5 31.4 %all-reduce.9 = (bf16[1536]{0:T(1024)(128)(2,1)S(1)}, bf16[1536]{0:T(1024)(128)(2,1)}, bf16[1536]{0:T(1024)(128)(2,1)}) all-reduce(bf16[1536]{0:T(1024)(128)(2,1)S(1)} %dynamic-update-slice, bf16[1536]{0:T(1024)(128)(2,1)S(1)} %dynamic-update-slice.1, bf16[1536]{0:T(1024)(128)(2,1)S(1)} %dynamic-update-slice.2), channel_id=1, replica_groups=mesh['dp'=8,'tensor'=4] {'dp'}, use_global_device_ids=true, to_apply=%add | all-reduce | flops 4608 | bytes 18432
  58.9 66.9 %all-gather.14.cloned.1.call-done = bf16[2048,1536]{1,0:T(8,128)(2,1)} async-done(((bf16[512,1536]{1,0:T(8,128)(2,1)}), bf16[2048,1536]{1,0:T(8,128)(2,1)}) %all-gather.14.cloned.1.call-update) | async-done | bytes 6291472 | tf_op jit(solution)/shard_map/all_gather | solution.py:150
  125.8 9.7 fusion.88
  153.1 57.3 %while.52 = (s32[]{:T(128)}, bf16[2,1024,6,64]{1,3,2,0:T(8,128)(2,1)}, f32[2,6,1024,1]{2,1,3,0:T(8,128)S(1)}, bf16[2,1024,6,64]{1,3,2,0:T(8,128)(2,1)}, bf16[2,1...) while((s32[]{:T(128)}, bf16[2,1024,6,64]{1,3,2,0:T(8,128)(2,1)}, ...), condition=%wide.region_5.6_spmd, body=%wide.region_2.5_spmd.sunk | while | flops 1648748544 | bytes 179529840 | solution.py:201
  157.9 8.3 copy-done
  170.0 11.5 fusion.201
  186.3 8.3 copy-done
  198.3 11.5 fusion.201
  213.9 8.3 fusion.123
  223.5 119.7 %reduce-scatter.16.cloned.1.call-done = f32[512,1536]{1,0:T(8,128)} async-done(((f32[2048,1536]{1,0:T(8,128)}), f32[512,1536]{1,0:T(8,128)}) %reduce-scatter.16.cloned.1.call-update) | async-done | bytes 3145744 | tf_op jit(solution)/shard_map/reduce_scatter | solution.py:153
  349.8 17.5 all-gather.20.cloned.1.call-done
  371.1 20.2 all-gather.24.cloned.1.call-done
  391.2 72.4 %all-gather.22.cloned.1.call-done = bf16[2048,1536]{1,0:T(8,128)(2,1)} async-done(((bf16[512,1536]{1,0:T(8,128)(2,1)}), bf16[2048,1536]{1,0:T(8,128)(2,1)}) %all-gather.22.cloned.1.call-update) | async-done | bytes 6291472 | tf_op jit(solution)/shard_map/all_gather | solution.py:150
  463.6 7.7 multiply_convert_fusion.5
  478.6 7.3 while.53
  491.5 9.7 fusion.124
  504.2 118.0 %reduce-scatter.18.cloned.1.call-done = f32[512,1536]{1,0:T(8,128)} async-done(((f32[2048,1536]{1,0:T(8,128)}), f32[512,1536]{1,0:T(8,128)}) %reduce-scatter.18.cloned.1.call-update) | async-done | bytes 3145744 | tf_op jit(solution)/shard_map/reduce_scatter | solution.py:153
  629.2 85.7 %all-gather.30.cloned.1.call-done = bf16[1536,2,1536]{2,0,1:T(8,128)(2,1)} async-done(((bf16[192,2,1536]{2,0,1:T(8,128)(2,1)}), bf16[1536,2,1536]{2,0,1:T(8,128)(2,1)}) %all-gather.30.cloned.1.call-update) | async-done | bytes 9437200 | tf_op jit(solution)/shard_map/all_gather | solution.py:134
  715.0 12.9 copy.116
  727.9 58.1 %all-gather.28.cloned.1.call-done = bf16[2048,1536]{1,0:T(8,128)(2,1)} async-done(((bf16[512,1536]{1,0:T(8,128)(2,1)}), bf16[2048,1536]{1,0:T(8,128)(2,1)}) %all-gather.28.cloned.1.call-update) | async-done | bytes 6291472 | tf_op jit(solution)/shard_map/all_gather | solution.py:150
  786.0 26.4 %fusion.86 = f32[2048,2,1536]{0,2,1:T(8,128)} fusion(bf16[1536,2,1536]{0,2,1:T(8,128)(2,1)} %copy.116, bf16[2048,1536]{1,0:T(8,128)(2,1)} %all-gather.28.cloned.1.call-done), kind=kOutput, calls=%fused_computation.113 | convolution fusion | flops 19327352832 | bytes 40894464 | tf_op jit(solution)/shard_map/dot_general | solution.py:222
  812.5 26.8 %all-gather.32.cloned.1.call-done = bf16[1536,1536]{0,1:T(8,128)(2,1)} async-done(((bf16[1536,192]{0,1:T(8,128)(2,1)}), bf16[1536,1536]{0,1:T(8,128)(2,1)}) %all-gather.32.cloned.1.call-update) | async-done | bytes 4718608 | tf_op jit(solution)/shard_map/all_gather | solution.py:135
  839.3 70.8 %all-gather.34.cloned.1.call-done = bf16[2048,1536]{1,0:T(8,128)(2,1)} async-done(((bf16[512,1536]{1,0:T(8,128)(2,1)}), bf16[2048,1536]{1,0:T(8,128)(2,1)}) %all-gather.34.cloned.1.call-update) | async-done | bytes 6291472 | tf_op jit(solution)/shard_map/all_gather | solution.py:161
  910.1 24.4 %fusion.82 = (bf16[2048,1,1536]{0,2,1:T(8,128)(2,1)}, bf16[2048,1,1536]{0,2,1:T(8,128)(2,1)}) fusion(f32[2048,2,1536]{0,2,1:T(8,128)} %fusion.86, bf16[2048,1536]{1,0:T(8,128)(2,1)} %all-gather.34.cloned.1.call-done, bf16[1536,1536]{0,1:T(8,128)(2,1)} %all-gather.32.cloned.1.call-done), kind=kOutput, calls=%fused_computation.103 | convolution fusion | flops 9707716608 | bytes 48758784 | tf_op jit(solution)/shard_map/dot_general | solution.py:60
  934.6 27.3 %convolution_bitcast_fusion.2 = f32[2048,1536]{1,0:T(8,128)} fusion(bf16[1536,2,1536]{2,0,1:T(8,128)(2,1)} %all-gather.30.cloned.1.call-done, bf16[2048,1,1536]{0,2,1:T(8,128)(2,1)} %get-tuple-element.408, bf16[2048,1,1536]{0,2,1:T(8,128)(2,1)} %get-tuple-element.407), kind=kOutput, calls=%fused_computation.115 | convolution fusion | flops 19333644288 | bytes 34603008 | tf_op jit(solution)/shard_map/dot_general | solution.py:60
  961.9 10.8 multiply_convert_fusion.2
  975.3 15.3 fusion.125
  990.9 91.9 %reduce-scatter.22.cloned.1.call-done = f32[512,1536]{1,0:T(8,128)} async-done(((f32[2048,1536]{1,0:T(8,128)}), f32[512,1536]{1,0:T(8,128)}) %reduce-scatter.22.cloned.1.call-update) | async-done | bytes 3145744 | tf_op jit(solution)/shard_map/reduce_scatter | solution.py:164
  1086.1 120.3 %reduce-scatter.20.cloned.1.call-done = f32[512,1536]{1,0:T(8,128)} async-done(((f32[2048,1536]{1,0:T(8,128)}), f32[512,1536]{1,0:T(8,128)}) %reduce-scatter.20.cloned.1.call-update) | async-done | bytes 3145744 | tf_op jit(solution)/shard_map/reduce_scatter | solution.py:153
  1214.2 70.2 %all-gather.36.cloned.1.call-done = bf16[2048,1536]{1,0:T(8,128)(2,1)} async-done(((bf16[512,1536]{1,0:T(8,128)(2,1)}), bf16[2048,1536]{1,0:T(8,128)(2,1)}) %all-gather.36.cloned.1.call-update) | async-done | bytes 6291472 | tf_op jit(solution)/shard_map/all_gather | solution.py:161
  1284.5 6.2 convolution_convert_fusion.1
  1299.1 14.8 while.54
  1319.8 6.5 fusion.126
  1326.6 120.6 %reduce-scatter.24.cloned.1.call-done = f32[512,1536]{1,0:T(8,128)} async-done(((f32[2048,1536]{1,0:T(8,128)}), f32[512,1536]{1,0:T(8,128)}) %reduce-scatter.24.cloned.1.call-update) | async-done | bytes 3145744 | tf_op jit(solution)/shard_map/reduce_scatter | solution.py:164
  1473.2 27.2 %fusion.83 = f32[1536,2,1536]{2,0,1:T(8,128)} fusion(bf16[2048,1536]{1,0:T(8,128)(2,1)} %all-gather.28.cloned.1.call-done, bf16[2048,1,1536]{0,2,1:T(8,128)(2,1)} %get-tuple-element.408, bf16[2048,1,1536]{0,2,1:T(8,128)(2,1)} %get-tuple-element.407), kind=kOutput, calls=%fused_computation.106 | convolution fusion | flops 19352518656 | bytes 37748736 | tf_op jit(solution)/shard_map/dot_general | solution.py:54
  1500.5 25.8 %all-gather.38.cloned.1.call-done = bf16[2048,1536]{1,0:T(8,128)(2,1)} async-done(((bf16[512,1536]{1,0:T(8,128)(2,1)}), bf16[2048,1536]{1,0:T(8,128)(2,1)}) %all-gather.38.cloned.1.call-update) | async-done | bytes 6291472 | tf_op jit(solution)/shard_map/all_gather | solution.py:161
  1526.3 6.2 convolution_convert_fusion
  1537.0 251.9 %while.55 = (s32[]{:T(128)}, f32[2,1024,6,64]{1,3,2,0:T(8,128)}, f32[2,1024,6,64]{1,0,3,2:T(2,128)}, bf16[2,1024,6,64]{1,0,3,2:T(2,128)(2,1)}, bf16[2,1024,6,64]...) while((s32[]{:T(128)}, f32[2,1024,6,64]{1,3,2,0:T(8,128)}, ...), condition=%wide.region_28.29_spmd, body=%wide.region_26.28_spmd.sunk | while | flops 4083148800 | bytes 226684112 | solution.py:293
  1537.2 14.0 fusion.221
  1551.1 10.5 fusion.222
  1562.9 25.9 %dynamic_update_slice.61 = bf16[2,1024,6,64]{1,0,3,2:T(2,128)(2,1)} dynamic-update-slice(bf16[2,1024,6,64]{1,0,3,2:T(2,128)(2,1)} %get-tuple-element.716, bf16[1,1024,6,64]{1,0,3,2:T(2,128)(2,1)S(1)} %copy.191, s32[]{:T(128)S(6)} %copy.241, s32[]{:T(128)} %constant.118.clone.1..sunk, s32[]{:T(128)} %constant.118.clone.1..sunk, s32[]{:T(128)} %constant.118.clone.1..sunk) | dynamic-update-slice | bytes 1572868 | tf_op jit(solution)/shard_map/while/body/jit(dynamic_update_index_in_dim)/dynamic_update_slice | solution.py:264
  1588.8 15.9 multiply_reduce_fusion.11
  1604.7 17.4 multiply_convert_fusion.10
  1634.6 27.8 %dynamic_update_slice.60 = f32[2,1024,6,64]{1,0,3,2:T(2,128)} dynamic-update-slice(f32[2,1024,6,64]{1,0,3,2:T(2,128)} %get-tuple-element.715, f32[1,1024,6,64]{1,0,3,2:T(1,128)} %copy.190, s32[]{:T(128)S(6)} %copy.241, s32[]{:T(128)} %constant.118.clone.1..sunk, s32[]{:T(128)} %constant.118.clone.1..sunk, s32[]{:T(128)} %constant.118.clone.1..sunk) | dynamic-update-slice | bytes 3145732 | tf_op jit(solution)/shard_map/while/body/jit(dynamic_update_index_in_dim)/dynamic_update_slice | solution.py:264
  1662.3 14.0 fusion.221
  1676.3 10.6 fusion.222
  1688.2 25.9 %dynamic_update_slice.61 = bf16[2,1024,6,64]{1,0,3,2:T(2,128)(2,1)} dynamic-update-slice(bf16[2,1024,6,64]{1,0,3,2:T(2,128)(2,1)} %get-tuple-element.716, bf16[1,1024,6,64]{1,0,3,2:T(2,128)(2,1)S(1)} %copy.191, s32[]{:T(128)S(6)} %copy.241, s32[]{:T(128)} %constant.118.clone.1..sunk, s32[]{:T(128)} %constant.118.clone.1..sunk, s32[]{:T(128)} %constant.118.clone.1..sunk) | dynamic-update-slice | bytes 1572868 | tf_op jit(solution)/shard_map/while/body/jit(dynamic_update_index_in_dim)/dynamic_update_slice | solution.py:264
  1714.0 17.1 multiply_reduce_fusion.11
  1731.2 17.3 multiply_convert_fusion.10
  1760.9 27.8 %dynamic_update_slice.60 = f32[2,1024,6,64]{1,0,3,2:T(2,128)} dynamic-update-slice(f32[2,1024,6,64]{1,0,3,2:T(2,128)} %get-tuple-element.715, f32[1,1024,6,64]{1,0,3,2:T(1,128)} %copy.190, s32[]{:T(128)S(6)} %copy.241, s32[]{:T(128)} %constant.118.clone.1..sunk, s32[]{:T(128)} %constant.118.clone.1..sunk, s32[]{:T(128)} %constant.118.clone.1..sunk) | dynamic-update-slice | bytes 3145732 | tf_op jit(solution)/shard_map/while/body/jit(dynamic_update_index_in_dim)/dynamic_update_slice | solution.py:264
  1807.4 11.1 fusion.127
  1818.6 15.6 fusion.133
  1835.7 8.0 fusion.132
  1843.8 8.2 fusion.130
  1852.0 8.0 fusion.129
  1860.3 13.5 fusion.90
  1884.3 55.0 %reduce-scatter.26.cloned.1.call-done = f32[512,1536]{1,0:T(8,128)} async-done(((f32[2048,1536]{1,0:T(8,128)}), f32[512,1536]{1,0:T(8,128)}) %reduce-scatter.26.cloned.1.call-update) | async-done | bytes 3145744 | tf_op jit(solution)/shard_map/reduce_scatter | solution.py:164
  1943.6 29.8 %all-reduce.7 = (f32[1536]{0:T(1024)S(1)}, f32[1536]{0:T(1024)S(1)}, f32[1536]{0:T(1024)S(1)}) all-reduce(f32[1536]{0:T(1024)S(1)} %get-tuple-element.320, f32[1536]{0:T(1024)S(1)} %copy-done.77, f32[1536]{0:T(1024)S(1)} %copy-done.76), channel_id=9, replica_groups=mesh['dp'=8,'tensor'=4] {'dp'}, use_global_device_ids=true, to_apply=%region_34.35.clone | all-reduce | flops 4608 | bytes 36864
  1973.6 9.2 all-reduce.8
  1988.7 53.6 %reduce-scatter.38.cloned.1.call-done = f32[1536,192]{0,1:T(8,128)} async-done(((f32[1536,1536]{0,1:T(8,128)}), f32[1536,192]{0,1:T(8,128)}) %reduce-scatter.38.cloned.1.call-update) | async-done | bytes 1179664 | tf_op jit(solution)/shard_map/reduce_scatter | solution.py:326
  2042.3 37.3 %reduce-scatter.34.cloned.1.call-done = f32[384,192]{0,1:T(8,128)} async-done(((f32[384,1536]{0,1:T(8,128)}), f32[384,192]{0,1:T(8,128)}) %reduce-scatter.34.cloned.1.call-update) | async-done | bytes 294928 | tf_op jit(solution)/shard_map/reduce_scatter | solution.py:324
  2079.6 38.4 %reduce-scatter.32.cloned.1.call-done = f32[192,384]{1,0:T(8,128)} async-done(((f32[1536,384]{1,0:T(8,128)}), f32[192,384]{1,0:T(8,128)}) %reduce-scatter.32.cloned.1.call-update) | async-done | bytes 294928 | tf_op jit(solution)/shard_map/reduce_scatter | solution.py:322
  2118.0 38.3 %reduce-scatter.30.cloned.1.call-done = f32[384,192]{0,1:T(8,128)} async-done(((f32[384,1536]{0,1:T(8,128)}), f32[384,192]{0,1:T(8,128)}) %reduce-scatter.30.cloned.1.call-update) | async-done | bytes 294928 | tf_op jit(solution)/shard_map/reduce_scatter | solution.py:321
  2156.3 79.2 %reduce-scatter.28.cloned.1.call-done = f32[192,3,384]{2,0,1:T(8,128)} async-done(((f32[1536,3,384]{2,0,1:T(8,128)}), f32[192,3,384]{2,0,1:T(8,128)}) %reduce-scatter.28.cloned.1.call-update) | async-done | bytes 884752 | tf_op jit(solution)/shard_map/reduce_scatter | solution.py:320
  (419 shorter events, 239.8 us)
Async XLA Ops:
  7.2 38.5 %copy-start.8 = (bf16[512,1536]{1,0:T(8,128)(2,1)S(1)}, bf16[512,1536]{1,0:T(8,128)(2,1)}, u32[]{:S(2)}) copy-start(bf16[512,1536]{1,0:T(8,128)(2,1)} %param.22) | copy-start | bytes 4718596
  7.2 47.2 %all-gather.16.cloned.1.call-start = ((), (), s32[]{:S(2)}) async-start(), calls=%async_computation.14 | async-start | bytes 3981312 | tf_op jit(solution)/shard_map/all_gather | solution.py:129
  7.9 117.9 %all-gather.14.cloned.1.call-start = ((), (), s32[]{:S(2)}) async-start(), calls=%async_computation.13 | async-start | bytes 7864320 | tf_op jit(solution)/shard_map/all_gather | solution.py:150
  49.2 164.8 %all-gather.18.cloned.1.call-start = ((), (), s32[]{:S(2)}) async-start(), calls=%async_computation.15 | async-start | bytes 1327104 | tf_op jit(solution)/shard_map/all_gather | solution.py:130
  49.9 293.2 %reduce-scatter.16.cloned.1.call-start = ((), (), s32[]{:S(2)}) async-start(), calls=%async_computation.16 | async-start | bytes 15728640 | tf_op jit(solution)/shard_map/reduce_scatter | solution.py:153
  58.9 76.5 %copy-start.43 = (bf16[1536,3,384]{0,2,1:T(8,128)(2,1)}, bf16[1536,3,384]{0,2,1:T(8,128)(2,1)S(1)}, u32[]{:S(2)}) copy-start(bf16[1536,3,384]{0,2,1:T(8,128)(2,1)S(1)} %copy.100) | copy-start | bytes 10616836
  157.9 8.3 copy-start
  186.3 8.3 copy-start
  213.9 8.3 copy-start.30
  222.2 120.9 %copy-start.9 = (bf16[512,1536]{1,0:T(8,128)(2,1)S(1)}, bf16[512,1536]{1,0:T(8,128)(2,1)}, u32[]{:S(2)}) copy-start(bf16[512,1536]{1,0:T(8,128)(2,1)} %param.22) | copy-start | bytes 4718596
  222.2 145.1 %all-gather.20.cloned.1.call-start = ((), (), s32[]{:S(2)}) async-start(), calls=%async_computation.17 | async-start | bytes 1327104 | tf_op jit(solution)/shard_map/all_gather | solution.py:132
  222.8 168.4 %all-gather.24.cloned.1.call-start = ((), (), s32[]{:S(2)}) async-start(), calls=%async_computation.19 | async-start | bytes 1327104 | tf_op jit(solution)/shard_map/all_gather | solution.py:131
  223.4 240.2 %all-gather.22.cloned.1.call-start = ((), (), s32[]{:S(2)}) async-start(), calls=%async_computation.18 | async-start | bytes 7864320 | tf_op jit(solution)/shard_map/all_gather | solution.py:150
  223.5 122.4 %copy-start.64 = (f32[1536]{0:T(1024)}, f32[1536]{0:T(1024)S(1)}, u32[]{:S(2)}) copy-start(f32[1536]{0:T(1024)S(1)} %convert_element_type.219) | copy-start | bytes 18436
  348.7 142.8 %all-gather.26.cloned.1.call-start = ((), (), s32[]{:S(2)}) async-start(), calls=%async_computation.20 | async-start | bytes 1327104 | tf_op jit(solution)/shard_map/all_gather | solution.py:133
  349.5 272.7 %reduce-scatter.18.cloned.1.call-start = ((), (), s32[]{:S(2)}) async-start(), calls=%async_computation.21 | async-start | bytes 15728640 | tf_op jit(solution)/shard_map/reduce_scatter | solution.py:153
  349.8 19.0 copy-start.41
  486.0 5.5 copy-start.66
  501.3 120.9 %copy-start.4 = (f32[512,1536]{1,0:T(8,128)S(1)}, f32[512,1536]{1,0:T(8,128)}, u32[]{:S(2)}) copy-start(f32[512,1536]{1,0:T(8,128)} %copy-done.3) | copy-start | bytes 9437188
  501.3 213.7 %all-gather.30.cloned.1.call-start = ((), (), s32[]{:S(2)}) async-start(), calls=%async_computation.23 | async-start | bytes 10616832 | tf_op jit(solution)/shard_map/all_gather | solution.py:134
  504.2 281.9 %all-gather.28.cloned.1.call-start = ((), (), s32[]{:S(2)}) async-start(), calls=%async_computation.22 | async-start | bytes 7864320 | tf_op jit(solution)/shard_map/all_gather | solution.py:150
  627.9 211.4 %all-gather.32.cloned.1.call-start = ((), (), s32[]{:S(2)}) async-start(), calls=%async_computation.24 | async-start | bytes 5308416 | tf_op jit(solution)/shard_map/all_gather | solution.py:135
  628.4 281.7 %all-gather.34.cloned.1.call-start = ((), (), s32[]{:S(2)}) async-start(), calls=%async_computation.26 | async-start | bytes 7864320 | tf_op jit(solution)/shard_map/all_gather | solution.py:161
  629.2 453.5 %reduce-scatter.22.cloned.1.call-start = ((), (), s32[]{:S(2)}) async-start(), calls=%async_computation.27 | async-start | bytes 15728640 | tf_op jit(solution)/shard_map/reduce_scatter | solution.py:164
  961.8 244.6 %reduce-scatter.20.cloned.1.call-start = ((), (), s32[]{:S(2)}) async-start(), calls=%async_computation.25 | async-start | bytes 15728640 | tf_op jit(solution)/shard_map/reduce_scatter | solution.py:153
  990.6 92.1 %copy-start.7 = (f32[512,1536]{1,0:T(8,128)S(1)}, f32[512,1536]{1,0:T(8,128)}, u32[]{:S(2)}) copy-start(f32[512,1536]{1,0:T(8,128)} %copy-done.6) | copy-start | bytes 9437188
  990.6 293.8 %all-gather.36.cloned.1.call-start = ((), (), s32[]{:S(2)}) async-start(), calls=%async_computation.28 | async-start | bytes 7864320 | tf_op jit(solution)/shard_map/all_gather | solution.py:161
  1206.4 6.1 copy-start.19
  1210.8 241.0 %copy-start.78 = (f32[512]{0:T(512)}, f32[512]{0:T(512)S(1)}, u32[]{:S(2)}) copy-start(f32[512]{0:T(512)S(1)} %negate_multiply_fusion.2) | copy-start | bytes 6148
  1212.6 71.9 %copy-start.51 = (bf16[384,1536]{0,1:T(8,128)(2,1)S(1)}, bf16[384,1536]{0,1:T(8,128)(2,1)}, u32[]{:S(2)}) copy-start(bf16[384,1536]{0,1:T(8,128)(2,1)} %all-gather.26.cloned.1.call-done) | copy-start | bytes 3538948
  1214.2 233.1 %reduce-scatter.24.cloned.1.call-start = ((), (), s32[]{:S(2)}) async-start(), calls=%async_computation.29 | async-start | bytes 15728640 | tf_op jit(solution)/shard_map/reduce_scatter | solution.py:164
  1326.3 120.9 %copy-start.5 = (f32[512,1536]{1,0:T(8,128)S(1)}, f32[512,1536]{1,0:T(8,128)}, u32[]{:S(2)}) copy-start(f32[512,1536]{1,0:T(8,128)} %copy-done.3) | copy-start | bytes 9437188
  1326.3 120.9 %copy-start.65 = (f32[1536]{0:T(1024)S(1)}, f32[1536]{0:T(1024)}, u32[]{:S(2)}) copy-start(f32[1536]{0:T(1024)} %copy-done.64) | copy-start | bytes 18436
  1326.3 120.9 %copy-start.71 = (f32[512]{0:T(512)S(1)}, f32[512]{0:T(512)}, u32[]{:S(2)}) copy-start(f32[512]{0:T(512)} %copy-done.70) | copy-start | bytes 6148
  1326.3 120.9 %copy-start.73 = (f32[512]{0:T(512)S(1)}, f32[512]{0:T(512)}, u32[]{:S(2)}) copy-start(f32[512]{0:T(512)} %copy-done.72) | copy-start | bytes 6148
  1326.4 124.4 %copy-start.83 = (f32[512]{0:T(512)S(1)}, f32[512]{0:T(512)}, u32[]{:S(2)}) copy-start(f32[512]{0:T(512)} %copy-done.82) | copy-start | bytes 6148
  1326.4 199.9 %all-gather.38.cloned.1.call-start = ((), (), s32[]{:S(2)}) async-start(), calls=%async_computation.30 | async-start | bytes 7864320 | tf_op jit(solution)/shard_map/all_gather | solution.py:161
  1456.0 419.1 %all-reduce.12.cloned.1.call-start = ((), (), s32[]{:S(2)}) async-start(), calls=%async_computation.39 | async-start | bytes 4718592
  1463.2 413.7 %reduce-scatter.40.cloned.1.call-start = ((), (), s32[]{:S(2)}) async-start(), calls=%async_computation.38 | async-start | bytes 1474560
  1472.7 406.5 %reduce-scatter.36.cloned.1.call-start = ((), (), s32[]{:S(2)}) async-start(), calls=%async_computation.36 | async-start | bytes 21233664 | tf_op jit(solution)/shard_map/reduce_scatter | solution.py:325
  1500.4 25.9 %copy-start.49 = (bf16[384,1536]{0,1:T(8,128)(2,1)S(1)}, bf16[384,1536]{0,1:T(8,128)(2,1)}, u32[]{:S(2)}) copy-start(bf16[384,1536]{0,1:T(8,128)(2,1)} %all-gather.18.cloned.1.call-done) | copy-start | bytes 3538948
  1500.4 438.9 %reduce-scatter.26.cloned.1.call-start = ((), (), s32[]{:S(2)}) async-start(), calls=%async_computation.31 | async-start | bytes 15728640 | tf_op jit(solution)/shard_map/reduce_scatter | solution.py:164
  1537.2 14.0 copy-start.11
  1562.9 25.9 %copy-start.23 = (bf16[2,1024,6,64]{1,3,2,0:T(8,128)(2,1)S(1)}, bf16[2,1024,6,64]{1,3,2,0:T(8,128)(2,1)}, u32[]{:S(2)}) copy-start(bf16[2,1024,6,64]{1,3,2,0:T(8,128)(2,1)} %get-tuple-element.732) | copy-start | bytes 4718596 | tf_op jit(solution)/shard_map/while
  1634.6 27.8 %copy-start.12 = (bf16[2,1024,6,64]{1,3,2,0:T(8,128)(2,1)S(1)}, bf16[2,1024,6,64]{1,3,2,0:T(8,128)(2,1)}, u32[]{:S(2)}) copy-start(bf16[2,1024,6,64]{1,3,2,0:T(8,128)(2,1)} %copy-done.11) | copy-start | bytes 4718596 | tf_op jit(solution)/shard_map/while
  1662.3 14.0 copy-start.11
  1688.2 25.9 %copy-start.23 = (bf16[2,1024,6,64]{1,3,2,0:T(8,128)(2,1)S(1)}, bf16[2,1024,6,64]{1,3,2,0:T(8,128)(2,1)}, u32[]{:S(2)}) copy-start(bf16[2,1024,6,64]{1,3,2,0:T(8,128)(2,1)} %get-tuple-element.732) | copy-start | bytes 4718596 | tf_op jit(solution)/shard_map/while
  1760.9 27.8 %copy-start.12 = (bf16[2,1024,6,64]{1,3,2,0:T(8,128)(2,1)S(1)}, bf16[2,1024,6,64]{1,3,2,0:T(8,128)(2,1)}, u32[]{:S(2)}) copy-start(bf16[2,1024,6,64]{1,3,2,0:T(8,128)(2,1)} %copy-done.11) | copy-start | bytes 4718596 | tf_op jit(solution)/shard_map/while
  1792.7 7.3 copy-start.24
  1818.6 223.7 %reduce-scatter.38.cloned.1.call-start = ((), (), s32[]{:S(2)}) async-start(), calls=%async_computation.37 | async-start | bytes 10616832 | tf_op jit(solution)/shard_map/reduce_scatter | solution.py:326
  1834.3 9.5 copy-start.34
  1834.3 245.3 %reduce-scatter.34.cloned.1.call-start = ((), (), s32[]{:S(2)}) async-start(), calls=%async_computation.35 | async-start | bytes 2654208 | tf_op jit(solution)/shard_map/reduce_scatter | solution.py:324
  1843.7 8.3 copy-start.31
  1843.7 274.3 %reduce-scatter.32.cloned.1.call-start = ((), (), s32[]{:S(2)}) async-start(), calls=%async_computation.34 | async-start | bytes 2654208 | tf_op jit(solution)/shard_map/reduce_scatter | solution.py:322
  1852.0 304.3 %reduce-scatter.30.cloned.1.call-start = ((), (), s32[]{:S(2)}) async-start(), calls=%async_computation.33 | async-start | bytes 2654208 | tf_op jit(solution)/shard_map/reduce_scatter | solution.py:321
  1860.0 375.5 %reduce-scatter.28.cloned.1.call-start = ((), (), s32[]{:S(2)}) async-start(), calls=%async_computation.32 | async-start | bytes 7962624 | tf_op jit(solution)/shard_map/reduce_scatter | solution.py:320
  1876.9 62.5 %copy-start.10 = (bf16[512,1536]{1,0:T(8,128)(2,1)S(1)}, bf16[512,1536]{1,0:T(8,128)(2,1)}, u32[]{:S(2)}) copy-start(bf16[512,1536]{1,0:T(8,128)(2,1)} %param.22) | copy-start | bytes 4718596
  1876.9 62.5 %copy-start.63 = (f32[1536]{0:T(1024)S(1)}, f32[1536]{0:T(1024)}, u32[]{:S(2)}) copy-start(f32[1536]{0:T(1024)} %copy-done.62) | copy-start | bytes 18436
  1876.9 62.5 %copy-start.69 = (f32[512]{0:T(512)S(1)}, f32[512]{0:T(512)}, u32[]{:S(2)}) copy-start(f32[512]{0:T(512)} %copy-done.68) | copy-start | bytes 6148
  1884.3 57.7 %copy-start.81 = (f32[512]{0:T(512)S(1)}, f32[512]{0:T(512)}, u32[]{:S(2)}) copy-start(f32[512]{0:T(512)} %copy-done.80) | copy-start | bytes 6148
  1884.3 57.8 %copy-start.75 = (f32[512]{0:T(512)S(1)}, f32[512]{0:T(512)}, u32[]{:S(2)}) copy-start(f32[512]{0:T(512)} %copy-done.74) | copy-start | bytes 6148
  1942.1 40.7 %copy-start.21 = (bf16[512,1536]{1,0:T(8,128)(2,1)S(1)}, bf16[512,1536]{1,0:T(8,128)(2,1)}, u32[]{:S(2)}) copy-start(bf16[512,1536]{1,0:T(8,128)(2,1)} %param.35) | copy-start | bytes 4718596
  1942.1 40.7 %copy-start.79 = (f32[512]{0:T(512)S(1)}, f32[512]{0:T(512)}, u32[]{:S(2)}) copy-start(f32[512]{0:T(512)} %copy-done.78) | copy-start | bytes 6148
  1942.1 40.7 %copy-start.85 = (f32[512]{0:T(512)S(1)}, f32[512]{0:T(512)}, u32[]{:S(2)}) copy-start(f32[512]{0:T(512)} %copy-done.84) | copy-start | bytes 6148
  (61 other events, 154.9 us)
Sparse Core Ops, SparseCore 0:
  9.6 44.6 all-gather.15
  56.8 68.9 all-gather.13
  127.4 22.6 all-gather.17
  222.3 120.7 reduce-scatter.15
  344.6 22.6 all-gather.19
  368.8 22.4 all-gather.23
  393.7 69.9 all-gather.21
  465.3 22.6 all-gather.25
  501.4 120.7 reduce-scatter.17
  624.2 90.6 all-gather.29
  717.4 68.5 all-gather.27
  787.5 51.6 all-gather.31
  841.1 68.9 all-gather.33
  962.0 120.7 reduce-scatter.21
  1085.7 120.7 reduce-scatter.19
  1214.3 70.1 all-gather.35
  1326.5 120.7 reduce-scatter.23
  1456.1 70.1 all-gather.37
  1529.2 66.7 all-reduce.11
  1598.7 27.7 reduce-scatter.39
  1628.9 187.9 reduce-scatter.35
  1820.0 119.3 reduce-scatter.25
  1942.2 100.0 reduce-scatter.37
  2045.0 34.4 reduce-scatter.33
  2082.5 35.4 reduce-scatter.31
  2120.7 35.5 reduce-scatter.29
  2159.0 76.4 reduce-scatter.27
where the time goes:
time: 2260 us; the launch traced here: 2240 us
  waiting for transfers between devices  1390 us (62%)
  matrix products  388 us (17%)
  local copies, waits for them, and re-layouts  265 us (12%)
  other arithmetic  102 us (5%)
  blocking collectives  70.4 us (3%)
    reduce_scatter x3, waiting for transfers between devices, project_out(): lax.psum_scatter(jnp.dot(mixed_all, weight, preferred_element_type=jnp.fl...  358 us
    reduce_scatter x3, waiting for transfers between devices, gather_back(): lax.psum_scatter(times_transposed(grad_all, weight), 'tensor', scatter_di...  267 us
    all_gather x3, waiting for transfers between devices, spread_rows(): return lax.all_gather(local_part, 'tensor', axis=0, tiled=True)  197 us
    all_gather x3, waiting for transfers between devices, spread_grads(): return lax.all_gather(local_part, 'tensor', axis=0, tiled=True)  167 us
    dynamic_update_slice x8, local copies, waits for them, and re-layouts, body(): lax.map(cross_backward, (by_sequence(cross_query), cross_kv, valid_slots,...  115 us
    all_gather x1, waiting for transfers between devices, body(): lax.all_gather(gate_up_weight, 'dp', axis=0, tiled=True)  85.7 us
    dot_general x7, matrix products, times_transposed(): lax.dot_general(left, right, (((1,), (1,)), ((), ())), preferred_element_...  83.3 us
    dot_general x7, matrix products, rows_by_rows(): lax.dot_general(left, right, (((0,), (0,)), ((), ())), preferred_element_...  82.3 us
  transfers between devices with their start and end apart: 27, of which 22 were waited for; matrix products, arithmetic and copies ran while one was open for 27% of the time, Pallas kernels for 0%

commit v1 on v0

--- a/solution.py
+++ b/solution.py
@@ -1,6 +1,11 @@
+import functools
+
 import jax
 import jax.numpy as jnp
 from jax import lax
+from jax.experimental import pallas as pl
+from jax.experimental.pallas import tpu as pltpu
+from jax.sharding import Mesh
 from jax.sharding import PartitionSpec as P
 
 HD = 64
@@ -8,6 +13,11 @@
 
 EPSILON = 1e-05
 MASKED_SCORE = -1e30
+BF = jnp.bfloat16
+F32 = jnp.float32
+NN = (((1,), (0,)), ((), ()))
+NT = (((1,), (1,)), ((), ()))
+VMEM_BYTES = 60 << 20
 
 
 def layer_norm(values, gain):
@@ -96,7 +106,7 @@
     return (grad_query, grad_keys, grad_values)
 
 
-def body(
+def general_body(
     block_in,
     cond_tokens,
     cond_count,
@@ -343,9 +353,9 @@
     )
 
 
-def solution(mesh):
+def general_solution(mesh):
     return jax.shard_map(
-        body,
+        general_body,
         mesh=mesh,
         in_specs=(
             P(("dp", "tensor"), None),
@@ -380,3 +390,625 @@
         ),
         check_vma=False,
     )
+
+
+def dot(left, right, dims=NN):
+    return lax.dot_general(left, right, dims, preferred_element_type=F32)
+
+
+def rot(values, tables):
+    cosine, sine_up, sine_down = tables
+    return (
+        values * cosine
+        + pltpu.roll(values, 16, 1) * sine_up
+        + pltpu.roll(values, 112, 1) * sine_down
+    )
+
+
+def rot_back(grads, tables):
+    cosine, sine_up, sine_down = tables
+    return (
+        grads * cosine
+        - pltpu.roll(grads, 16, 1) * sine_up
+        - pltpu.roll(grads, 112, 1) * sine_down
+    )
+
+
+def rot_tables(positions):
+    quarter = HD // 4
+    inverse = 10000.0 ** (-jnp.arange(quarter).astype(F32) / quarter)
+    angle_grid = positions.astype(F32)[:, None] * inverse[None, :]
+    cosine, sine = jnp.cos(angle_grid), jnp.sin(angle_grid)
+    rest = jnp.zeros((positions.shape[0], 2 * quarter), F32)
+    none = jnp.zeros_like(sine)
+    return (
+        jnp.concatenate([cosine, cosine, rest + 1.0] * 2, axis=1),
+        jnp.concatenate([none, sine, rest] * 2, axis=1),
+        jnp.concatenate([-sine, none, rest] * 2, axis=1),
+    )
+
+
+def to_rows(picks, columns):
+    first = columns.astype(BF)
+    rest = columns - first.astype(F32)
+    second = rest.astype(BF)
+    third = (rest - second.astype(F32)).astype(BF)
+    return dot(picks, first, NT) + dot(picks, second, NT) + dot(picks, third, NT)
+
+
+def iota(shape, axis):
+    return lax.broadcasted_iota(jnp.int32, shape, axis)
+
+
+def self_forward_kernel(
+    step, rows_ref, own_ref, other_ref, c_ref, su_ref, sd_ref,
+    q_ref, k_ref, v_ref, mine_ref, theirs_ref, lse_ref,
+):
+    count, width = rows_ref.shape
+    half = width // 2
+    qkv = dot(rows_ref[:, :half], own_ref[0]) + dot(rows_ref[:, half:], other_ref[0])
+    tables = (c_ref[...], su_ref[...], sd_ref[...])
+    query = (rot(qkv[:, :128], tables) * 0.125).astype(BF)
+    key = rot(qkv[:, 128:256], tables).astype(BF)
+    value = qkv[:, 256:].astype(BF)
+    q_ref[...] = query
+    k_ref[...] = key
+    v_ref[...] = value
+    lane = iota((step, 128), 1)
+    picks = jnp.where(iota((8, 128), 0) == iota((8, 128), 1), 1.0, 0.0).astype(BF)
+    for at in range(0, count, step):
+        part = query[at : at + step]
+        mixed, logs = [], []
+        for head in range(2):
+            here = (lane // HD) == head
+            scores = dot(jnp.where(here, part, jnp.zeros_like(part)), key, NT)
+            top = jnp.max(scores, axis=1, keepdims=True)
+            weights = jnp.exp(scores - top)
+            total = jnp.sum(weights, axis=1, keepdims=True)
+            mixed.append(dot(weights.astype(BF), value) * (1.0 / total))
+            logs.append(top + jnp.log(total))
+        out = jnp.where(lane < HD, mixed[0], mixed[1]).astype(BF)
+        both = jnp.where(lane == 0, logs[0], jnp.where(lane == 1, logs[1], 0.0))
+        lse_ref[0, :, at : at + step] = to_rows(picks, both)
+        if at < count // 2:
+            mine_ref[at : at + step, :] = out
+        else:
+            theirs_ref[at - count // 2 : at - count // 2 + step, :] = out
+
+
+def whole(shape):
+    return pl.BlockSpec(shape, lambda p: (0,) * len(shape))
+
+
+def columns_of(rows):
+    return pl.BlockSpec((rows, 128), lambda p: (0, p))
+
+
+def self_forward(rows, own, other, tables):
+    count, width = rows.shape
+    per = own.shape[2] // 384
+    pairs = own.shape[0] * per
+    wide = pairs * 128
+    weight = pl.BlockSpec((1, own.shape[1], 384), lambda p: (p // per, 0, p % per))
+    return pl.pallas_call(
+        functools.partial(self_forward_kernel, min(512, count // 2)),
+        grid=(pairs,),
+        in_specs=[whole((count, width)), weight, weight] + [whole((count, 128))] * 3,
+        out_specs=[columns_of(count)] * 3
+        + [columns_of(count // 2)] * 2
+        + [pl.BlockSpec((1, 8, count), lambda p: (p, 0, 0))],
+        out_shape=[jax.ShapeDtypeStruct((count, wide), BF)] * 3
+        + [jax.ShapeDtypeStruct((count // 2, wide), BF)] * 2
+        + [jax.ShapeDtypeStruct((pairs, 8, count), F32)],
+        compiler_params=pltpu.CompilerParams(vmem_limit_bytes=VMEM_BYTES),
+        cost_estimate=pl.CostEstimate(
+            flops=6 * count * width * wide + 8 * count * count * wide,
+            bytes_accessed=6 * width * wide + 12 * count * wide,
+            transcendentals=2 * count * count * pairs,
+        ),
+        name="self_forward",
+    )(rows, own, other, *tables)
+
+
+def self_backward_kernel(
+    step, q_ref, k_ref, v_ref, mine_ref, theirs_ref, dmine_ref, dtheirs_ref, lse_ref,
+    c_ref, su_ref, sd_ref, out_ref,
+):
+    count = q_ref.shape[0]
+    query = q_ref[...]
+    grads = jnp.concatenate([dmine_ref[...], dtheirs_ref[...]], axis=0)
+    mixed = jnp.concatenate([mine_ref[...], theirs_ref[...]], axis=0)
+    picks = jnp.where((iota((8, 128), 1) // HD) == iota((8, 128), 0), 1.0, 0.0).astype(BF)
+    delta = to_rows(picks, grads.astype(F32) * mixed.astype(F32))
+    lane = iota((step, 128), 1)
+    row = iota((128, step), 0)
+    keys_across = jnp.transpose(k_ref[...].astype(F32)).astype(BF)
+    query_across = jnp.zeros((128, count), F32)
+    tables = (c_ref[...], su_ref[...], sd_ref[...])
+    for at in range(0, count, step):
+        here = slice(at, at + step)
+        key, value = k_ref[here, :], v_ref[here, :]
+        across = keys_across[:, here]
+        dkeys, dvalues = [], []
+        for head in range(2):
+            inside = (lane // HD) == head
+            scores = dot(jnp.where(inside, key, jnp.zeros_like(key)), query, NT)
+            probs = jnp.exp(scores - lse_ref[0, head : head + 1, :])
+            dprobs = dot(jnp.where(inside, value, jnp.zeros_like(value)), grads, NT)
+            dscores = (probs * (dprobs - delta[head : head + 1, :])).astype(BF)
+            dvalues.append(dot(probs.astype(BF), grads))
+            dkeys.append(dot(dscores, query))
+            picked = jnp.where((row // HD) == head, across, jnp.zeros_like(across))
+            query_across = query_across + dot(picked, dscores)
+        dkey = jnp.where(lane < HD, dkeys[0], dkeys[1])
+        dvalue = jnp.where(lane < HD, dvalues[0], dvalues[1])
+        out_ref[here, 128:256] = rot_back(dkey, [t[here] for t in tables]).astype(BF)
+        out_ref[here, 256:384] = dvalue.astype(BF)
+    dquery = jnp.transpose(query_across)
+    out_ref[:, 0:128] = (rot_back(dquery, tables) * 0.125).astype(BF)
+
+
+def self_backward(query, key, value, mine, theirs, dmine, dtheirs, lse, tables):
+    count, wide = query.shape
+    pairs = wide // 128
+    return pl.pallas_call(
+        functools.partial(self_backward_kernel, min(512, count // 2)),
+        grid=(pairs,),
+        in_specs=[columns_of(count)] * 3
+        + [columns_of(count // 2)] * 4
+        + [pl.BlockSpec((1, 8, count), lambda p: (p, 0, 0))]
+        + [whole((count, 128))] * 3,
+        out_specs=pl.BlockSpec((count, 384), lambda p: (0, p)),
+        out_shape=jax.ShapeDtypeStruct((count, 3 * wide), BF),
+        compiler_params=pltpu.CompilerParams(vmem_limit_bytes=VMEM_BYTES),
+        cost_estimate=pl.CostEstimate(
+            flops=20 * count * count * wide,
+            bytes_accessed=20 * count * wide,
+            transcendentals=2 * count * count * pairs,
+        ),
+        name="self_backward",
+    )(query, key, value, mine, theirs, dmine, dtheirs, lse, *tables)
+
+
+def ffn_kernel(
+    has_start, tile, rows_ref, across_ref, dy_ref, dyx_ref, own_ref, other_ref, *rest,
+):
+    if has_start:
+        y_in, d_in, y_out, d_out, gown_ref, gother_ref = rest
+    else:
+        y_out, d_out, gown_ref, gother_ref = rest
+    half = rows_ref.shape[1] // 2
+    both = 2 * tile
+
+    @pl.when(pl.program_id(0) == 0)
+    def _():
+        if has_start:
+            y_out[...] = y_in[...]
+            d_out[...] = d_in[...]
+        else:
+            y_out[...] = jnp.zeros_like(y_out)
+            d_out[...] = jnp.zeros_like(d_out)
+
+    own, other = own_ref[0], other_ref[0]
+    gate_up = dot(rows_ref[:, :half], own[:, :both]) + dot(rows_ref[:, half:], other[:, :both])
+    dhidden = dot(dy_ref[:, :half], own[:, both:]) + dot(dy_ref[:, half:], other[:, both:])
+    gate, up = gate_up[:, :tile], gate_up[:, tile:]
+    sigma = 1.0 / (1.0 + jnp.exp(-gate))
+    silu = gate * sigma
+    hidden = (silu * up).astype(BF)
+    dup = (dhidden * silu).astype(BF)
+    dgate = (dhidden * up * (sigma * (1.0 + gate * (1.0 - sigma)))).astype(BF)
+    dgate_up = jnp.concatenate([dgate, dup], axis=1)
+    y_out[:, :half] += dot(hidden, own[:, both:], NT)
+    y_out[:, half:] += dot(hidden, other[:, both:], NT)
+    d_out[:, :half] += dot(dgate_up, own[:, :both], NT)
+    d_out[:, half:] += dot(dgate_up, other[:, :both], NT)
+    gown_ref[0, :, :both] = dot(across_ref[:half, :], dgate_up).astype(BF)
+    gother_ref[0, :, :both] = dot(across_ref[half:, :], dgate_up).astype(BF)
+    gown_ref[0, :, both:] = dot(dyx_ref[:half, :], hidden).astype(BF)
+    gother_ref[0, :, both:] = dot(dyx_ref[half:, :], hidden).astype(BF)
+
+
+def ffn(rows, across, dy, dyx, own, other, tile, start=None):
+    count, width = rows.shape
+    groups, half, wide = own.shape
+    tiles = wide // (3 * tile)
+    block = pl.BlockSpec((1, half, 3 * tile), lambda p: (p // tiles, 0, p % tiles))
+    full = whole((count, width))
+    flipped = whole((width, count))
+    once = pl.BlockSpec((count, width), lambda p: (0, 0), pipeline_mode=pl.Buffered(1))
+    fixed = pl.BlockSpec((width, count), lambda p: (0, 0), pipeline_mode=pl.Buffered(1))
+    extra = [] if start is None else list(start)
+    return pl.pallas_call(
+        functools.partial(ffn_kernel, start is not None, tile),
+        grid=(groups * tiles,),
+        in_specs=[once, fixed, once, fixed, block, block] + [once] * len(extra),
+        out_specs=[once, once, block, block],
+        out_shape=[jax.ShapeDtypeStruct((count, width), F32)] * 2
+        + [jax.ShapeDtypeStruct(own.shape, BF)] * 2,
+        input_output_aliases={} if start is None else {6: 0, 7: 1},
+        compiler_params=pltpu.CompilerParams(vmem_limit_bytes=VMEM_BYTES),
+        cost_estimate=pl.CostEstimate(
+            flops=6 * count * width * groups * wide,
+            bytes_accessed=8 * groups * width * wide // 2 + 24 * count * width,
+            transcendentals=count * groups * wide // 3,
+        ),
+        name="feed_forward",
+    )(rows, across, dy, dyx, own, other, *extra)
+
+
+def cross_scores(query, key, allowed):
+    scores = jnp.einsum("qhd,khd->hqk", query, key, preferred_element_type=F32)
+    return jnp.where(allowed[None, None, :], scores, MASKED_SCORE)
+
+
+def normalize(values):
+    centre = values - jnp.mean(values, axis=-1, keepdims=True)
+    scale = lax.rsqrt(jnp.mean(centre * centre, axis=-1, keepdims=True) + EPSILON)
+    return centre * scale, scale
+
+
+def normalize_back(grads, gain, normal, scale):
+    inner = grads * gain
+    return (
+        inner
+        - jnp.mean(inner, axis=-1, keepdims=True)
+        - normal * jnp.mean(inner * normal, axis=-1, keepdims=True)
+    ) * scale
+
+
+def swap(array, axis, bit=1):
+    return lax.ppermute(array, axis, [(i, i ^ bit) for i in range(lax.axis_size(axis))])
+
+
+def pick(flag, on, off):
+    return jnp.where(flag, on, off)
+
+
+def pair_body(
+    block_in,
+    cond_tokens,
+    cond_count,
+    norm1_gain,
+    norm2_gain,
+    norm3_gain,
+    qkv_weight,
+    attn_out_weight,
+    cross_q_weight,
+    cross_kv_weight,
+    cross_out_weight,
+    gate_up_weight,
+    down_weight,
+    out_cotangent,
+    chunks,
+    tile,
+):
+    rows, width = block_in.shape
+    shard = qkv_weight.shape[0]
+    head_cols = attn_out_weight.shape[0]
+    hidden_cols = down_weight.shape[0]
+    cond_slots, cond_width = cond_tokens.shape[1:]
+    cond_shard = cross_kv_weight.shape[0]
+    dp = lax.axis_index("dp")
+    seq = lax.axis_index("seq")
+    side = lax.axis_index("half")
+    dp_size = lax.axis_size("dp")
+    z_size = dp_size // 2
+    core = (dp % 2) == 1
+    z = dp // 2
+    half = width // 2
+    pairs_here = head_cols // 128
+    per_chunk = hidden_cols // chunks
+    z_bits = []
+    bit = z_size // 2
+    while bit:
+        z_bits.append(bit)
+        bit //= 2
+
+    def over_z(array):
+        array = array[None]
+        for bit in z_bits:
+            got = swap(array, "dp", 2 * bit)
+            upper = (z & bit) != 0
+            both = jnp.stack([pick(upper, got, array), pick(upper, array, got)], axis=1)
+            array = both.reshape((-1,) + array.shape[1:])
+        return array
+
+    def gather(pack, wide):
+        array = over_z(pack).reshape(half, pack.shape[1])
+        array = jnp.stack([array, swap(array, "seq")])
+        if wide:
+            array = jnp.stack([array, swap(array, "half")])
+        return array, swap(array, "dp", 1)
+
+    def to_core_order(array, piece):
+        parts = array.reshape(array.shape[0], z_size, 2, piece)
+        even = parts[:, :, 0].reshape(array.shape[0], -1)
+        odd = parts[:, :, 1].reshape(array.shape[0], -1)
+        return jnp.concatenate([pick(core, odd, even), pick(core, even, odd)], axis=1)
+
+    def from_core_order(array, piece):
+        count = array.shape[0]
+        middle = array.shape[1] // 2
+        own, other = array[:, :middle], array[:, middle:]
+        even = pick(core, other, own).reshape(count, z_size, piece)
+        odd = pick(core, own, other).reshape(count, z_size, piece)
+        return jnp.stack([even, odd], axis=2).reshape(count, -1)
+
+    def scatter_z(array):
+        array = array.reshape((z_size, -1) + array.shape[1:])
+        for bit in z_bits[::-1]:
+            array = array.reshape((-1, 2) + array.shape[1:])
+            mine = (z & bit) // bit
+            keep = lax.dynamic_index_in_dim(array, mine, 1, keepdims=False)
+            send = lax.dynamic_index_in_dim(array, 1 - mine, 1, keepdims=False)
+            array = keep.astype(F32) + swap(send, "dp", 2 * bit).astype(F32)
+            if bit != z_bits[0]:
+                array = array.astype(BF)
+        return array.astype(F32)[0]
+
+    def fold(keep, send, axis, bit=1):
+        return (keep.astype(F32) + swap(send, axis, bit).astype(F32)).astype(BF)
+
+    gu_parts = gate_up_weight.reshape(shard, 2, chunks, per_chunk // tile, 1, tile)
+    down_across = down_weight.T.reshape(shard, 1, chunks, per_chunk // tile, 1, tile)
+    ffn_pack = jnp.concatenate([gu_parts, down_across], axis=1)
+    ffn_pack = ffn_pack.transpose(2, 0, 3, 1, 4, 5).reshape(chunks, shard, 3 * per_chunk)
+    qkv_pack = (
+        qkv_weight.reshape(shard, 3, pairs_here, 128)
+        .transpose(0, 2, 1, 3)
+        .reshape(shard, 3 * head_cols)
+    )
+    square_pack = jnp.concatenate(
+        [
+            attn_out_weight.T,
+            cross_q_weight,
+            cross_kv_weight.transpose(1, 0, 2).reshape(shard, head_cols),
+            cross_out_weight.T,
+        ],
+        axis=1,
+    )
+    gains = jnp.stack([norm1_gain, norm2_gain, norm3_gain])
+
+    qkv_own, qkv_other = gather(qkv_pack, False)
+    gains = over_z(gains)
+    gains = jnp.concatenate([gains, swap(gains, "dp", 1)])
+    gains = gains.transpose(1, 0, 2).reshape(3, width).astype(F32)
+
+    mine_in = to_core_order(block_in, shard)
+    all_in = jnp.concatenate([mine_in, swap(mine_in, "half")], axis=0)
+    top_grads = to_core_order(out_cotangent, shard)
+    all_top = jnp.concatenate([top_grads, swap(top_grads, "half")], axis=0)
+    square_own, square_other = gather(square_pack, True)
+    ffn_weights = [gather(ffn_pack[i], False) for i in range(chunks)]
+
+    def square(section):
+        cut = slice(section * head_cols, (section + 1) * head_cols)
+        both = jnp.stack([square_own[..., cut], square_other[..., cut]])
+        return both.transpose(0, 3, 1, 2, 4).reshape(width, 4 * head_cols)
+
+    positions = jnp.concatenate([side * rows + jnp.arange(rows), (1 - side) * rows + jnp.arange(rows)])
+    tables = rot_tables(positions)
+    first_normal, first_scale = normalize(all_in.astype(F32))
+    first_all = (first_normal * gains[0]).astype(BF)
+    query, key, value, mine, theirs, lse = self_forward(first_all, qkv_own, qkv_other, tables)
+    mixed = jnp.concatenate([mine, swap(theirs, "half")], axis=1)
+    w_out = square(0)
+    after_self = mine_in.astype(F32) + dot(mixed, w_out, NT)
+    second_normal, second_scale = normalize(after_self)
+    second = (second_normal * gains[1]).astype(BF)
+    heads = 4 * head_cols // HD
+    w_cq = square(1)
+    cross_query = (dot(second, w_cq) * 0.125).astype(BF).reshape(rows, heads, HD)
+    my_cond = to_core_order(cond_tokens[seq], cond_shard)
+    w_ckv = square(2).reshape(width // (2 * cond_shard), 2, cond_shard, 4 * head_cols)
+    w_ckv = w_ckv.transpose(0, 2, 1, 3).reshape(cond_width, 2 * 4 * head_cols)
+    cross_kv = dot(my_cond, w_ckv).astype(BF).reshape(cond_slots, 2, heads, HD)
+    allowed = jnp.arange(cond_slots) < cond_count[seq]
+    cross_mixed, cross_lse = attend_forward(cross_query, cross_kv[:, 0], cross_kv[:, 1], allowed)
+    cross_flat = cross_mixed.reshape(rows, 4 * head_cols)
+    w_co = square(3)
+    after_cross = after_self + dot(cross_flat, w_co, NT)
+    third_normal, third_scale = normalize(after_cross)
+    third = (third_normal * gains[2]).astype(BF)
+    third_all = jnp.concatenate([third, swap(third, "half")], axis=0)
+    third_across = third_all.T
+    top_across = all_top.T
+    sums = None
+    ffn_grads = []
+    for own, other in ffn_weights:
+        y_sum, d_sum, gown, gother = ffn(
+            third_all, third_across, all_top, top_across, own, other, tile, sums
+        )
+        sums = (y_sum, d_sum)
+        ffn_grads.append((gown, gother))
+    grad_third = d_sum[:rows] + swap(d_sum[rows:].astype(BF), "half").astype(F32)
+    y_mine = y_sum[:rows] + swap(y_sum[rows:].astype(BF), "half").astype(F32)
+    block_out = from_core_order((after_cross + y_mine).astype(BF), shard)
+
+    def scatter_ffn(gown, gother):
+        kept = fold(gown, gother, "dp")
+        kept = fold(kept[0], kept[1], "seq")
+        return scatter_z(kept)
+
+    ffn_owned = jnp.stack([scatter_ffn(*pair) for pair in ffn_grads])
+    ffn_owned = ffn_owned.reshape(chunks, shard, per_chunk // tile, 3, tile)
+    ffn_owned = ffn_owned.transpose(1, 3, 0, 2, 4).reshape(shard, 3, hidden_cols)
+    grad_gate_up = ffn_owned[:, :2]
+    grad_down = ffn_owned[:, 2].T
+
+    gain_third = jnp.sum(grad_third * third_normal, axis=0)
+    grad_cross_rows = top_grads.astype(F32) + normalize_back(
+        grad_third, gains[2], third_normal, third_scale
+    )
+    second_grads = grad_cross_rows.astype(BF)
+    grad_cross_mixed = dot(second_grads, w_co).astype(BF)
+    grad_co = rows_by_rows(second_grads, cross_flat).astype(BF)
+    cross_gq, cross_gk, cross_gv = attend_backward(
+        cross_query,
+        cross_kv[:, 0],
+        cross_kv[:, 1],
+        allowed,
+        cross_lse,
+        grad_cross_mixed.reshape(rows, heads, HD),
+    )
+    grad_cross_query = (cross_gq * 0.125).astype(BF).reshape(rows, 4 * head_cols)
+    grad_cross_kv = (
+        jnp.stack([cross_gk, cross_gv], axis=1).astype(BF).reshape(cond_slots, 8 * head_cols)
+    )
+    grad_cq = rows_by_rows(second, grad_cross_query).astype(BF)
+    grad_ckv = rows_by_rows(my_cond, grad_cross_kv).astype(BF)
+    grad_ckv = grad_ckv.reshape(width // (2 * cond_shard), cond_shard, 2, 4 * head_cols)
+    grad_ckv = grad_ckv.transpose(0, 2, 1, 3).reshape(width, 4 * head_cols)
+
+    def scatter_square(stack):
+        wide = stack.shape[2]
+        kept = fold(stack[:, :half], stack[:, half:], "dp")
+        kept = fold(kept[..., : wide // 2], kept[..., wide // 2 :], "half")
+        kept = fold(kept[..., : wide // 4], kept[..., wide // 4 :], "seq")
+        return jnp.stack([scatter_z(kept[i]) for i in range(stack.shape[0])])
+
+    owned = scatter_square(jnp.stack([grad_cq, grad_ckv, grad_co]))
+    grad_cross_q = owned[0]
+    grad_cross_kv_weight = owned[1].reshape(2, cond_shard, head_cols).transpose(1, 0, 2)
+    grad_cross_out = owned[2].T
+
+    cond_mine = from_core_order(times_transposed(grad_cross_kv, w_ckv), cond_shard)
+    cond_mine = cond_mine.reshape(cond_slots, 2, 2, cond_width // 4)
+    cond_keep = lax.dynamic_index_in_dim(cond_mine, side, 2, keepdims=False)
+    cond_send = lax.dynamic_index_in_dim(cond_mine, 1 - side, 2, keepdims=False)
+    cond_mine = cond_keep + swap(cond_send, "half")
+    cond_keep = lax.dynamic_index_in_dim(cond_mine, seq, 1, keepdims=False)
+    cond_send = lax.dynamic_index_in_dim(cond_mine, 1 - seq, 1, keepdims=False)
+    cond_got = swap(cond_send, "seq")
+    odd = seq == 1
+    grad_cond = jnp.stack([pick(odd, cond_got, cond_keep), pick(odd, cond_keep, cond_got)])
+
+    grad_second = times_transposed(grad_cross_query, w_cq)
+    gain_second = jnp.sum(grad_second * second_normal, axis=0)
+    grad_self_rows = grad_cross_rows + normalize_back(
+        grad_second, gains[1], second_normal, second_scale
+    )
+    first_grads = grad_self_rows.astype(BF)
+    grad_mixed = dot(first_grads, w_out).astype(BF)
+    grad_out = rows_by_rows(first_grads, mixed).astype(BF)
+    dmine = grad_mixed[:, : 2 * head_cols]
+    dtheirs = swap(grad_mixed[:, 2 * head_cols :], "half")
+    grad_qkv_rows = self_backward(
+        query, key, value, mine, theirs, dmine, dtheirs, lse, tables
+    )
+    grad_attn_out = scatter_square(grad_out[None])[0].T
+    cut = 3 * head_cols
+    parts = [grad_qkv_rows[:, :cut], grad_qkv_rows[:, cut:]]
+
+    def first_back(weights):
+        return times_transposed(parts[0], weights[0]) + times_transposed(parts[1], weights[1])
+
+    grad_first = jnp.concatenate([first_back(qkv_own), first_back(qkv_other)], axis=1)
+    gain_first = jnp.sum(grad_first * first_normal, axis=0)
+    grad_first = grad_first[:rows] + swap(grad_first[rows:].astype(BF), "half").astype(F32)
+    g_other = rows_by_rows(first_all[:, half:], grad_qkv_rows).astype(BF)
+    g_own = rows_by_rows(first_all[:, :half], grad_qkv_rows).astype(BF)
+    kept = fold(g_own, g_other, "dp")
+    kept = fold(kept[:, :cut], kept[:, cut:], "seq")
+    grad_qkv = (
+        scatter_z(kept).reshape(shard, pairs_here, 3, 128).transpose(0, 2, 1, 3)
+    ).reshape(shard, 3, head_cols)
+    grad_input = grad_self_rows + normalize_back(
+        grad_first, gains[0], first_normal[:rows], first_scale[:rows]
+    )
+    grad_input = from_core_order(grad_input, shard)
+
+    gain_grads = jnp.stack([gain_first, gain_second, gain_third])
+    gain_grads = gain_grads[:, :half] + swap(gain_grads[:, half:], "dp", 1)
+    gain_grads = gain_grads + swap(gain_grads, "seq")
+    gain_grads = gain_grads + swap(gain_grads, "half")
+    gain_grads = scatter_z(gain_grads.reshape(3, z_size, shard).transpose(1, 0, 2).reshape(-1, shard))
+    return (
+        block_out,
+        grad_input,
+        grad_cond,
+        gain_grads[0],
+        gain_grads[1],
+        gain_grads[2],
+        grad_qkv,
+        grad_attn_out,
+        grad_cross_q,
+        grad_cross_kv_weight,
+        grad_cross_out,
+        grad_gate_up,
+        grad_down,
+    )
+
+
+def power_of_two(number):
+    return number > 0 and number & (number - 1) == 0
+
+
+def pair_solution(mesh, sequences):
+    dp, tensor = mesh.devices.shape
+    finer = Mesh(mesh.devices.reshape(dp, sequences, tensor // sequences), ("dp", "seq", "half"))
+    every = ("dp", "seq", "half")
+    both = ("seq", "half")
+    return jax.shard_map(
+        functools.partial(pair_body, chunks=CHUNKS, tile=TILE),
+        mesh=finer,
+        in_specs=(
+            P(every, None),
+            P("dp", None, None),
+            P("dp"),
+            P("dp"),
+            P("dp"),
+            P("dp"),
+            P("dp", None, both),
+            P(both, "dp"),
+            P("dp", both),
+            P("dp", None, both),
+            P(both, "dp"),
+            P("dp", None, both),
+            P(both, "dp"),
+            P(every, None),
+        ),
+        out_specs=(
+            P(every, None),
+            P(every, None),
+            P("dp", None, both),
+            P("dp"),
+            P("dp"),
+            P("dp"),
+            P("dp", None, both),
+            P(both, "dp"),
+            P("dp", both),
+            P("dp", None, both),
+            P(both, "dp"),
+            P("dp", None, both),
+            P(both, "dp"),
+        ),
+        check_vma=False,
+    )
+
+
+CHUNKS = 2
+TILE = 256
+
+
+def solution(mesh):
+    dp, tensor = mesh.devices.shape
+
+    def run(*args):
+        cond_tokens, qkv, down = args[1], args[6], args[12]
+        sequences = cond_tokens.shape[0] // dp
+        fits = (
+            sequences == 2
+            and tensor == 4
+            and power_of_two(dp)
+            and dp >= 4
+            and qkv.shape[2] % (tensor * 128) == 0
+            and down.shape[0] % (tensor * CHUNKS * TILE) == 0
+            and qkv.shape[0] == 2 * cond_tokens.shape[2]
+        )
+        if fits:
+            return pair_solution(mesh, sequences)(*args)
+        return general_solution(mesh)(*args)
+
+    return run

time: 2260 us -> 1510 us (0.67)
  waiting for transfers between devices: 1390 us -> 634 us
  matrix products: 388 us -> 93.4 us
  Pallas kernels: 0 us -> 185 us
  other arithmetic: 102 us -> 226 us
  blocking collectives: 70.4 us -> 0 us
  starting transfers between devices: 2.68 us -> 68.3 us
    reduce_scatter x12 -> x0, waiting for transfers between devices: 872 us -> none  [the longest x3 358 us: project_out(): lax.psum_scatter(jnp.dot(mixed_all, weight, preferred_element_type=jnp.fl...]
    ppermute x0 -> x61, waiting for transfers between devices: none -> 634 us  [swap(): lax.ppermute(array, axis, [(i, i ^ bit) for i in range(lax.axis_size(axis...]
    all_gather x13 -> x0, waiting for transfers between devices: 518 us -> none  [the longest x3 197 us: spread_rows(): return lax.all_gather(local_part, 'tensor', axis=0, tiled=True)]
    pallas_call x0 -> x4, Pallas kernels: none -> 185 us  [the longest x2 111 us: ffn(): pl.pallas_call(functools.partial(ffn_kernel, start is not None, tile), gr...]
    dynamic_update_slice x8 -> x0, local copies, waits for them, and re-layouts: 115 us -> none  [body(): lax.map(cross_backward, (by_sequence(cross_query), cross_kv, valid_slots,...]
    dot_general x11 -> x6, matrix products: 107 us -> 23.6 us  [dot(): return lax.dot_general(left, right, dims, preferred_element_type=F32)]
    ppermute x0 -> x61, starting transfers between devices: none -> 68.3 us  [swap(): lax.ppermute(array, axis, [(i, i ^ bit) for i in range(lax.axis_size(axis...]
    another operation x8 -> x31, other arithmetic: 0.74 us -> 64.7 us  [the longest x3 17.7 us: gather(): array = jnp.stack([array, swap(array, 'seq')])]
  transfers between devices with their start and end apart: 27 -> 61, of which waited for: 22 -> 31; matrix products, arithmetic and copies ran while one was open for 27% -> 38% of each run, Pallas kernels for 0% -> 9%
where the time goes in v1:
time: 1510 us; the launch traced here: 1490 us
  waiting for transfers between devices  634 us (42%)
  local copies, waits for them, and re-layouts  285 us (19%)
  other arithmetic  226 us (15%)
  Pallas kernels  185 us (12%)
  matrix products  93.4 us (6%)
  starting transfers between devices  68.3 us (5%)
    ppermute x61, waiting for transfers between devices, swap(): lax.ppermute(array, axis, [(i, i ^ bit) for i in range(lax.axis_size(axis...  634 us
    pallas_call x2, Pallas kernels, ffn(): pl.pallas_call(functools.partial(ffn_kernel, start is not None, tile), gr...  111 us
    ppermute x61, starting transfers between devices, swap(): lax.ppermute(array, axis, [(i, i ^ bit) for i in range(lax.axis_size(axis...  68.3 us
    convert_element_type x12, other arithmetic, fold(): return (keep.astype(F32) + swap(send, axis, bit).astype(F32)).astype(BF)  51.5 us
    pallas_call x1, Pallas kernels, self_backward(): pl.pallas_call(functools.partial(self_backward_kernel, min(512, count //...  38.3 us
    transpose x4, local copies, waits for them, and re-layouts, square(): return both.transpose(0, 3, 1, 2, 4).reshape(width, 4 * head_cols)  37.9 us
    pallas_call x1, Pallas kernels, self_forward(): pl.pallas_call(functools.partial(self_forward_kernel, min(512, count // 2...  36.2 us
    unnamed x206, local copies, waits for them, and re-layouts  35.8 us
  transfers between devices with their start and end apart: 61, of which 31 were waited for; matrix products, arithmetic and copies ran while one was open for 38% of the time, Pallas kernels for 9%

profile of v1, /device:TPU:0, one launch (start us, length us, event | category | flops | bytes accessed | tf_op | source)
XLA Modules:
  0.0 1494.6 jit_solution(10979225905349838912)
XLA Ops:
  6.9 26.0 %collective-permute-done.9 = bf16[1,192,1536]{2,1,0:T(8,128)(2,1)S(1)} collective-permute-done((bf16[1,192,1536]{2,1,0:T(8,128)(2,1)S(1)}, bf16[1,192,1536]{2,1,0:T(8,128)(2,1)S(1)}, u32[]{:S(2)}, u32[]{:S(2)}) %collective-permute-start.9) | collective-permute-done | bytes 589856 | tf_op jit(solution)/shard_map/ppermute | solution.py:661
  35.9 26.6 %collective-permute-done.10 = bf16[2,192,1536]{2,1,0:T(8,128)(2,1)S(1)} collective-permute-done((bf16[2,192,1536]{2,1,0:T(8,128)(2,1)}, bf16[2,192,1536]{2,1,0:T(8,128)(2,1)S(1)}, u32[]{:S(2)}, u32[]{:S(2)}) %collective-permute-start.10) | collective-permute-done | bytes 1179680 | tf_op jit(solution)/shard_map/ppermute | solution.py:661
  94.1 22.1 %collective-permute-done.11 = bf16[768,1536]{1,0:T(8,128)(2,1)} collective-permute-done((bf16[768,1536]{1,0:T(8,128)(2,1)}, bf16[768,1536]{1,0:T(8,128)(2,1)}, u32[]{:S(2)}, u32[]{:S(2)}) %collective-permute-start.11) | collective-permute-done | bytes 2359328 | tf_op jit(solution)/shard_map/ppermute | solution.py:661
  116.2 6.5 fusion.78
  172.7 37.2 %collective-permute-done.5 = bf16[2,192,1152]{2,1,0:T(8,128)(2,1)S(1)} collective-permute-done((bf16[2,192,1152]{2,1,0:T(8,128)(2,1)S(1)}, bf16[2,192,1152]{2,1,0:T(8,128)(2,1)S(1)}, u32[]{:S(2)}, u32[]{:S(2)}) %collective-permute-start.5) | collective-permute-done | bytes 884768 | tf_op jit(solution)/shard_map/ppermute | solution.py:661
  213.1 12.0 collective-permute-done.12
  225.1 8.4 pad_maximum_fusion
  242.3 10.0 collective-permute-done.6
  257.1 21.1 %collective-permute-done.21 = bf16[2,192,2304]{2,1,0:T(8,128)(2,1)} collective-permute-done((bf16[2,192,2304]{2,1,0:T(8,128)(2,1)}, bf16[2,192,2304]{2,1,0:T(8,128)(2,1)}, u32[]{:S(2)}, u32[]{:S(2)}) %collective-permute-start.21) | collective-permute-done | bytes 1769504 | tf_op jit(solution)/shard_map/ppermute | solution.py:661
  282.4 33.6 %collective-permute-done.17 = bf16[2,192,2304]{2,1,0:T(8,128)(2,1)} collective-permute-done((bf16[2,192,2304]{2,1,0:T(8,128)(2,1)}, bf16[2,192,2304]{2,1,0:T(8,128)(2,1)}, u32[]{:S(2)}, u32[]{:S(2)}) %collective-permute-start.17) | collective-permute-done | bytes 1769504 | tf_op jit(solution)/shard_map/ppermute | solution.py:661
  322.6 8.0 fusion.7
  330.6 8.7 multiply_convert_fusion.1
  344.0 36.2 %self_forward.1 = (bf16[1024,768]{1,0:T(8,128)(2,1)}, bf16[1024,768]{1,0:T(8,128)(2,1)}, bf16[1024,768]{1,0:T(8,128)(2,1)}, bf16[512,768]{1,0:T(8,128)(2,1)}, bf...) custom-call(bf16[1024,1536]{1,0:T(8,128)(2,1)} %copy.201.rows_ref, bf16[2,768,1152]{2,1,0:T(8,128)(2,1)} %pad_maximum_fusion.6.own_ref, ...), custom_call_target="tpu_custom_call" | custom-call | flops 13690208256 | bytes 16515072 | tf_op jit(solution)/shard_map/self_forward/pallas_call | solution.py:493
  381.7 13.9 collective-permute-done.22
  395.7 6.6 pad_maximum_fusion.4.own_ref
  402.3 68.1 %collective-permute-done.18 = bf16[768,2304]{1,0:T(8,128)(2,1)} collective-permute-done((bf16[768,2304]{1,0:T(8,128)(2,1)}, bf16[768,2304]{1,0:T(8,128)(2,1)}, u32[]{:S(2)}, u32[]{:S(2)}) %collective-permute-start.18) | collective-permute-done | bytes 3538976 | tf_op jit(solution)/shard_map/ppermute | solution.py:661
  470.4 6.7 pad_maximum_fusion.3.own_ref
  479.0 5.9 fusion.33
  484.9 5.8 slice_bitcast_fusion.5
  494.9 9.3 copy.206
  504.2 11.5 reshape_reshape.29
  515.7 9.3 copy.207
  533.1 8.9 maximum_bitcast_fusion
  542.0 9.4 copy.204
  551.4 11.4 reshape.340
  562.8 7.3 fusion.87
  570.2 9.3 copy.209
  579.5 11.4 reshape.343
  591.3 6.3 fusion.27
  599.6 9.9 copy.212
  609.4 11.8 reshape.346
  635.0 9.4 fusion.79
  649.1 21.5 %collective-permute-done.14 = bf16[512,1536]{0,1:T(8,128)(2,1)} collective-permute-done((bf16[512,1536]{0,1:T(8,128)(2,1)}, bf16[512,1536]{0,1:T(8,128)(2,1)}, u32[]{:S(2)}, u32[]{:S(2)}) %collective-permute-start.14) | collective-permute-done | bytes 1572896 | tf_op jit(solution)/shard_map/ppermute | solution.py:661
  680.7 53.5 %feed_forward.2 = (f32[1024,1536]{1,0:T(8,128)}, f32[1024,1536]{1,0:T(8,128)}, bf16[2,768,2304]{2,1,0:T(8,128)(2,1)}, bf16[2,768,2304]{2,1,0:T(8,128)(2,1)}) custom-call(bf16[1024,1536]{1,0:T(8,128)(2,1)} %copy.225.rows_ref, bf16[1536,1024]{1,0:T(8,128)(2,1)} %get-tuple-element.126.across_ref, bf16[1024,1536]{1,0:T(8,128)(2,1)} %copy.226.dy_ref, ...), custom_call_target="tpu_custom_call" | custom-call | flops 43486543872 | bytes 66060288 | tf_op jit(solution)/shard_map/feed_forward/pallas_call | solution.py:622
  734.2 57.0 %feed_forward.3 = (f32[1024,1536]{1,0:T(8,128)}, f32[1024,1536]{1,0:T(8,128)}, bf16[2,768,2304]{2,1,0:T(8,128)(2,1)}, bf16[2,768,2304]{2,1,0:T(8,128)(2,1)}) custom-call(bf16[1024,1536]{1,0:T(8,128)(2,1)} %copy.225.rows_ref, bf16[1536,1024]{1,0:T(8,128)(2,1)} %get-tuple-element.126.across_ref, ...), custom_call_target="tpu_custom_call", output_to_operand_aliasing={{0}: (6, {}), {1}: (7, {})} | custom-call | flops 43486543872 | bytes 66060288 | tf_op jit(solution)/shard_map/feed_forward/pallas_call | solution.py:622
  791.3 6.6 copy.231
  802.5 6.6 copy.227
  813.5 25.1 %collective-permute-done.25 = bf16[512,1536]{0,1:T(8,128)(2,1)} collective-permute-done((bf16[512,1536]{0,1:T(8,128)(2,1)}, bf16[512,1536]{0,1:T(8,128)(2,1)}, u32[]{:S(2)}, u32[]{:S(2)}) %collective-permute-start.25) | collective-permute-done | bytes 1572896 | tf_op jit(solution)/shard_map/ppermute | solution.py:661
  842.1 29.0 %collective-permute-done.24 = bf16[512,1536]{0,1:T(8,128)(2,1)} collective-permute-done((bf16[512,1536]{0,1:T(8,128)(2,1)}, bf16[512,1536]{0,1:T(8,128)(2,1)}, u32[]{:S(2)}, u32[]{:S(2)}) %collective-permute-start.24) | collective-permute-done | bytes 1572896 | tf_op jit(solution)/shard_map/ppermute | solution.py:661
  871.1 6.8 multiply_add_fusion.2
  888.3 8.0 multiply_reduce_fusion
  914.8 6.8 fusion.4
  930.7 11.8 reshape.358
  953.4 7.5 pad_maximum_fusion.1
  979.9 38.3 %self_backward.1 = bf16[1024,2304]{1,0:T(8,128)(2,1)} custom-call(bf16[1024,768]{1,0:T(8,128)(2,1)} %get-tuple-element.33.q_ref, bf16[1024,768]{1,0:T(8,128)(2,1)} %get-tuple-element.34.k_ref, bf16[1024,768]{1,0:T(8,128)(2,1)} %get-tuple-element.35.v_ref, bf16[512,768]{1,0:T(8,128)(2,1)} %get-tuple-element.27.mine_ref, ...), custom_call_target="tpu_custom_call" | custom-call | flops 16106127360 | bytes 15728640 | tf_op jit(solution)/shard_map/self_backward/pallas_call | solution.py:554
  1034.3 8.3 fusion.9
  1056.3 8.4 convolution_convert_fusion.5
  1073.0 18.3 %collective-permute-done.27 = bf16[512,1536]{0,1:T(8,128)(2,1)} collective-permute-done((bf16[512,1536]{0,1:T(8,128)(2,1)}, bf16[512,1536]{0,1:T(8,128)(2,1)}, u32[]{:S(2)}, u32[]{:S(2)}) %collective-permute-start.27) | collective-permute-done | bytes 1572896 | tf_op jit(solution)/shard_map/ppermute | solution.py:661
  1094.7 20.5 %collective-permute-done.40 = bf16[1,768,768]{2,1,0:T(8,128)(2,1)S(1)} collective-permute-done((bf16[1,768,768]{2,1,0:T(8,128)(2,1)S(1)}, bf16[1,768,768]{2,1,0:T(8,128)(2,1)S(1)}, u32[]{:S(2)}, u32[]{:S(2)}) %collective-permute-start.40) | collective-permute-done | bytes 1179680 | tf_op jit(solution)/shard_map/ppermute | solution.py:661
  1121.5 9.3 collective-permute-done.41
  1140.4 9.5 add_convert_fusion.1
  1155.5 9.5 add_convert_fusion
  1165.0 16.6 %collective-permute-done.36 = bf16[768,1152]{1,0:T(8,128)(2,1)} collective-permute-done((bf16[768,1152]{1,0:T(8,128)(2,1)S(1)}, bf16[768,1152]{1,0:T(8,128)(2,1)}, u32[]{:S(2)}, u32[]{:S(2)}) %collective-permute-start.36) | collective-permute-done | bytes 1769504 | tf_op jit(solution)/shard_map/ppermute | solution.py:661
  1191.3 14.1 collective-permute-done.37
  1206.3 9.9 add_convert_fusion.2
  1221.1 36.3 %collective-permute-done.54 = bf16[768,2304]{1,0:T(8,128)(2,1)} collective-permute-done((bf16[768,2304]{1,0:T(8,128)(2,1)}, bf16[768,2304]{1,0:T(8,128)(2,1)}, u32[]{:S(2)}, u32[]{:S(2)}) %collective-permute-start.54) | collective-permute-done | bytes 3538976 | tf_op jit(solution)/shard_map/ppermute | solution.py:661
  1263.3 66.6 %collective-permute-done.58 = bf16[768,2304]{1,0:T(8,128)(2,1)} collective-permute-done((bf16[768,2304]{1,0:T(8,128)(2,1)}, bf16[768,2304]{1,0:T(8,128)(2,1)}, u32[]{:S(2)}, u32[]{:S(2)}) %collective-permute-start.58) | collective-permute-done | bytes 3538976 | tf_op jit(solution)/shard_map/ppermute | solution.py:661
  1348.4 44.2 %collective-permute-done.59 = bf16[2,192,2304]{2,1,0:T(8,128)(2,1)} collective-permute-done((bf16[2,192,2304]{2,1,0:T(8,128)(2,1)}, bf16[2,192,2304]{2,1,0:T(8,128)(2,1)}, u32[]{:S(2)}, u32[]{:S(2)}) %collective-permute-start.59) | collective-permute-done | bytes 1769504 | tf_op jit(solution)/shard_map/ppermute | solution.py:661
  1401.2 31.9 %collective-permute-done.60 = bf16[1,192,2304]{2,1,0:T(8,128)(2,1)S(1)} collective-permute-done((bf16[1,192,2304]{2,1,0:T(8,128)(2,1)S(1)}, bf16[1,192,2304]{2,1,0:T(8,128)(2,1)S(1)}, u32[]{:S(2)}, u32[]{:S(2)}) %collective-permute-start.60) | collective-permute-done | bytes 884768 | tf_op jit(solution)/shard_map/ppermute | solution.py:661
  1435.3 6.3 reshape.359
  1447.3 6.6 reshape.360
  1466.2 9.6 collective-permute-done.49
  1476.0 5.8 collective-permute-done.47
  1482.0 8.8 collective-permute-done.50
  (528 shorter events, 384.1 us)
Async XLA Ops:
  2.8 30.1 %collective-permute-start.9 = (bf16[1,192,1536]{2,1,0:T(8,128)(2,1)S(1)}, bf16[1,192,1536]{2,1,0:T(8,128)(2,1)S(1)}, u32[]{:S(2)}, u32[]{:S(2)}) collective-permute-start(bf16[1,192,1536]{2,1,0:T(8,128)(2,1)S(1)} %maximum_bitcast_fusion.9), channel_id=1, source_target_pairs={{0,16},{4,20},{8,24},{12,28},{16,0},{20,4},{24,8},{28,12},{1,17},{... | collective-permute-start | bytes 1769480 | tf_op jit(solution)/shard_map/ppermute | solution.py:661
  35.2 27.4 %collective-permute-start.10 = (bf16[2,192,1536]{2,1,0:T(8,128)(2,1)}, bf16[2,192,1536]{2,1,0:T(8,128)(2,1)S(1)}, u32[]{:S(2)}, u32[]{:S(2)}) collective-permute-start(bf16[2,192,1536]{2,1,0:T(8,128)(2,1)} %maximum_bitcast_fusion.7), channel_id=1, source_target_pairs={{0,8},{4,12},{8,0},{12,4},{16,24},{20,28},{24,16},{28,20},{1,9},{5... | collective-permute-start | bytes 3538952 | tf_op jit(solution)/shard_map/ppermute | solution.py:661
  64.4 51.8 %collective-permute-start.11 = (bf16[768,1536]{1,0:T(8,128)(2,1)}, bf16[768,1536]{1,0:T(8,128)(2,1)}, u32[]{:S(2)}, u32[]{:S(2)}) collective-permute-start(bf16[768,1536]{1,0:T(8,128)(2,1)} %bitcast.31), channel_id=1, source_target_pairs={{0,2},{2,0},{1,3},{3,1},{4,6},{6,4},{5,7},{7,5},{8,10},{10,8},{9,1... | collective-permute-start | bytes 7077896 | tf_op jit(solution)/shard_map/ppermute | solution.py:661
  74.8 95.1 %collective-permute-start.20 = (bf16[1,192,2304]{2,1,0:T(8,128)(2,1)}, bf16[1,192,2304]{2,1,0:T(8,128)(2,1)}, u32[]{:S(2)}, u32[]{:S(2)}) collective-permute-start(bf16[1,192,2304]{2,1,0:T(8,128)(2,1)} %slice.256), channel_id=1, source_target_pairs={{0,16},{4,20},{8,24},{12,28},{16,0},{20,4},{24,8},{28,12},{1,17},{... | collective-permute-start | bytes 2654216 | tf_op jit(solution)/shard_map/ppermute | solution.py:661
  80.1 87.8 %collective-permute-start.4 = (bf16[1,192,1152]{2,1,0:T(8,128)(2,1)}, bf16[1,192,1152]{2,1,0:T(8,128)(2,1)}, u32[]{:S(2)}, u32[]{:S(2)}) collective-permute-start(bf16[1,192,1152]{2,1,0:T(8,128)(2,1)} %broadcast_in_dim_reshape.3), channel_id=1, source_target_pairs={{0,16},{4,20},{8,24},{12,28},{16,0},{20,4},{24,8},{28,12},{1,17},{... | collective-permute-start | bytes 1327112 | tf_op jit(solution)/shard_map/ppermute | solution.py:661
  87.2 475.6 %copy-start.6 = (bf16[512,4,1,192]{0,3,2,1:T(8,128)(2,1)}, bf16[512,4,1,192]{0,3,2,1:T(8,128)(2,1)S(1)}, u32[]{:S(2)}) copy-start(bf16[512,4,1,192]{0,3,2,1:T(8,128)(2,1)S(1)} %get-tuple-element.181) | copy-start | bytes 2359300
  87.2 475.6 %copy-start.8 = (bf16[512,4,1,192]{0,3,2,1:T(8,128)(2,1)}, bf16[512,4,1,192]{0,3,2,1:T(8,128)(2,1)S(1)}, u32[]{:S(2)}) copy-start(bf16[512,4,1,192]{0,3,2,1:T(8,128)(2,1)S(1)} %get-tuple-element.182) | copy-start | bytes 2359300
  88.5 233.1 %collective-permute-start = (bf16[512,1536]{0,1:T(8,128)(2,1)}, bf16[512,1536]{0,1:T(8,128)(2,1)S(1)}, u32[]{:S(2)}, u32[]{:S(2)}) collective-permute-start(bf16[512,1536]{0,1:T(8,128)(2,1)} %pad_maximum_fusion.16), channel_id=1, source_target_pairs={{0,1},{1,0},{2,3},{3,2},{4,5},{5,4},{6,7},{7,6},{8,9},{9,8},{10,11... | collective-permute-start | bytes 4718600 | tf_op jit(solution)/shard_map/ppermute | solution.py:661
  91.2 49.3 %collective-permute-start.1 = (bf16[1,3,192]{2,1,0:T(4,128)(2,1)}, bf16[1,3,192]{2,1,0:T(4,128)(2,1)}, u32[]{:S(2)}, u32[]{:S(2)}) collective-permute-start(bf16[1,3,192]{2,1,0:T(4,128)(2,1)} %maximum_bitcast_fusion.11), channel_id=1, source_target_pairs={{0,16},{4,20},{8,24},{12,28},{16,0},{20,4},{24,8},{28,12},{1,17},{... | collective-permute-start | bytes 3464 | tf_op jit(solution)/shard_map/ppermute | solution.py:661
  122.7 102.4 %collective-permute-start.12 = (bf16[2,768,1536]{2,1,0:T(8,128)(2,1)}, bf16[2,768,1536]{2,1,0:T(8,128)(2,1)}, u32[]{:S(2)}, u32[]{:S(2)}) collective-permute-start(bf16[2,768,1536]{2,1,0:T(8,128)(2,1)} %get-tuple-element.113), channel_id=1, source_target_pairs={{0,1},{1,0},{2,3},{3,2},{4,5},{5,4},{6,7},{7,6},{8,9},{9,8},{10,11... | collective-permute-start | bytes 14155784 | tf_op jit(solution)/shard_map/ppermute | solution.py:661
  139.2 389.4 %copy-start.50 = (bf16[130,768]{1,0:T(8,128)(2,1)}, bf16[130,768]{1,0:T(8,128)(2,1)S(1)}, u32[]{:S(2)}) copy-start(bf16[130,768]{1,0:T(8,128)(2,1)S(1)} %constant_dynamic-update-slice_fusion.2) | copy-start | bytes 599044
  141.2 23.1 %collective-permute-start.2 = (bf16[2,3,192]{2,1,0:T(4,128)(2,1)S(1)}, bf16[2,3,192]{2,1,0:T(4,128)(2,1)S(1)}, u32[]{:S(2)}, u32[]{:S(2)}) collective-permute-start(bf16[2,3,192]{2,1,0:T(4,128)(2,1)S(1)} %maximum_bitcast_fusion.10), channel_id=1, source_target_pairs={{0,8},{4,12},{8,0},{12,4},{16,24},{20,28},{24,16},{28,20},{1,9},{5... | collective-permute-start | bytes 6920 | tf_op jit(solution)/shard_map/ppermute | solution.py:661
  164.3 74.2 %collective-permute-start.16 = (bf16[1,192,2304]{2,1,0:T(8,128)(2,1)}, bf16[1,192,2304]{2,1,0:T(8,128)(2,1)}, u32[]{:S(2)}, u32[]{:S(2)}) collective-permute-start(bf16[1,192,2304]{2,1,0:T(8,128)(2,1)} %slice.254), channel_id=1, source_target_pairs={{0,16},{4,20},{8,24},{12,28},{16,0},{20,4},{24,8},{28,12},{1,17},{... | collective-permute-start | bytes 2654216 | tf_op jit(solution)/shard_map/ppermute | solution.py:661
  167.8 1.4 collective-permute-start.3
  169.3 40.6 %collective-permute-start.5 = (bf16[2,192,1152]{2,1,0:T(8,128)(2,1)S(1)}, bf16[2,192,1152]{2,1,0:T(8,128)(2,1)S(1)}, u32[]{:S(2)}, u32[]{:S(2)}) collective-permute-start(bf16[2,192,1152]{2,1,0:T(8,128)(2,1)S(1)} %maximum_bitcast_fusion.8), channel_id=1, source_target_pairs={{0,8},{4,12},{8,0},{12,4},{16,24},{20,28},{24,16},{28,20},{1,9},{5... | collective-permute-start | bytes 2654216 | tf_op jit(solution)/shard_map/ppermute | solution.py:661
  211.6 40.6 %collective-permute-start.6 = (bf16[768,1152]{1,0:T(8,128)(2,1)}, bf16[768,1152]{1,0:T(8,128)(2,1)}, u32[]{:S(2)}, u32[]{:S(2)}) collective-permute-start(bf16[768,1152]{1,0:T(8,128)(2,1)} %bitcast.17), channel_id=1, source_target_pairs={{0,2},{2,0},{1,3},{3,1},{4,6},{6,4},{5,7},{7,5},{8,10},{10,8},{9,1... | collective-permute-start | bytes 5308424 | tf_op jit(solution)/shard_map/ppermute | solution.py:661
  233.5 251.4 %collective-permute-start.13 = (bf16[2,2,768,1536]{3,2,1,0:T(8,128)(2,1)}, bf16[2,2,768,1536]{3,2,1,0:T(8,128)(2,1)}, u32[]{:S(2)}, u32[]{:S(2)}) collective-permute-start(bf16[2,2,768,1536]{3,2,1,0:T(8,128)(2,1)} %pad_maximum_fusion), channel_id=1, source_target_pairs={{0,4},{4,0},{8,12},{12,8},{16,20},{20,16},{24,28},{28,24},{1,5},{5... | collective-permute-start | bytes 28311560 | tf_op jit(solution)/shard_map/ppermute | solution.py:661
  236.4 41.9 %collective-permute-start.21 = (bf16[2,192,2304]{2,1,0:T(8,128)(2,1)}, bf16[2,192,2304]{2,1,0:T(8,128)(2,1)}, u32[]{:S(2)}, u32[]{:S(2)}) collective-permute-start(bf16[2,192,2304]{2,1,0:T(8,128)(2,1)} %maximum_bitcast_fusion.6), channel_id=1, source_target_pairs={{0,8},{4,12},{8,0},{12,4},{16,24},{20,28},{24,16},{28,20},{1,9},{5... | collective-permute-start | bytes 5308424 | tf_op jit(solution)/shard_map/ppermute | solution.py:661
  242.1 73.9 %collective-permute-start.17 = (bf16[2,192,2304]{2,1,0:T(8,128)(2,1)}, bf16[2,192,2304]{2,1,0:T(8,128)(2,1)}, u32[]{:S(2)}, u32[]{:S(2)}) collective-permute-start(bf16[2,192,2304]{2,1,0:T(8,128)(2,1)} %maximum_bitcast_fusion.5), channel_id=1, source_target_pairs={{0,8},{4,12},{8,0},{12,4},{16,24},{20,28},{24,16},{28,20},{1,9},{5... | collective-permute-start | bytes 5308424 | tf_op jit(solution)/shard_map/ppermute | solution.py:661
  252.3 382.7 %collective-permute-start.15 = (bf16[512,1536]{0,1:T(8,128)(2,1)}, bf16[512,1536]{0,1:T(8,128)(2,1)}, u32[]{:S(2)}, u32[]{:S(2)}) collective-permute-start(bf16[512,1536]{0,1:T(8,128)(2,1)} %pad_maximum_fusion.17), channel_id=1, source_target_pairs={{0,1},{1,0},{2,3},{3,2},{4,5},{5,4},{6,7},{7,6},{8,9},{9,8},{10,11... | collective-permute-start | bytes 4718600 | tf_op jit(solution)/shard_map/ppermute | solution.py:661
  278.3 65.7 %collective-permute-start.7 = (bf16[2,768,1152]{2,1,0:T(8,128)(2,1)}, bf16[2,768,1152]{2,1,0:T(8,128)(2,1)}, u32[]{:S(2)}, u32[]{:S(2)}) collective-permute-start(bf16[2,768,1152]{2,1,0:T(8,128)(2,1)} %pad_maximum_fusion.6.own_ref), channel_id=1, source_target_pairs={{0,4},{4,0},{8,12},{12,8},{16,20},{20,16},{24,28},{28,24},{1,5},{5... | collective-permute-start | bytes 10616840 | tf_op jit(solution)/shard_map/ppermute | solution.py:661
  315.9 79.7 %collective-permute-start.22 = (bf16[768,2304]{1,0:T(8,128)(2,1)}, bf16[768,2304]{1,0:T(8,128)(2,1)}, u32[]{:S(2)}, u32[]{:S(2)}) collective-permute-start(bf16[768,2304]{1,0:T(8,128)(2,1)} %bitcast.76), channel_id=1, source_target_pairs={{0,2},{2,0},{1,3},{3,1},{4,6},{6,4},{5,7},{7,5},{8,10},{10,8},{9,1... | collective-permute-start | bytes 10616840 | tf_op jit(solution)/shard_map/ppermute | solution.py:661
  321.5 148.9 %collective-permute-start.18 = (bf16[768,2304]{1,0:T(8,128)(2,1)}, bf16[768,2304]{1,0:T(8,128)(2,1)}, u32[]{:S(2)}, u32[]{:S(2)}) collective-permute-start(bf16[768,2304]{1,0:T(8,128)(2,1)} %bitcast.68), channel_id=1, source_target_pairs={{0,2},{2,0},{1,3},{3,1},{4,6},{6,4},{5,7},{7,5},{8,10},{10,8},{9,1... | collective-permute-start | bytes 10616840 | tf_op jit(solution)/shard_map/ppermute | solution.py:661
  380.2 97.9 %collective-permute-start.8 = (bf16[512,768]{1,0:T(8,128)(2,1)}, bf16[512,768]{1,0:T(8,128)(2,1)S(1)}, u32[]{:S(2)}, u32[]{:S(2)}) collective-permute-start(bf16[512,768]{1,0:T(8,128)(2,1)} %get-tuple-element.28.theirs_ref), channel_id=1, source_target_pairs={{0,1},{1,0},{2,3},{3,2},{4,5},{5,4},{6,7},{7,6},{8,9},{9,8},{10,11... | collective-permute-start | bytes 2359304 | tf_op jit(solution)/shard_map/ppermute | solution.py:661
  402.3 278.4 %collective-permute-start.23 = (bf16[2,768,2304]{2,1,0:T(8,128)(2,1)}, bf16[2,768,2304]{2,1,0:T(8,128)(2,1)}, u32[]{:S(2)}, u32[]{:S(2)}) collective-permute-start(bf16[2,768,2304]{2,1,0:T(8,128)(2,1)} %pad_maximum_fusion.4.own_ref), channel_id=1, source_target_pairs={{0,4},{4,0},{8,12},{12,8},{16,20},{20,16},{24,28},{28,24},{1,5},{5... | collective-permute-start | bytes 21233672 | tf_op jit(solution)/shard_map/ppermute | solution.py:661
  477.1 257.1 %collective-permute-start.19 = (bf16[2,768,2304]{2,1,0:T(8,128)(2,1)}, bf16[2,768,2304]{2,1,0:T(8,128)(2,1)}, u32[]{:S(2)}, u32[]{:S(2)}) collective-permute-start(bf16[2,768,2304]{2,1,0:T(8,128)(2,1)} %pad_maximum_fusion.3.own_ref), channel_id=1, source_target_pairs={{0,4},{4,0},{8,12},{12,8},{16,20},{20,16},{24,28},{28,24},{1,5},{5... | collective-permute-start | bytes 21233672 | tf_op jit(solution)/shard_map/ppermute | solution.py:661
  633.5 37.1 %collective-permute-start.14 = (bf16[512,1536]{0,1:T(8,128)(2,1)}, bf16[512,1536]{0,1:T(8,128)(2,1)}, u32[]{:S(2)}, u32[]{:S(2)}) collective-permute-start(bf16[512,1536]{0,1:T(8,128)(2,1)} %multiply_convert_fusion.3), channel_id=1, source_target_pairs={{0,1},{1,0},{2,3},{3,2},{4,5},{5,4},{6,7},{7,6},{8,9},{9,8},{10,11... | collective-permute-start | bytes 4718600 | tf_op jit(solution)/shard_map/ppermute | solution.py:661
  801.0 37.6 %collective-permute-start.25 = (bf16[512,1536]{0,1:T(8,128)(2,1)}, bf16[512,1536]{0,1:T(8,128)(2,1)}, u32[]{:S(2)}, u32[]{:S(2)}) collective-permute-start(bf16[512,1536]{0,1:T(8,128)(2,1)} %slice.524), channel_id=1, source_target_pairs={{0,1},{1,0},{2,3},{3,2},{4,5},{5,4},{6,7},{7,6},{8,9},{9,8},{10,11... | collective-permute-start | bytes 4718600 | tf_op jit(solution)/shard_map/ppermute | solution.py:661
  812.4 58.7 %collective-permute-start.24 = (bf16[512,1536]{0,1:T(8,128)(2,1)}, bf16[512,1536]{0,1:T(8,128)(2,1)}, u32[]{:S(2)}, u32[]{:S(2)}) collective-permute-start(bf16[512,1536]{0,1:T(8,128)(2,1)} %slice.525), channel_id=1, source_target_pairs={{0,1},{1,0},{2,3},{3,2},{4,5},{5,4},{6,7},{7,6},{8,9},{9,8},{10,11... | collective-permute-start | bytes 4718600 | tf_op jit(solution)/shard_map/ppermute | solution.py:661
  813.0 327.4 %collective-permute-start.53 = (bf16[2,768,2304]{2,1,0:T(8,128)(2,1)}, bf16[2,768,2304]{2,1,0:T(8,128)(2,1)}, u32[]{:S(2)}, u32[]{:S(2)}) collective-permute-start(bf16[2,768,2304]{2,1,0:T(8,128)(2,1)} %get-tuple-element.38), channel_id=1, source_target_pairs={{0,4},{4,0},{8,12},{12,8},{16,20},{20,16},{24,28},{28,24},{1,5},{5... | collective-permute-start | bytes 21233672 | tf_op jit(solution)/shard_map/ppermute | solution.py:661
  813.1 342.4 %collective-permute-start.57 = (bf16[2,768,2304]{2,1,0:T(8,128)(2,1)}, bf16[2,768,2304]{2,1,0:T(8,128)(2,1)}, u32[]{:S(2)}, u32[]{:S(2)}) collective-permute-start(bf16[2,768,2304]{2,1,0:T(8,128)(2,1)} %get-tuple-element.40), channel_id=1, source_target_pairs={{0,4},{4,0},{8,12},{12,8},{16,20},{20,16},{24,28},{28,24},{1,5},{5... | collective-permute-start | bytes 21233672 | tf_op jit(solution)/shard_map/ppermute | solution.py:661
  949.2 30.8 %collective-permute-start.26 = (bf16[512,768]{1,0:T(8,128)(2,1)}, bf16[512,768]{1,0:T(8,128)(2,1)}, u32[]{:S(2)}, u32[]{:S(2)}) collective-permute-start(bf16[512,768]{1,0:T(8,128)(2,1)} %get-tuple-element.141), channel_id=1, source_target_pairs={{0,1},{1,0},{2,3},{3,2},{4,5},{5,4},{6,7},{7,6},{8,9},{9,8},{10,11... | collective-permute-start | bytes 2359304 | tf_op jit(solution)/shard_map/ppermute | solution.py:661
  952.7 21.1 %collective-permute-start.28 = (f32[130,2,192]{2,0,1:T(8,128)S(1)}, f32[130,2,192]{2,0,1:T(8,128)}, u32[]{:S(2)}, u32[]{:S(2)}) collective-permute-start(f32[130,2,192]{2,0,1:T(8,128)S(1)} %dynamic-slice_bitcast_fusion.7), channel_id=1, source_target_pairs={{0,1},{1,0},{2,3},{3,2},{4,5},{5,4},{6,7},{7,6},{8,9},{9,8},{10,11... | collective-permute-start | bytes 599048 | tf_op jit(solution)/shard_map/ppermute | solution.py:661
  971.9 92.8 %collective-permute-start.39 = (bf16[1,768,1536]{2,1,0:T(8,128)(2,1)}, bf16[1,768,1536]{2,1,0:T(8,128)(2,1)}, u32[]{:S(2)}, u32[]{:S(2)}) collective-permute-start(bf16[1,768,1536]{2,1,0:T(8,128)(2,1)} %slice.363), channel_id=1, source_target_pairs={{0,4},{4,0},{8,12},{12,8},{16,20},{20,16},{24,28},{28,24},{1,5},{5... | collective-permute-start | bytes 7077896 | tf_op jit(solution)/shard_map/ppermute | solution.py:661
  974.8 5.1 collective-permute-start.29
  1042.6 1.2 collective-permute-start.30
  1043.8 6.9 collective-permute-start.31
  1050.8 3.8 collective-permute-start.32
  1053.7 37.6 %collective-permute-start.27 = (bf16[512,1536]{0,1:T(8,128)(2,1)}, bf16[512,1536]{0,1:T(8,128)(2,1)}, u32[]{:S(2)}, u32[]{:S(2)}) collective-permute-start(bf16[512,1536]{0,1:T(8,128)(2,1)} %fusion.24), channel_id=1, source_target_pairs={{0,1},{1,0},{2,3},{3,2},{4,5},{5,4},{6,7},{7,6},{8,9},{9,8},{10,11... | collective-permute-start | bytes 4718600 | tf_op jit(solution)/shard_map/ppermute | solution.py:661
  1054.7 9.9 collective-permute-start.33
  1064.7 69.3 %collective-permute-start.35 = (bf16[768,2304]{1,0:T(8,128)(2,1)}, bf16[768,2304]{1,0:T(8,128)(2,1)}, u32[]{:S(2)}, u32[]{:S(2)}) collective-permute-start(bf16[768,2304]{1,0:T(8,128)(2,1)} %convolution_convert_fusion.4), channel_id=1, source_target_pairs={{0,4},{4,0},{8,12},{12,8},{16,20},{20,16},{24,28},{28,24},{1,5},{5... | collective-permute-start | bytes 10616840 | tf_op jit(solution)/shard_map/ppermute | solution.py:661
  1064.7 6.2 collective-permute-start.34
  1070.9 44.3 %collective-permute-start.40 = (bf16[1,768,768]{2,1,0:T(8,128)(2,1)S(1)}, bf16[1,768,768]{2,1,0:T(8,128)(2,1)S(1)}, u32[]{:S(2)}, u32[]{:S(2)}) collective-permute-start(bf16[1,768,768]{2,1,0:T(8,128)(2,1)S(1)} %slice.365), channel_id=1, source_target_pairs={{0,1},{1,0},{2,3},{3,2},{4,5},{5,4},{6,7},{7,6},{8,9},{9,8},{10,11... | collective-permute-start | bytes 3538952 | tf_op jit(solution)/shard_map/ppermute | solution.py:661
  1091.3 115.0 %collective-permute-start.44 = (bf16[3,768,1536]{2,1,0:T(8,128)(2,1)}, bf16[3,768,1536]{2,1,0:T(8,128)(2,1)}, u32[]{:S(2)}, u32[]{:S(2)}) collective-permute-start(bf16[3,768,1536]{2,1,0:T(8,128)(2,1)} %slice.369), channel_id=1, source_target_pairs={{0,4},{4,0},{8,12},{12,8},{16,20},{20,16},{24,28},{28,24},{1,5},{5... | collective-permute-start | bytes 21233672 | tf_op jit(solution)/shard_map/ppermute | solution.py:661
  1116.5 14.4 collective-permute-start.41
  1132.3 54.9 %collective-permute-start.42 = (bf16[2,192,384]{2,1,0:T(8,128)(2,1)S(1)}, bf16[2,192,384]{2,1,0:T(8,128)(2,1)S(1)}, u32[]{:S(2)}, u32[]{:S(2)}) collective-permute-start(bf16[2,192,384]{2,1,0:T(8,128)(2,1)S(1)} %dynamic-slice_bitcast_fusion.6), channel_id=1, source_target_pairs={{0,8},{4,12},{8,0},{12,4},{16,24},{20,28},{24,16},{28,20},{1,9},{5... | collective-permute-start | bytes 884744 | tf_op jit(solution)/shard_map/ppermute | solution.py:661
  1139.9 41.7 %collective-permute-start.36 = (bf16[768,1152]{1,0:T(8,128)(2,1)S(1)}, bf16[768,1152]{1,0:T(8,128)(2,1)}, u32[]{:S(2)}, u32[]{:S(2)}) collective-permute-start(bf16[768,1152]{1,0:T(8,128)(2,1)S(1)} %slice.361), channel_id=1, source_target_pairs={{0,2},{2,0},{1,3},{3,1},{4,6},{6,4},{5,7},{7,5},{8,10},{10,8},{9,1... | collective-permute-start | bytes 5308424 | tf_op jit(solution)/shard_map/ppermute | solution.py:661
  1153.9 103.5 %collective-permute-start.54 = (bf16[768,2304]{1,0:T(8,128)(2,1)}, bf16[768,2304]{1,0:T(8,128)(2,1)}, u32[]{:S(2)}, u32[]{:S(2)}) collective-permute-start(bf16[768,2304]{1,0:T(8,128)(2,1)} %slice_bitcast_fusion.2), channel_id=1, source_target_pairs={{0,2},{2,0},{1,3},{3,1},{4,6},{6,4},{5,7},{7,5},{8,10},{10,8},{9,1... | collective-permute-start | bytes 10616840 | tf_op jit(solution)/shard_map/ppermute | solution.py:661
  1184.1 21.2 %collective-permute-start.37 = (bf16[2,192,1152]{2,1,0:T(8,128)(2,1)S(1)}, bf16[2,192,1152]{2,1,0:T(8,128)(2,1)S(1)}, u32[]{:S(2)}, u32[]{:S(2)}) collective-permute-start(bf16[2,192,1152]{2,1,0:T(8,128)(2,1)S(1)} %dynamic-slice_bitcast_fusion.2), channel_id=1, source_target_pairs={{0,8},{4,12},{8,0},{12,4},{16,24},{20,28},{24,16},{28,20},{1,9},{5... | collective-permute-start | bytes 2654216 | tf_op jit(solution)/shard_map/ppermute | solution.py:661
  1186.7 143.2 %collective-permute-start.58 = (bf16[768,2304]{1,0:T(8,128)(2,1)}, bf16[768,2304]{1,0:T(8,128)(2,1)}, u32[]{:S(2)}, u32[]{:S(2)}) collective-permute-start(bf16[768,2304]{1,0:T(8,128)(2,1)} %slice_bitcast_fusion), channel_id=1, source_target_pairs={{0,2},{2,0},{1,3},{3,1},{4,6},{6,4},{5,7},{7,5},{8,10},{10,8},{9,1... | collective-permute-start | bytes 10616840 | tf_op jit(solution)/shard_map/ppermute | solution.py:661
  1187.3 149.2 %collective-permute-start.43 = (bf16[1,192,384]{2,1,0:T(8,128)(2,1)S(1)}, bf16[1,192,384]{2,1,0:T(8,128)(2,1)S(1)}, u32[]{:S(2)}, u32[]{:S(2)}) collective-permute-start(bf16[1,192,384]{2,1,0:T(8,128)(2,1)S(1)} %constant_dynamic-slice_fusion.5), channel_id=1, source_target_pairs={{0,16},{4,20},{8,24},{12,28},{16,0},{20,4},{24,8},{28,12},{1,17},{... | collective-permute-start | bytes 442376 | tf_op jit(solution)/shard_map/ppermute | solution.py:661
  1205.6 131.6 %collective-permute-start.38 = (bf16[1,192,1152]{2,1,0:T(8,128)(2,1)S(1)}, bf16[1,192,1152]{2,1,0:T(8,128)(2,1)S(1)}, u32[]{:S(2)}, u32[]{:S(2)}) collective-permute-start(bf16[1,192,1152]{2,1,0:T(8,128)(2,1)S(1)} %constant_dynamic-slice_fusion.6), channel_id=1, source_target_pairs={{0,16},{4,20},{8,24},{12,28},{16,0},{20,4},{24,8},{28,12},{1,17},{... | collective-permute-start | bytes 1327112 | tf_op jit(solution)/shard_map/ppermute | solution.py:661
  1220.5 176.0 %collective-permute-start.45 = (bf16[3,768,768]{2,1,0:T(8,128)(2,1)}, bf16[3,768,768]{2,1,0:T(8,128)(2,1)}, u32[]{:S(2)}, u32[]{:S(2)}) collective-permute-start(bf16[3,768,768]{2,1,0:T(8,128)(2,1)} %slice.371), channel_id=1, source_target_pairs={{0,1},{1,0},{2,3},{3,2},{4,5},{5,4},{6,7},{7,6},{8,9},{9,8},{10,11... | collective-permute-start | bytes 10616840 | tf_op jit(solution)/shard_map/ppermute | solution.py:661
  1262.9 78.9 %collective-permute-start.55 = (bf16[2,192,2304]{2,1,0:T(8,128)(2,1)}, bf16[2,192,2304]{2,1,0:T(8,128)(2,1)}, u32[]{:S(2)}, u32[]{:S(2)}) collective-permute-start(bf16[2,192,2304]{2,1,0:T(8,128)(2,1)} %dynamic-slice_bitcast_fusion.1), channel_id=1, source_target_pairs={{0,8},{4,12},{8,0},{12,4},{16,24},{20,28},{24,16},{28,20},{1,9},{5... | collective-permute-start | bytes 5308424 | tf_op jit(solution)/shard_map/ppermute | solution.py:661
  1336.1 56.5 %collective-permute-start.59 = (bf16[2,192,2304]{2,1,0:T(8,128)(2,1)}, bf16[2,192,2304]{2,1,0:T(8,128)(2,1)}, u32[]{:S(2)}, u32[]{:S(2)}) collective-permute-start(bf16[2,192,2304]{2,1,0:T(8,128)(2,1)} %dynamic-slice_bitcast_fusion), channel_id=1, source_target_pairs={{0,8},{4,12},{8,0},{12,4},{16,24},{20,28},{24,16},{28,20},{1,9},{5... | collective-permute-start | bytes 5308424 | tf_op jit(solution)/shard_map/ppermute | solution.py:661
  1344.4 55.7 %collective-permute-start.56 = (bf16[1,192,2304]{2,1,0:T(8,128)(2,1)S(1)}, bf16[1,192,2304]{2,1,0:T(8,128)(2,1)S(1)}, u32[]{:S(2)}, u32[]{:S(2)}) collective-permute-start(bf16[1,192,2304]{2,1,0:T(8,128)(2,1)S(1)} %constant_dynamic-slice_fusion.1), channel_id=1, source_target_pairs={{0,16},{4,20},{8,24},{12,28},{16,0},{20,4},{24,8},{28,12},{1,17},{... | collective-permute-start | bytes 2654216 | tf_op jit(solution)/shard_map/ppermute | solution.py:661
  1394.6 38.5 %collective-permute-start.60 = (bf16[1,192,2304]{2,1,0:T(8,128)(2,1)S(1)}, bf16[1,192,2304]{2,1,0:T(8,128)(2,1)S(1)}, u32[]{:S(2)}, u32[]{:S(2)}) collective-permute-start(bf16[1,192,2304]{2,1,0:T(8,128)(2,1)S(1)} %constant_dynamic-slice_fusion), channel_id=1, source_target_pairs={{0,16},{4,20},{8,24},{12,28},{16,0},{20,4},{24,8},{28,12},{1,17},{... | collective-permute-start | bytes 2654216 | tf_op jit(solution)/shard_map/ppermute | solution.py:661
  1399.5 54.4 %collective-permute-start.46 = (bf16[3,768,384]{2,1,0:T(8,128)(2,1)S(1)}, bf16[3,768,384]{2,1,0:T(8,128)(2,1)}, u32[]{:S(2)}, u32[]{:S(2)}) collective-permute-start(bf16[3,768,384]{2,1,0:T(8,128)(2,1)S(1)} %slice.373), channel_id=1, source_target_pairs={{0,2},{2,0},{1,3},{3,1},{4,6},{6,4},{5,7},{7,5},{8,10},{10,8},{9,1... | collective-permute-start | bytes 5308424 | tf_op jit(solution)/shard_map/ppermute | solution.py:661
  1456.6 9.1 collective-permute-start.51
  1462.7 13.1 collective-permute-start.49
  1463.1 18.6 %collective-permute-start.47 = (bf16[2,192,384]{2,1,0:T(8,128)(2,1)S(1)}, bf16[2,192,384]{2,1,0:T(8,128)(2,1)S(1)}, u32[]{:S(2)}, u32[]{:S(2)}) collective-permute-start(bf16[2,192,384]{2,1,0:T(8,128)(2,1)S(1)} %dynamic-slice_bitcast_fusion.5), channel_id=1, source_target_pairs={{0,8},{4,12},{8,0},{12,4},{16,24},{20,28},{24,16},{28,20},{1,9},{5... | collective-permute-start | bytes 884744 | tf_op jit(solution)/shard_map/ppermute | solution.py:661
  1465.9 25.9 %collective-permute-start.52 = (bf16[1,192,384]{2,1,0:T(8,128)(2,1)S(1)}, bf16[1,192,384]{2,1,0:T(8,128)(2,1)S(1)}, u32[]{:S(2)}, u32[]{:S(2)}) collective-permute-start(bf16[1,192,384]{2,1,0:T(8,128)(2,1)S(1)} %constant_dynamic-slice_fusion.2), channel_id=1, source_target_pairs={{0,16},{4,20},{8,24},{12,28},{16,0},{20,4},{24,8},{28,12},{1,17},{... | collective-permute-start | bytes 442376 | tf_op jit(solution)/shard_map/ppermute | solution.py:661
  1475.9 14.8 collective-permute-start.50
  1481.9 11.5 collective-permute-start.48
  (96 other events, 1998.6 us)

commit v2 on v0

--- a/solution.py
+++ b/solution.py
@@ -1,6 +1,12 @@
+import functools
+import math
+
 import jax
 import jax.numpy as jnp
 from jax import lax
+from jax.experimental import pallas as pl
+from jax.experimental.pallas import tpu as pltpu
+from jax.sharding import Mesh
 from jax.sharding import PartitionSpec as P
 
 HD = 64
@@ -8,6 +14,11 @@
 
 EPSILON = 1e-05
 MASKED_SCORE = -1e30
+BF = jnp.bfloat16
+F32 = jnp.float32
+NN = (((1,), (0,)), ((), ()))
+NT = (((1,), (1,)), ((), ()))
+VMEM_BYTES = 60 << 20
 
 
 def layer_norm(values, gain):
@@ -96,7 +107,7 @@
     return (grad_query, grad_keys, grad_values)
 
 
-def body(
+def general_body(
     block_in,
     cond_tokens,
     cond_count,
@@ -343,9 +354,9 @@
     )
 
 
-def solution(mesh):
+def general_solution(mesh):
     return jax.shard_map(
-        body,
+        general_body,
         mesh=mesh,
         in_specs=(
             P(("dp", "tensor"), None),
@@ -380,3 +391,1433 @@
         ),
         check_vma=False,
     )
+
+
+def dot(left, right, dims=NN):
+    return lax.dot_general(left, right, dims, preferred_element_type=F32)
+
+
+def iota(shape, axis):
+    return lax.broadcasted_iota(jnp.int32, shape, axis)
+
+
+def whole(shape):
+    return pl.BlockSpec(shape, lambda *p: (0,) * len(shape), pipeline_mode=pl.Buffered(1))
+
+
+def columns_of(rows, first=0):
+    return pl.BlockSpec((rows, 128), lambda p, s: (0, first + p))
+
+
+SCALAR = pl.BlockSpec(memory_space=pltpu.SMEM)
+
+
+def shaped(shape, dtype):
+    return jax.ShapeDtypeStruct(shape, dtype)
+
+
+def call(kernel, grid, ins, outs, name, micros, scratch=(), after=(), scalars=None):
+    lead = 0 if scalars is None else 1
+
+    def without_after(*refs):
+        kernel(*refs[: lead + len(ins)], *refs[lead + len(ins) + len(after) :])
+
+    in_specs = [spec for spec, _ in ins] + [pl.BlockSpec(memory_space=pl.ANY)] * len(after)
+    out_specs = [spec for spec, _ in outs]
+    if lead:
+        how = dict(
+            grid_spec=pltpu.PrefetchScalarGridSpec(
+                num_scalar_prefetch=1, grid=grid, in_specs=in_specs, out_specs=out_specs,
+                scratch_shapes=list(scratch),
+            )
+        )
+    else:
+        how = dict(
+            grid=grid, in_specs=in_specs, out_specs=out_specs, scratch_shapes=list(scratch)
+        )
+    return pl.pallas_call(
+        without_after,
+        **how,
+        out_shape=[shape for _, shape in outs],
+        compiler_params=pltpu.CompilerParams(vmem_limit_bytes=VMEM_BYTES),
+        cost_estimate=pl.CostEstimate(
+            flops=int(micros * FLOPS), bytes_accessed=0, transcendentals=0
+        ),
+        name=name,
+    )(*([] if scalars is None else [scalars]), *[array for _, array in ins], *after)
+
+
+def unravel(shard):
+    size = 4 * shard
+    source, target = iota((size, size), 0), iota((size, size), 1)
+    z, core, at = source // (2 * shard), (source // shard) % 2, source % shard
+    return jnp.where(core * 2 * shard + z * shard + at == target, 1.0, 0.0).astype(BF)
+
+
+def put_in_order(values, turn, odd):
+    size = turn.shape[0]
+    own, other = [], []
+    for at in range(0, values.shape[1], size):
+        both = dot(values[:, at : at + size], turn)
+        even, odds = both[:, : size // 2], both[:, size // 2 :]
+        own.append(jnp.where(odd, odds, even))
+        other.append(jnp.where(odd, even, odds))
+    return jnp.concatenate(own + other, axis=1)
+
+
+def put_back(values, turn, odd, parts):
+    size = turn.shape[0]
+    middle = values.shape[1] // 2
+    result = []
+    for at in range(0, middle, size // 2):
+        own = values[:, at : at + size // 2]
+        other = values[:, middle + at : middle + at + size // 2]
+        both = jnp.concatenate(
+            [jnp.where(odd, other, own), jnp.where(odd, own, other)], axis=1
+        )
+        total = None
+        for _ in range(parts):
+            term = both.astype(BF)
+            moved = dot(term, turn, NT)
+            total = moved if total is None else total + moved
+            both = both - term.astype(F32)
+        result.append(total)
+    return jnp.concatenate(result, axis=1)
+
+
+def hold(array, after):
+    anywhere = pl.BlockSpec(memory_space=pl.ANY)
+    return pl.pallas_call(
+        lambda *refs: None,
+        in_specs=[anywhere] * (1 + len(after)),
+        out_specs=anywhere,
+        out_shape=shaped(array.shape, array.dtype),
+        input_output_aliases={0: 0},
+        cost_estimate=pl.CostEstimate(flops=0, bytes_accessed=0, transcendentals=0),
+        name="hold",
+    )(array, *after)
+
+
+def normalize(values):
+    centre = values - jnp.mean(values, axis=-1, keepdims=True)
+    scale = lax.rsqrt(jnp.mean(centre * centre, axis=-1, keepdims=True) + EPSILON)
+    return centre * scale, scale
+
+
+def normalize_back(grads, gain, normal, scale):
+    inner = grads * gain
+    return (
+        inner
+        - jnp.mean(inner, axis=-1, keepdims=True)
+        - normal * jnp.mean(inner * normal, axis=-1, keepdims=True)
+    ) * scale
+
+
+def first_norm(mine_ref, theirs_ref, gains_ref, out_ref, across_ref):
+    rows = mine_ref.shape[0]
+    step = 256
+    for ref, base in ((mine_ref, 0), (theirs_ref, rows)):
+        for at in range(0, rows, step):
+            normal, _ = normalize(ref[at : at + step, :].astype(F32))
+            out = (normal * gains_ref[0:1, :]).astype(BF)
+            out_ref[base + at : base + at + step, :] = out
+            across_ref[:, base + at : base + at + step] = jnp.transpose(out)
+
+
+QKV_CHAINS = (("z2", "z1", "y", "c"), ("z2", "y", "z1", "c"))
+SQUARE_CHAINS = (
+    ("z2", "z1", "y", "x", "c"),
+    ("z2", "z1", "x", "y", "c"),
+    ("z2", "x", "y", "z1", "c"),
+    ("z2", "z1", "y", "x", "c"),
+)
+AXES = ("z2", "z1", "c", "y", "x")
+STEPS = (
+    "Q0.0", "Q1.0", "S0.0", "Q1.1", "S1.0", "in", "S2.0", "S3.0", "Q0.1", "S0.1", "top",
+    "Q0.2", "Q1.2", "S2.1", "S1.1", "S0.2", "S3.1", "Q0.3", "Q1.3", "S1.2", "S2.2", "S3.2",
+    "S0.3", "S2.3", "S1.3", "S0.4", "S2.4", "S3.3", "S1.4", "S3.4",
+)
+
+
+def gather_kernel(
+    qkv_ref, square_ref, gains_ref, rows_ref, tops_ref, gu_ref, down_ref,
+    wq_ref, w0_ref, w1_ref, w2_ref, w3_ref,
+    mine_ref, theirs_ref, tops_out, their_tops_ref, gains_out, first_ref, across_ref, turn_ref,
+    *rest,
+):
+    *pack_refs, sum_ref, slot_ref, sends, receives, local_sems = rest
+    dp, seq, side = (lax.axis_index(name) for name in ("dp", "seq", "half"))
+    here = {"z2": dp // 4, "z1": (dp // 2) % 2, "c": dp % 2, "y": seq, "x": side}
+    partners = {
+        "z2": (dp + 4 - 8 * (dp // 4), seq, side),
+        "z1": (dp + 2 - 4 * ((dp // 2) % 2), seq, side),
+        "c": (dp + 1 - 2 * (dp % 2), seq, side),
+        "y": (dp, 1 - seq, side),
+        "x": (dp, seq, 1 - side),
+    }
+    barrier = pltpu.get_barrier_semaphore()
+    for axis in AXES:
+        pl.semaphore_signal(
+            barrier, inc=1, device_id=partners[axis], device_id_type=pl.DeviceIdType.MESH
+        )
+    pl.semaphore_wait(barrier, len(AXES))
+    count = [0]
+
+    def send(source, target, axis):
+        copy = pltpu.make_async_remote_copy(
+            source, target, sends.at[count[0]], receives.at[count[0]],
+            device_id=partners[axis], device_id_type=pl.DeviceIdType.MESH,
+        )
+        count[0] += 1
+        copy.start()
+        return copy
+
+    chains = {}
+    columns = qkv_ref.shape[1]
+    cut = columns // 2 // 128 * 128 + 128
+    for at, (order, low, high) in enumerate(
+        ((QKV_CHAINS[0], 0, cut), (QKV_CHAINS[1], cut, columns))
+    ):
+        chains["Q%d" % at] = (wq_ref, qkv_ref, low, high, order, AXES[:4])
+    wide = square_ref.shape[1] // 4
+    for at, (order, ref) in enumerate(zip(SQUARE_CHAINS, (w0_ref, w1_ref, w2_ref, w3_ref))):
+        chains["S%d" % at] = (ref, square_ref, at * wide, (at + 1) * wide, order, AXES)
+
+    own_copies = {}
+
+    def region(name, step):
+        ref, _, low, high, order, axes = chains[name]
+        grown = order[:step]
+        index = tuple(slice(None) if axis in grown else here[axis] for axis in axes)
+        if name[0] == "Q":
+            index += (slice(None), slice(low, high))
+        return ref.at[index]
+
+    def begin(name, step):
+        _, source, low, high, order, _ = chains[name]
+        if step == 0:
+            part = source.at[:, slice(low, high)]
+            copy = pltpu.make_async_copy(part, region(name, 0), local_sems.at[len(own_copies)])
+            copy.start()
+            own_copies[name] = copy
+            return send(part, region(name, 0), order[0])
+        if step == 1:
+            own_copies[name].wait()
+        return send(region(name, step), region(name, step), order[step])
+
+    flying = {}
+    for name in chains:
+        flying[name] = begin(name, 0)
+    odd = here["c"] == 1
+    turn_ref[...] = unravel(qkv_ref.shape[0])
+    turn = turn_ref[...]
+    mine_ref[...] = put_in_order(rows_ref[...], turn, odd).astype(BF)
+    swaps = {"in": send(mine_ref, theirs_ref, "x")}
+    tops_out[...] = put_in_order(tops_ref[...], turn, odd).astype(BF)
+    sum_ref[...] = gains_ref[...]
+    for at, axis in enumerate(("c", "z1", "z2")):
+        copy = send(sum_ref, slot_ref.at[at], axis)
+        copy.wait()
+        sum_ref[...] += slot_ref[at]
+    gains_out[...] = put_in_order(sum_ref[...].astype(BF), turn, odd)
+    hidden = down_ref.shape[0]
+    tiles = hidden // len(pack_refs) // TILE
+    for i, pack_ref in enumerate(pack_refs):
+        for j in range(tiles):
+            at, low = 3 * j * TILE, (i * tiles + j) * TILE
+            pack_ref[:, at : at + TILE] = gu_ref[:, low : low + TILE]
+            pack_ref[:, at + TILE : at + 2 * TILE] = gu_ref[:, hidden + low : hidden + low + TILE]
+            pack_ref[:, at + 2 * TILE : at + 3 * TILE] = jnp.transpose(
+                down_ref[low : low + TILE, :]
+            )
+
+    for event in STEPS:
+        if event in ("in", "top"):
+            swaps[event].wait()
+            if event == "in":
+                swaps["top"] = send(tops_out, their_tops_ref, "x")
+                first_norm(mine_ref, theirs_ref, gains_out, first_ref, across_ref)
+            continue
+        name, step = event.split(".")
+        flying[name].wait()
+        if int(step) + 1 < len(chains[name][4]):
+            flying[name] = begin(name, int(step) + 1)
+
+
+def gather_first(qkv, square, gains, rows, tops, gate_up, down):
+    anywhere, vmem = pl.BlockSpec(memory_space=pl.ANY), pl.BlockSpec(memory_space=pltpu.VMEM)
+    shard = qkv.shape[0]
+    wide = square.shape[1] // 4
+    count, width = rows.shape
+    copies = 4 * 2 + 5 * 4 + 2 + 3
+    return pl.pallas_call(
+        gather_kernel,
+        in_specs=[anywhere, anywhere] + [vmem] * 5,
+        out_specs=[anywhere] * 5 + [vmem] * (8 + CHUNKS),
+        out_shape=[shaped((2, 2, 2, 2) + qkv.shape, BF)]
+        + [shaped((2, 2, 2, 2, 2, shard, wide), BF)] * 4
+        + [shaped(rows.shape, BF)] * 4
+        + [shaped(gains.shape, F32), shaped((2 * count, width), BF), shaped((width, 2 * count), BF)]
+        + [shaped((4 * shard, 4 * shard), BF)]
+        + [shaped((shard, 3 * down.shape[0] // CHUNKS), BF)] * CHUNKS,
+        scratch_shapes=[
+            pltpu.VMEM(gains.shape, F32),
+            pltpu.VMEM((3,) + gains.shape, F32),
+            pltpu.SemaphoreType.DMA((copies,)),
+            pltpu.SemaphoreType.DMA((copies,)),
+            pltpu.SemaphoreType.DMA((6,)),
+        ],
+        compiler_params=pltpu.CompilerParams(
+            vmem_limit_bytes=VMEM_BYTES, collective_id=0, has_side_effects=True
+        ),
+        name="gather_first",
+    )(qkv, square, gains, rows, tops, gate_up, down)
+
+
+def across_kernel(*refs):
+    count = len(refs) // 2
+    for source, target in zip(refs[:count], refs[count:]):
+        step = 256
+        for at in range(0, source.shape[0], step):
+            target[:, at : at + step] = jnp.transpose(source[at : at + step, :])
+
+
+def across(*arrays):
+    shape = arrays[0].shape
+    flipped = (shape[1], shape[0])
+    return call(
+        across_kernel, (1,),
+        [(whole(shape), array) for array in arrays],
+        [(whole(flipped), shaped(flipped, BF))] * len(arrays),
+        "across", 3 * len(arrays),
+    )
+
+
+def rot(values, tables):
+    cosine, sine_up, sine_down = tables
+    return (
+        values * cosine
+        + pltpu.roll(values, 16, 1) * sine_up
+        + pltpu.roll(values, 112, 1) * sine_down
+    )
+
+
+def rot_back(grads, tables):
+    cosine, sine_up, sine_down = tables
+    return (
+        grads * cosine
+        - pltpu.roll(grads, 16, 1) * sine_up
+        - pltpu.roll(grads, 112, 1) * sine_down
+    )
+
+
+def rot_tables(positions):
+    quarter = HD // 4
+    inverse = 10000.0 ** (-jnp.arange(quarter).astype(F32) / quarter)
+    angle_grid = positions.astype(F32)[:, None] * inverse[None, :]
+    cosine, sine = jnp.cos(angle_grid), jnp.sin(angle_grid)
+    rest = jnp.zeros((positions.shape[0], 2 * quarter), F32)
+    none = jnp.zeros_like(sine)
+    return (
+        jnp.concatenate([cosine, cosine, rest + 1.0] * 2, axis=1),
+        jnp.concatenate([none, sine, rest] * 2, axis=1),
+        jnp.concatenate([-sine, none, rest] * 2, axis=1),
+    )
+
+
+def to_rows(picks, columns):
+    first = columns.astype(BF)
+    rest = columns - first.astype(F32)
+    second = rest.astype(BF)
+    third = (rest - second.astype(F32)).astype(BF)
+    return dot(picks, first, NT) + dot(picks, second, NT) + dot(picks, third, NT)
+
+
+def self_forward_kernel(
+    step, place_ref, rows_ref, own_ref, other_ref, c_ref, su_ref, sd_ref,
+    q_ref, k_ref, v_ref, mine_ref, theirs_ref, lse_ref,
+):
+    count, width = rows_ref.shape
+    half = width // 2
+    own, other = own_ref[...].reshape(half, 384), other_ref[...].reshape(half, 384)
+    qkv = dot(rows_ref[:, :half], own) + dot(rows_ref[:, half:], other)
+    tables = (c_ref[...], su_ref[...], sd_ref[...])
+    query = (rot(qkv[:, :128], tables) * 0.125).astype(BF)
+    key = rot(qkv[:, 128:256], tables).astype(BF)
+    value = qkv[:, 256:].astype(BF)
+    q_ref[...] = query
+    k_ref[...] = key
+    v_ref[...] = value
+    lane = iota((step, 128), 1)
+    picks = jnp.where(iota((8, 128), 0) == iota((8, 128), 1), 1.0, 0.0).astype(BF)
+    for at in range(0, count, step):
+        part = query[at : at + step]
+        mixed, logs = [], []
+        for head in range(2):
+            here = (lane // HD) == head
+            scores = dot(jnp.where(here, part, jnp.zeros_like(part)), key, NT)
+            top = jnp.max(scores, axis=1, keepdims=True)
+            weights = jnp.exp(scores - top)
+            total = jnp.sum(weights, axis=1, keepdims=True)
+            mixed.append(dot(weights.astype(BF), value) * (1.0 / total))
+            logs.append(top + jnp.log(total))
+        out = jnp.where(lane < HD, mixed[0], mixed[1]).astype(BF)
+        both = jnp.where(lane == 0, logs[0], jnp.where(lane == 1, logs[1], 0.0))
+        lse_ref[0, :, at : at + step] = to_rows(picks, both)
+        if at < count // 2:
+            mine_ref[at : at + step, :] = out
+        else:
+            theirs_ref[at - count // 2 : at - count // 2 + step, :] = out
+
+
+def self_weights(weights, first=0):
+    shape = (weights.shape[0], 1, 1, weights.shape[3], 384)
+    return [
+        (pl.BlockSpec(shape, lambda p, s: (0, s[0], p % 2, 0, first // 2 + p // 2)), weights),
+        (pl.BlockSpec(shape, lambda p, s: (0, 1 - s[0], p % 2, 0, first // 2 + p // 2)), weights),
+    ]
+
+
+def self_forward(place, rows, weights, tables, after=()):
+    count, width = rows.shape
+    wide = weights.shape[2] * weights.shape[4] // 3
+    pairs = wide // 128
+    return call(
+        functools.partial(self_forward_kernel, 512),
+        (pairs,),
+        [(whole(rows.shape), rows)] + self_weights(weights)
+        + [(whole((count, 128)), table) for table in tables],
+        [(columns_of(count), shaped((count, wide), BF))] * 3
+        + [(columns_of(count // 2), shaped((count // 2, wide), BF))] * 2
+        + [(pl.BlockSpec((1, 8, count), lambda p, s: (p, 0, 0)), shaped((pairs, 8, count), F32))],
+        "self_forward", 7 * pairs,
+        after=after,
+        scalars=place,
+    )
+
+
+def self_backward_kernel(
+    step, begins, ends, place_ref, q_ref, k_ref, v_ref, mine_ref, theirs_ref, dmine_ref, dtheirs_ref, lse_ref,
+    c_ref, su_ref, sd_ref, across_ref, own_ref, other_ref, *rest,
+):
+    if begins:
+        gown_ref, gother_ref, *outs, qkv_ref, sum_ref = rest
+    else:
+        start_ref, gown_ref, gother_ref, *outs, qkv_ref, sum_ref = rest
+    count = q_ref.shape[0]
+    query = q_ref[...]
+    grads = jnp.concatenate([dmine_ref[...], dtheirs_ref[...]], axis=0)
+    mixed = jnp.concatenate([mine_ref[...], theirs_ref[...]], axis=0)
+    picks = jnp.where((iota((8, 128), 1) // HD) == iota((8, 128), 0), 1.0, 0.0).astype(BF)
+    delta = to_rows(picks, grads.astype(F32) * mixed.astype(F32))
+    lane = iota((step, 128), 1)
+    row = iota((128, step), 0)
+    keys_across = jnp.transpose(k_ref[...].astype(F32)).astype(BF)
+    query_across = jnp.zeros((128, count), F32)
+    tables = (c_ref[...], su_ref[...], sd_ref[...])
+    for at in range(0, count, step):
+        here = slice(at, at + step)
+        key, value = k_ref[here, :], v_ref[here, :]
+        flipped = keys_across[:, here]
+        dkeys, dvalues = [], []
+        for head in range(2):
+            inside = (lane // HD) == head
+            scores = dot(jnp.where(inside, key, jnp.zeros_like(key)), query, NT)
+            probs = jnp.exp(scores - lse_ref[0, head : head + 1, :])
+            dprobs = dot(jnp.where(inside, value, jnp.zeros_like(value)), grads, NT)
+            dscores = (probs * (dprobs - delta[head : head + 1, :])).astype(BF)
+            dvalues.append(dot(probs.astype(BF), grads))
+            dkeys.append(dot(dscores, query))
+            picked = jnp.where((row // HD) == head, flipped, jnp.zeros_like(flipped))
+            query_across = query_across + dot(picked, dscores)
+        dkey = jnp.where(lane < HD, dkeys[0], dkeys[1])
+        dvalue = jnp.where(lane < HD, dvalues[0], dvalues[1])
+        qkv_ref[here, 128:256] = rot_back(dkey, [t[here] for t in tables]).astype(BF)
+        qkv_ref[here, 256:384] = dvalue.astype(BF)
+    dquery = jnp.transpose(query_across)
+    qkv_ref[:, 0:128] = (rot_back(dquery, tables) * 0.125).astype(BF)
+
+    first = pl.program_id(0) == 0
+    last = pl.program_id(0) == pl.num_programs(0) - 1
+    half = across_ref.shape[0] // 2
+    own, other = own_ref[...].reshape(half, 384), other_ref[...].reshape(half, 384)
+    both = qkv_ref[...]
+    gown_ref[0] = dot(across_ref[:half, :], both).astype(BF)
+    gother_ref[0] = dot(across_ref[half:, :], both).astype(BF)
+    back = jnp.concatenate([dot(both, own, NT), dot(both, other, NT)], axis=1)
+
+    @pl.when(first)
+    def _():
+        sum_ref[...] = back if begins else start_ref[...] + back
+
+    @pl.when(jnp.logical_not(first))
+    def _():
+        sum_ref[...] += back
+
+    @pl.when(last)
+    def _():
+        if ends:
+            outs[0][...] = sum_ref[: count // 2, :].astype(BF)
+            outs[1][...] = sum_ref[count // 2 :, :].astype(BF)
+        else:
+            outs[0][...] = sum_ref[...]
+
+
+def self_backward(
+    place, query, key, value, mine, theirs, dmine, dtheirs, lse, tables, flipped, weights, first, pairs,
+    start, ends, after=(),
+):
+    count = query.shape[0]
+    wide = 128 * pairs
+    width = flipped.shape[0]
+    out = pl.BlockSpec((1, width // 2, 384), lambda p, s: (p % 2, 0, p // 2))
+    out_shape = (2, width // 2, 192 * pairs)
+    rows, half = columns_of(count, first), columns_of(count // 2, first)
+    half_rows = (count // 2, width)
+    all_rows = (count, width)
+    if ends:
+        sums = [(whole(half_rows), shaped(half_rows, BF))] * 2
+    else:
+        sums = [(whole(all_rows), shaped(all_rows, F32))]
+    starts = [] if start is None else [(whole(all_rows), start)]
+    return call(
+        functools.partial(self_backward_kernel, 512, start is None, ends),
+        (pairs,),
+        [(rows, array) for array in (query, key, value)]
+        + [(half, array) for array in (mine, theirs, dmine, dtheirs)]
+        + [(pl.BlockSpec((1, 8, count), lambda p, s: (first + p, 0, 0)), lse)]
+        + [(whole((count, 128)), table) for table in tables]
+        + [(whole(flipped.shape), flipped)] + self_weights(weights, first) + starts,
+        [(out, shaped(out_shape, BF))] * 2 + sums,
+        "self_backward", 13 * pairs,
+        scratch=[pltpu.VMEM((count, 384), BF), pltpu.VMEM((count, width), F32)],
+        after=after,
+        scalars=place,
+    )
+
+
+def ffn_kernel(
+    tile, carried, place_ref, mine_ref, theirs_ref, fmine_ref, ftheirs_ref,
+    tmine_ref, ttheirs_ref, gmine_ref, gtheirs_ref, own_ref, other_ref, *rest,
+):
+    starts, rest = rest[: 4 * carried], rest[4 * carried :]
+    ymine_ref, ytheirs_ref, dmine_ref, dtheirs_ref, gown_ref, gother_ref, y_ref, d_ref = rest
+    rows, width = mine_ref.shape
+    half = width // 2
+    both = 2 * tile
+    first = pl.program_id(0) == 0
+    last = pl.program_id(0) == pl.num_programs(0) - 1
+
+    @pl.when(first)
+    def _():
+        if carried:
+            for part in range(2):
+                y_ref[part] = starts[part][...].astype(F32)
+                d_ref[part] = starts[2 + part][...].astype(F32)
+        else:
+            y_ref[...] = jnp.zeros_like(y_ref)
+            d_ref[...] = jnp.zeros_like(d_ref)
+
+    own = own_ref[...].reshape(half, 3 * tile)
+    other = other_ref[...].reshape(half, 3 * tile)
+    hidden_parts, dgate_up_parts = [], []
+    for part, (ref, top_ref) in enumerate(((mine_ref, tmine_ref), (theirs_ref, ttheirs_ref))):
+        gate_up = dot(ref[:, :half], own[:, :both]) + dot(ref[:, half:], other[:, :both])
+        dhidden = dot(top_ref[:, :half], own[:, both:]) + dot(top_ref[:, half:], other[:, both:])
+        gate, up = gate_up[:, :tile], gate_up[:, tile:]
+        sigma = 1.0 / (1.0 + jnp.exp(-gate))
+        silu = gate * sigma
+        hidden = (silu * up).astype(BF)
+        dup = (dhidden * silu).astype(BF)
+        dgate = (dhidden * up * (sigma * (1.0 + gate * (1.0 - sigma)))).astype(BF)
+        dgate_up = jnp.concatenate([dgate, dup], axis=1)
+        y_ref[part, :, :half] += dot(hidden, own[:, both:], NT)
+        y_ref[part, :, half:] += dot(hidden, other[:, both:], NT)
+        d_ref[part, :, :half] += dot(dgate_up, own[:, :both], NT)
+        d_ref[part, :, half:] += dot(dgate_up, other[:, :both], NT)
+        hidden_parts.append(hidden)
+        dgate_up_parts.append(dgate_up)
+    for out, cut in ((gown_ref, slice(0, half)), (gother_ref, slice(half, width))):
+        out[0, :, :both] = (
+            dot(fmine_ref[cut, :], dgate_up_parts[0]) + dot(ftheirs_ref[cut, :], dgate_up_parts[1])
+        ).astype(BF)
+        out[0, :, both:] = (
+            dot(gmine_ref[cut, :], hidden_parts[0]) + dot(gtheirs_ref[cut, :], hidden_parts[1])
+        ).astype(BF)
+
+    @pl.when(last)
+    def _():
+        ymine_ref[...] = y_ref[0].astype(BF)
+        ytheirs_ref[...] = y_ref[1].astype(BF)
+        dmine_ref[...] = d_ref[0].astype(BF)
+        dtheirs_ref[...] = d_ref[1].astype(BF)
+
+
+def ffn(place, rows, flipped, tops, tops_flipped, weights, tile, starts=(), after=()):
+    count, width = rows[0].shape
+    zs, _, groups, shard, wide = weights.shape
+    half = zs * shard
+    tiles = wide // (3 * tile)
+    own_block = pl.BlockSpec(
+        (zs, 1, 1, shard, 3 * tile), lambda p, s: (0, s[0], p // tiles, 0, p % tiles)
+    )
+    other_block = pl.BlockSpec(
+        (zs, 1, 1, shard, 3 * tile), lambda p, s: (0, 1 - s[0], p // tiles, 0, p % tiles)
+    )
+    block = pl.BlockSpec((1, half, 3 * tile), lambda p, s: (p // tiles, 0, p % tiles))
+    out = shaped((groups, half, wide), BF)
+    once, fixed = whole((count, width)), whole((width, count))
+    return call(
+        functools.partial(ffn_kernel, tile, len(starts) // 4),
+        (groups * tiles,),
+        [(once, a) for a in rows] + [(fixed, a) for a in flipped]
+        + [(once, a) for a in tops] + [(fixed, a) for a in tops_flipped]
+        + [(own_block, weights), (other_block, weights)] + [(once, a) for a in starts],
+        [(once, shaped((count, width), BF))] * 4 + [(block, out)] * 2,
+        "feed_forward", 9 * groups * tiles,
+        scratch=[pltpu.VMEM((2, count, width), F32)] * 2,
+        after=after,
+        scalars=place,
+    )
+
+
+def section(square, other):
+    zs, _, ys, xs, shard, wide = square.shape
+    return (
+        pl.BlockSpec(
+            (zs, 1, ys, xs, shard, wide),
+            lambda *a: (0, 1 - a[-1][0] if other else a[-1][0], 0, 0, 0, 0),
+            pipeline_mode=pl.Buffered(1),
+        ),
+        square,
+    )
+
+
+def sections(squares):
+    return [section(squares[n], other) for n in (0, 1, 3) for other in (False, True)]
+
+
+def weight_of(ref, x, y):
+    zs, _, _, _, shard, wide = ref.shape
+    return ref[:, 0, y, x].reshape(zs * shard, wide)
+
+
+def cond_kernel(place_ref, cond_ref, own_ref, other_ref, key_ref, value_ref):
+    shard = cond_ref.shape[1] // 8
+    half = 4 * shard
+    wide = own_ref.shape[-1]
+    for x in range(2):
+        for y in range(2):
+            at = (2 * x + y) * wide
+            for kind, out in ((0, key_ref), (1, value_ref)):
+                total = None
+                for part, ref in ((0, own_ref), (1, other_ref)):
+                    weight = ref[:, 0, y, x, kind * shard : (kind + 1) * shard, :]
+                    weight = weight.reshape(half, wide)
+                    term = dot(cond_ref[:, part * half : (part + 1) * half], weight)
+                    total = term if total is None else total + term
+                out[:, at : at + wide] = total.astype(BF)
+
+
+def cond_forward(place, cond, square):
+    slots, width = cond.shape
+    wide = 4 * square.shape[-1]
+    return call(
+        cond_kernel, (1,),
+        [(whole(cond.shape), cond), section(square, False), section(square, True)],
+        [(whole((slots, wide)), shaped((slots, wide), BF))] * 2,
+        "cond_forward", 6,
+        scalars=place,
+    )
+
+
+def beside(ref, y):
+    return jnp.concatenate(
+        [ref[:, at : at + 128] for at in range(y * 128, ref.shape[1], 256)], axis=1
+    )
+
+
+def middle_forward_kernel(
+    place_ref, rows_ref, mine_ref, theirs_ref, gains_ref, key_ref, value_ref,
+    out_own, out_other, cq_own, cq_other, co_own, co_other,
+    x1_ref, second_ref, query_ref, mixed_ref, x2_ref, third_ref,
+):
+    rows, width = rows_ref.shape
+    half = width // 2
+    wide = out_own.shape[-1]
+    slots = key_ref.shape[0]
+    valid = iota((rows, slots), 1) < place_ref[3]
+    lane = iota((rows, 128), 1)
+    for out, cut in ((out_own, 0), (out_other, half)):
+        total = rows_ref[:, cut : cut + half].astype(F32)
+        for x in range(2):
+            for y in range(2):
+                mixed = jnp.where(
+                    place_ref[2] == x, beside(mine_ref, y), beside(theirs_ref, y)
+                )
+                total += dot(mixed, weight_of(out, x, y), NT)
+        x1_ref[:, cut : cut + half] = total
+    normal, _ = normalize(x1_ref[...])
+    second = (normal * gains_ref[1:2, :]).astype(BF)
+    second_ref[...] = second
+    for x in range(2):
+        for y in range(2):
+            at = (2 * x + y) * wide
+            query = dot(second[:, :half], weight_of(cq_own, x, y)) + dot(
+                second[:, half:], weight_of(cq_other, x, y)
+            )
+            query_ref[:, at : at + wide] = (query * 0.125).astype(BF)
+    for at in range(0, 4 * wide, 128):
+        query, key, value = (
+            ref[:, at : at + 128] for ref in (query_ref, key_ref, value_ref)
+        )
+        mixed = []
+        for head in range(2):
+            part = jnp.where((lane // HD) == head, query, jnp.zeros_like(query))
+            scores = jnp.where(valid, dot(part, key, NT), MASKED_SCORE)
+            top = jnp.max(scores, axis=1, keepdims=True)
+            weights = jnp.exp(scores - top)
+            total = jnp.sum(weights, axis=1, keepdims=True)
+            mixed.append(dot(weights.astype(BF), value) * (1.0 / total))
+        mixed_ref[:, at : at + 128] = jnp.where(lane < HD, mixed[0], mixed[1]).astype(BF)
+    for out, cut in ((co_own, 0), (co_other, half)):
+        total = x1_ref[:, cut : cut + half]
+        for x in range(2):
+            for y in range(2):
+                at = (2 * x + y) * wide
+                total += dot(mixed_ref[:, at : at + wide], weight_of(out, x, y), NT)
+        x2_ref[:, cut : cut + half] = total
+    normal, _ = normalize(x2_ref[...])
+    third_ref[...] = (normal * gains_ref[2:3, :]).astype(BF)
+
+
+def middle_forward(place, rows, mine, theirs, gains, key, value, squares, after=()):
+    full = whole(rows.shape)
+    part = whole(mine.shape)
+    cond = whole(key.shape)
+    return call(
+        middle_forward_kernel, (1,),
+        [(full, rows), (part, mine), (part, theirs)]
+        + [(whole(gains.shape), gains), (cond, key), (cond, value)] + sections(squares),
+        [(full, shaped(rows.shape, dtype)) for dtype in (F32, BF, BF, BF, F32, BF)],
+        "middle_forward", 26,
+        after=after, scalars=place,
+    )
+
+
+def middle_backward_kernel(
+    place_ref, d_ref, r_ref, top_ref, x2_ref, x1_ref, gains_ref,
+    query_ref, key_ref, value_ref,
+    out_own, out_other, cq_own, cq_other, co_own, co_other,
+    dx1_ref, e2_ref, dquery_ref, dkey_ref, dvalue_ref, e1_ref, *refs,
+):
+    dmine_ref, dtheirs_ref, dmixed_ref = refs
+    rows, width = x1_ref.shape
+    half = width // 2
+    wide = out_own.shape[-1]
+    slots = key_ref.shape[0]
+    grad_third = d_ref[...].astype(F32) + r_ref[...].astype(F32)
+    normal, scale = normalize(x2_ref[...])
+    dx2 = top_ref[...].astype(F32) + normalize_back(grad_third, gains_ref[2:3, :], normal, scale)
+    dx1_ref[...] = dx2
+    e2 = dx2.astype(BF)
+    e2_ref[...] = e2
+    for x in range(2):
+        for y in range(2):
+            at = (2 * x + y) * wide
+            dmixed_ref[:, at : at + wide] = (
+                dot(e2[:, :half], weight_of(co_own, x, y))
+                + dot(e2[:, half:], weight_of(co_other, x, y))
+            ).astype(BF)
+    valid = iota((slots, rows), 0) < place_ref[3]
+    lane = iota((slots, 128), 1)
+    row = iota((128, slots), 0)
+    for at in range(0, 4 * wide, 128):
+        here = slice(at, at + 128)
+        query, key, value, grads = (
+            ref[:, here] for ref in (query_ref, key_ref, value_ref, dmixed_ref)
+        )
+        flipped = jnp.transpose(key.astype(F32)).astype(BF)
+        dkeys, dvalues = [], []
+        query_across = None
+        for head in range(2):
+            inside = (lane // HD) == head
+            scores = dot(jnp.where(inside, key, jnp.zeros_like(key)), query, NT)
+            scores = jnp.where(valid, scores, MASKED_SCORE)
+            weights = jnp.exp(scores - jnp.max(scores, axis=0, keepdims=True))
+            probs = weights * (1.0 / jnp.sum(weights, axis=0, keepdims=True))
+            dprobs = dot(jnp.where(inside, value, jnp.zeros_like(value)), grads, NT)
+            shared = jnp.sum(probs * dprobs, axis=0, keepdims=True)
+            dscores = (probs * (dprobs - shared)).astype(BF)
+            dvalues.append(dot(probs.astype(BF), grads))
+            dkeys.append(dot(dscores, query))
+            term = dot(jnp.where((row // HD) == head, flipped, jnp.zeros_like(flipped)), dscores)
+            query_across = term if query_across is None else query_across + term
+        dkey_ref[:, here] = jnp.where(lane < HD, dkeys[0], dkeys[1]).astype(BF)
+        dvalue_ref[:, here] = jnp.where(lane < HD, dvalues[0], dvalues[1]).astype(BF)
+        dquery_ref[:, here] = (jnp.transpose(query_across) * 0.125).astype(BF)
+    parts = []
+    for weight in (cq_own, cq_other):
+        total = None
+        for x in range(2):
+            for y in range(2):
+                at = (2 * x + y) * wide
+                term = dot(dquery_ref[:, at : at + wide], weight_of(weight, x, y), NT)
+                total = term if total is None else total + term
+        parts.append(total)
+    grad_second = jnp.concatenate(parts, axis=1)
+    normal, scale = normalize(x1_ref[...])
+    dx1 = dx1_ref[...] + normalize_back(grad_second, gains_ref[1:2, :], normal, scale)
+    dx1_ref[...] = dx1
+    e1 = dx1.astype(BF)
+    e1_ref[...] = e1
+    for y in range(2):
+        first, second = (
+            dot(e1[:, :half], weight_of(out_own, x, y))
+            + dot(e1[:, half:], weight_of(out_other, x, y))
+            for x in range(2)
+        )
+        low = place_ref[2] == 0
+        for out, grads in (
+            (dtheirs_ref, jnp.where(low, second, first).astype(BF)),
+            (dmine_ref, jnp.where(low, first, second).astype(BF)),
+        ):
+            for j in range(wide // 128):
+                at = (2 * j + y) * 128
+                out[:, at : at + 128] = grads[:, j * 128 : (j + 1) * 128]
+
+
+def middle_backward(
+    place, d, r, top, x2, x1, gains, query, key, value, squares, after=()
+):
+    full = whole(x1.shape)
+    rows, width = x1.shape
+    part = (rows, width // 2)
+    cond = whole(key.shape)
+    return call(
+        middle_backward_kernel, (1,),
+        [(full, array) for array in (d, r, top, x2, x1)]
+        + [(whole(gains.shape), gains), (full, query), (cond, key), (cond, value)]
+        + sections(squares),
+        [(full, shaped(x1.shape, F32)), (full, shaped(x1.shape, BF)), (full, shaped(x1.shape, BF))]
+        + [(cond, shaped(key.shape, BF))] * 2
+        + [(full, shaped(x1.shape, BF))]
+        + [(whole(part), shaped(part, BF))] * 2,
+        "middle_backward", 40,
+        scratch=[pltpu.VMEM((rows, width), BF)],
+        after=after,
+        scalars=place,
+    )
+
+
+def middle_weights_kernel(
+    pieces, place_ref, e1_ref, second_ref, dquery_ref, cond_ref, dkey_ref, dvalue_ref,
+    e2_ref, mixed_ref, kv_own, kv_other, *rest,
+):
+    mine_refs, theirs_refs = rest[:pieces], rest[pieces : 2 * pieces]
+    aown_ref, aother_ref, bown_ref, bother_ref, dcond_ref = rest[2 * pieces : 2 * pieces + 5]
+    f1_ref, fsecond_ref, f2_ref, fcond_ref = rest[2 * pieces + 5 :]
+    width = e1_ref.shape[1]
+    half = width // 2
+    wide = kv_own.shape[-1]
+    shard = cond_ref.shape[1] // 8
+    first = pl.program_id(0) == 0
+
+    @pl.when(first)
+    def _():
+        for source, target in (
+            (e1_ref, f1_ref), (second_ref, fsecond_ref), (e2_ref, f2_ref), (cond_ref, fcond_ref)
+        ):
+            target[...] = jnp.transpose(source[...])
+        dcond_ref[...] = jnp.zeros_like(dcond_ref)
+
+    from_theirs = pl.program_id(0) // 2 != place_ref[2]
+    mixed = jnp.concatenate(
+        [jnp.where(from_theirs, b[...], a[...]) for a, b in zip(mine_refs, theirs_refs)], axis=1
+    )
+    for part, (first_out, out, kv) in enumerate(
+        ((aown_ref, bown_ref, kv_own), (aother_ref, bother_ref, kv_other))
+    ):
+        cut = slice(part * half, (part + 1) * half)
+        first_out[0, 0, :, 0:wide] = dot(f1_ref[cut, :], mixed).astype(BF)
+        first_out[0, 0, :, wide : 2 * wide] = dot(fsecond_ref[cut, :], dquery_ref[...]).astype(BF)
+        out[0, 0, :, wide : 2 * wide] = dot(f2_ref[cut, :], mixed_ref[...]).astype(BF)
+        weights = []
+        for kind, grads in ((0, dkey_ref), (1, dvalue_ref)):
+            at = part * 4 * shard
+            both = dot(fcond_ref[at : at + 4 * shard, :], grads[...]).astype(BF)
+            for z in range(4):
+                low = (2 * z + kind) * shard
+                out[0, 0, low : low + shard, 0:wide] = both[z * shard : (z + 1) * shard]
+            weight = kv[:, 0, 0, 0, kind * shard : (kind + 1) * shard, :]
+            weights.append(weight.reshape(4 * shard, wide))
+        dcond_ref[:, part * 4 * shard : (part + 1) * 4 * shard] += dot(
+            dkey_ref[...], weights[0], NT
+        ) + dot(dvalue_ref[...], weights[1], NT)
+
+
+def middle_weights(
+    place, e1, mine, theirs, second, dquery, cond, dkey, dvalue, e2, mixed, square, after=()
+):
+    zs, _, _, _, square_shard, wide = square.shape
+    rows, width = e1.shape
+    slots = cond.shape[0]
+    full = whole(e1.shape)
+    block = pl.BlockSpec((rows, wide), lambda p, s: (0, p))
+    pairs = [
+        pl.BlockSpec((rows, 128), lambda p, s, j=j: (0, 2 * j + p % 2))
+        for j in range(mine.shape[1] // 256)
+    ]
+    cond_block = pl.BlockSpec((slots, wide), lambda p, s: (0, p))
+    shape = (zs, 1, 1, 1, square_shard, wide)
+    own = pl.BlockSpec(shape, lambda p, s: (0, s[0], p % 2, p // 2, 0, 0))
+    other = pl.BlockSpec(shape, lambda p, s: (0, 1 - s[0], p % 2, p // 2, 0, 0))
+    out = pl.BlockSpec((1, 1, width // 2, 2 * wide), lambda p, s: (p // 2, p % 2, 0, 0))
+    out_shape = (2, 2, width // 2, 2 * wide)
+    return call(
+        functools.partial(middle_weights_kernel, len(pairs)), (4,),
+        [(full, e1), (full, second), (block, dquery)]
+        + [(whole(cond.shape), cond), (cond_block, dkey), (cond_block, dvalue)]
+        + [(full, e2), (block, mixed), (own, square), (other, square)]
+        + [(pair, a) for a in (mine, theirs) for pair in pairs],
+        [(out, shaped(out_shape, BF))] * 4 + [(whole(cond.shape), shaped(cond.shape, F32))],
+        "middle_weights", 22,
+        scratch=[pltpu.VMEM((width, rows), BF)] * 3 + [pltpu.VMEM((cond.shape[1], slots), BF)],
+        after=after,
+        scalars=place,
+    )
+
+
+def fold_kernel(place_ref, keep_ref, got_keep_ref, send_ref, got_send_ref, keep_out, send_out):
+    send_out[...] = (send_ref[...].astype(F32) + got_send_ref[...].astype(F32)).astype(BF)
+    keep_out[...] = (keep_ref[...].astype(F32) + got_keep_ref[...].astype(F32)).astype(BF)
+
+
+def fold(place, bit, here, got, at):
+    shape = here.shape
+    before, after = math.prod(shape[:at]), math.prod(shape[at + 1 : -2])
+    view = (before, 2, after) + shape[-2:]
+    block = (1, 1, 1) + shape[-2:]
+    keep = pl.BlockSpec(block, lambda a, b, s: (a, s[bit], b, 0, 0))
+    send = pl.BlockSpec(block, lambda a, b, s: (a, 1 - s[bit], b, 0, 0))
+    out = pl.BlockSpec(block, lambda a, b, s: (a, 0, b, 0, 0))
+    out_shape = shaped((before, 1, after) + shape[-2:], BF)
+    here, got = here.reshape(view), got.reshape(view)
+    results = call(
+        fold_kernel, (before, after),
+        [(keep, here), (keep, got), (send, here), (send, got)],
+        [(out, out_shape)] * 2,
+        "fold", here.size * 1.3e-6, scalars=place,
+    )
+    left = shape[:at] + (1,) + shape[at + 1 :]
+    return [array.reshape(left) for array in results]
+
+
+def finish_ffn_kernel(weight_ref, gain_ref, *refs):
+    *sources, gu_ref, down_ref, norm_ref = refs
+    chunks = len(sources) // 2
+    tiles = sources[0].shape[1] // (3 * TILE)
+    hidden = chunks * tiles * TILE
+    total = jnp.zeros((gain_ref.shape[0], 1), F32)
+    for i in range(chunks):
+        keep, got = sources[2 * i], sources[2 * i + 1]
+        for j in range(tiles):
+            at = 3 * j * TILE
+            target = (i * tiles + j) * TILE
+            grads = keep[:, at : at + 3 * TILE].astype(F32) + got[:, at : at + 3 * TILE].astype(F32)
+            for kind in range(2):
+                cut = slice(kind * hidden + target, kind * hidden + target + TILE)
+                part = grads[:, kind * TILE : (kind + 1) * TILE]
+                gu_ref[:, cut] = part
+                total += jnp.sum(part * weight_ref[:, cut].astype(F32), axis=1, keepdims=True)
+            down_ref[target : target + TILE, :] = jnp.transpose(grads[:, 2 * TILE :])
+    norm_ref[...] = total / gain_ref[...]
+
+
+def finish_ffn(weight, gain, sources):
+    shard, wide = weight.shape
+    return call(
+        finish_ffn_kernel, (1,),
+        [(whole(weight.shape), weight), (whole(gain.shape), gain)]
+        + [(whole(a.shape), a) for a in sources],
+        [
+            (whole(weight.shape), shaped(weight.shape, F32)),
+            (whole((wide // 2, shard)), shaped((wide // 2, shard), F32)),
+            (whole(gain.shape), shaped(gain.shape, F32)),
+        ],
+        "finish_ffn", 5,
+    )
+
+
+def scatter_kernel(
+    queries, dx_ref, their_dx_ref, gain_ref, qkv_weight, query_weight, third_ref,
+    x2_ref, y_ref, y_got_ref, turn_ref, rows_ref, gains_ref, dx1_ref, *refs,
+):
+    inputs, refs = refs[: 4 + 2 * queries], refs[4 + 2 * queries :]
+    outs, refs = refs[:8], refs[8:]
+    block_ref, dinput_ref, out_ref, cq_ref, ckv_ref, co_ref, qkv_ref, norm_ref = outs
+    dx_slot, norm_slot, refs = refs[0], refs[1], refs[2:]
+    works, slots, refs = refs[: 2 + queries], refs[2 + queries : 5 * (2 + queries)], refs[5 * (2 + queries) :]
+    sends, receives, local_sems = refs
+    dp, seq, side = (lax.axis_index(name) for name in ("dp", "seq", "half"))
+    here = {"z2": dp // 4, "z1": (dp // 2) % 2, "c": dp % 2, "y": seq, "x": side}
+    partners = {
+        "z2": (dp + 4 - 8 * (dp // 4), seq, side),
+        "z1": (dp + 2 - 4 * ((dp // 2) % 2), seq, side),
+        "c": (dp + 1 - 2 * (dp % 2), seq, side),
+        "y": (dp, 1 - seq, side),
+        "x": (dp, seq, 1 - side),
+    }
+    barrier = pltpu.get_barrier_semaphore()
+    for axis in AXES:
+        pl.semaphore_signal(
+            barrier, inc=1, device_id=partners[axis], device_id_type=pl.DeviceIdType.MESH
+        )
+    pl.semaphore_wait(barrier, len(AXES))
+    count = [0, 0]
+
+    def send(source, target, axis):
+        copy = pltpu.make_async_remote_copy(
+            source, target, sends.at[count[0]], receives.at[count[0]],
+            device_id=partners[axis], device_id_type=pl.DeviceIdType.MESH,
+        )
+        count[0] += 1
+        copy.start()
+        return copy
+
+    def load(source, target):
+        copy = pltpu.make_async_copy(source, target, local_sems.at[count[1]])
+        count[1] += 1
+        copy.start()
+        return copy
+
+    def add(target, source):
+        target[...] = (target[...].astype(F32) + source[...].astype(F32)).astype(BF)
+
+    dx_copy = send(their_dx_ref, dx_slot, "x")
+    names = ["A", "B"] + ["Q%d" % i for i in range(queries)]
+    work = dict(zip(names, works))
+    slot = {name: slots[4 * i : 4 * i + 4] for i, name in enumerate(names)}
+    first = dict.fromkeys(names, "y")
+    first["B"] = "x"
+    flying = {}
+    for i in range(queries):
+        own, other = inputs[4 + 2 * i], inputs[5 + 2 * i]
+        name = "Q%d" % i
+        flying[name] = [load(own, work[name]), send(other, slot[name][0], "c")]
+    for i, name in enumerate("AB"):
+        flying[name] = [load(inputs[2 * i], work[name]), load(inputs[2 * i + 1], slot[name][0])]
+
+    def part(name, step):
+        ref, mine = work[name], here[first[name]]
+        if step == 0:
+            return ref.at[mine], ref.at[1 - mine]
+        if step == 1:
+            return ref.at[mine, :, here["z1"]], ref.at[mine, :, 1 - here["z1"]]
+        return ref.at[mine, here["z2"], here["z1"]], ref.at[mine, 1 - here["z2"], here["z1"]]
+
+    def advance(name, step):
+        for copy in flying[name]:
+            copy.wait()
+        keep = work[name] if step == 0 else part(name, step - 1)[0]
+        add(keep, slot[name][step])
+        axis = (first[name], "z1", "z2")[step]
+        flying[name] = [send(part(name, step)[1], slot[name][step + 1], axis)]
+
+    def end(name):
+        for copy in flying[name]:
+            copy.wait()
+        return part(name, 2)[0][...].astype(F32) + slot[name][3][...].astype(F32)
+
+    odd = here["c"] == 1
+    for name in ("A", "B") + tuple(names[2:]):
+        advance(name, 0)
+    total = x2_ref[...] + (y_ref[...].astype(F32) + y_got_ref[...].astype(F32))
+    block_ref[...] = put_back(total.astype(BF).astype(F32), turn_ref[...], odd, 1).astype(BF)
+    advance("A", 1)
+    dx_copy.wait()
+    normal, scale = normalize(rows_ref[...].astype(F32))
+    grads = dx_ref[...].astype(F32) + dx_slot[...].astype(F32)
+    total = dx1_ref[...] + normalize_back(grads, gains_ref[0:1, :], normal, scale)
+    dinput_ref[...] = put_back(total, turn_ref[...], odd, 2)
+    advance("A", 2)
+    advance(names[2], 1)
+    advance("B", 1)
+    for name in names[3:]:
+        advance(name, 1)
+    advance(names[2], 2)
+    advance("B", 2)
+    for name in names[3:]:
+        advance(name, 2)
+
+    wide = cq_ref.shape[1]
+    grads = end("A")
+    out_ref[...] = jnp.transpose(grads[:, :wide])
+    cq_ref[...] = grads[:, wide:]
+    second = jnp.sum(grads[:, wide:] * query_weight[...].astype(F32), axis=1, keepdims=True)
+    grads = end("B")
+    ckv_ref[...] = grads[:, :wide]
+    co_ref[...] = jnp.transpose(grads[:, wide:])
+    total = jnp.zeros(second.shape, F32)
+    j = 0
+    for name in names[2:]:
+        grads = end(name)
+        for at in range(0, grads.shape[1], 384):
+            for kind in range(3):
+                cut = slice(kind * wide + j * 128, kind * wide + (j + 1) * 128)
+                piece = grads[:, at + kind * 128 : at + (kind + 1) * 128]
+                qkv_ref[:, cut] = piece
+                total += jnp.sum(piece * qkv_weight[:, cut].astype(F32), axis=1, keepdims=True)
+            j += 1
+    lane = iota(norm_ref.shape, 1)
+    norm_ref[...] = jnp.where(
+        lane == 0,
+        total / gain_ref[:, 0:1],
+        jnp.where(lane == 1, second / gain_ref[:, 1:2], jnp.where(lane == 2, third_ref[...], 0.0)),
+    )
+    for at, axis in enumerate(("y", "x")):
+        send(norm_ref, norm_slot.at[at], axis).wait()
+        norm_ref[...] += norm_slot[at]
+
+
+def scatter_last(
+    dx, their_dx, gain_columns, qkv_weight, query_weight, third, x2, y, y_got, turn, rows, gains,
+    dx1, squares, queries,
+):
+    anywhere, vmem = pl.BlockSpec(memory_space=pl.ANY), pl.BlockSpec(memory_space=pltpu.VMEM)
+    shard, wide = query_weight.shape
+    shapes = [a.shape for a, _ in squares] + [a.shape for a, _ in queries]
+    assert all(shape[:3] == (2, 2, 2) for shape in shapes)
+    few = [dx, their_dx, gain_columns, qkv_weight, query_weight, third, x2, y, y_got, turn, rows]
+    few += [gains, dx1]
+    many = [a for pair in (*squares, *queries) for a in pair]
+    outs = [(x2.shape, BF), (x2.shape, F32), ((wide, shard), F32), ((shard, wide), F32)]
+    outs += [((shard, wide), F32), ((wide, shard), F32), ((shard, 3 * wide), F32)]
+    outs += [((shard, 128), F32)]
+    slots = [pltpu.VMEM(shape[at:], BF) for shape in shapes for at in range(4)]
+    copies = 1 + 2 + len(queries) * 4 + len(squares) * 3
+    return pl.pallas_call(
+        functools.partial(scatter_kernel, len(queries)),
+        in_specs=[vmem] * len(few) + [anywhere] * len(many),
+        out_specs=[vmem] * len(outs),
+        out_shape=[shaped(*out) for out in outs],
+        scratch_shapes=[pltpu.VMEM(rows.shape, BF), pltpu.VMEM((2, shard, 128), F32)]
+        + [pltpu.VMEM(shape, BF) for shape in shapes]
+        + slots
+        + [
+            pltpu.SemaphoreType.DMA((copies,)),
+            pltpu.SemaphoreType.DMA((copies,)),
+            pltpu.SemaphoreType.DMA((4 + len(queries),)),
+        ],
+        compiler_params=pltpu.CompilerParams(
+            vmem_limit_bytes=VMEM_BYTES, collective_id=1, has_side_effects=True
+        ),
+        name="scatter_last",
+    )(*few, *many)
+
+
+def swap(array, axis, bit=1):
+    return lax.ppermute(array, axis, [(i, i ^ bit) for i in range(lax.axis_size(axis))])
+
+
+def pair_body(
+    block_in,
+    cond_tokens,
+    cond_count,
+    norm1_gain,
+    norm2_gain,
+    norm3_gain,
+    qkv_weight,
+    attn_out_weight,
+    cross_q_weight,
+    cross_kv_weight,
+    cross_out_weight,
+    gate_up_weight,
+    down_weight,
+    out_cotangent,
+):
+    rows, width = block_in.shape
+    shard = qkv_weight.shape[0]
+    head_cols = attn_out_weight.shape[0]
+    hidden_cols = down_weight.shape[0]
+    cond_slots, cond_width = cond_tokens.shape[1:]
+    cond_shard = cross_kv_weight.shape[0]
+    dp = lax.axis_index("dp")
+    seq = lax.axis_index("seq")
+    side = lax.axis_index("half")
+    z_size = lax.axis_size("dp") // 2
+    core, z = dp % 2, dp // 2
+    odd = core.astype(jnp.int32).reshape(1)
+    half = width // 2
+    pairs_here = head_cols // 128
+    per_chunk = hidden_cols // CHUNKS
+    z_bits = []
+    bit = z_size // 2
+    while bit:
+        z_bits.append(bit)
+        bit //= 2
+
+    places = {"half": 0, "seq": 1}
+    steps = {"half": ("half", 1, 2), "seq": ("seq", 1, 1)}
+    for at, bit in enumerate(z_bits):
+        name = "z%d" % bit
+        places[name] = 2 + at
+        steps[name] = ("dp", 2 * bit, 4 + at)
+    far, near = "z%d" % z_bits[0], "z%d" % z_bits[-1]
+
+    class Way:
+        def __init__(self, own, other, wide, order):
+            full = (2 if wide else 1, 2) + (2,) * len(z_bits) + (shard, own.shape[-1])
+            self.order = list(order)
+            self.here = own.reshape(full)
+            self.got = swap(other, "dp", 1).reshape(full)
+
+        def step(self, after=(), late=()):
+            step = self.order.pop(0)
+            if late:
+                self.here = hold(self.here, late)
+            axis, bit, which = steps[step]
+            self.here, send = fold(place, which, self.here, self.got, places[step])
+            if after:
+                send = hold(send, after)
+            self.got = swap(send, axis, bit)
+            return self.here
+
+        def end(self):
+            while self.order:
+                self.step()
+            shape = self.here.shape[-2:]
+            return [self.here.reshape(shape), self.got.reshape(shape)]
+
+    qkv_pack = jnp.concatenate(
+        [
+            qkv_weight[:, :, j * 128 : (j + 1) * 128].reshape(shard, 384)
+            for j in range(pairs_here)
+        ],
+        axis=1,
+    )
+    square_pack = jnp.concatenate(
+        [
+            attn_out_weight.T,
+            cross_q_weight,
+            cross_kv_weight.transpose(1, 0, 2).reshape(shard, head_cols),
+            cross_out_weight.T,
+        ],
+        axis=1,
+    )
+    gains = jnp.stack([norm1_gain, norm2_gain, norm3_gain]).astype(F32)
+    gains = lax.dynamic_update_slice(jnp.zeros((8, width), F32), gains, (0, dp * shard))
+    gate_up_flat = gate_up_weight.reshape(shard, 2 * hidden_cols)
+    (
+        wq, w0, w1, w2, w3, mine_in, theirs_in, top_grads, their_top, gains, first_all,
+        first_across, turn, *ffn_pack,
+    ) = gather_first(
+        qkv_pack, square_pack, gains, block_in, out_cotangent, gate_up_flat, down_weight
+    )
+    wq = wq.reshape((z_size, 2, 2) + qkv_pack.shape)
+    squares = [w.reshape((z_size, 2, 2, 2, shard, head_cols)) for w in (w0, w1, w2, w3)]
+    place = jnp.stack([core, seq, side, cond_count[seq], z // 2, z % 2]).astype(jnp.int32)
+    ffn_weights = []
+    for i in range(CHUNKS):
+        gathered = lax.all_gather(ffn_pack[i], ("dp", "seq"))
+        ffn_weights.append(gathered.reshape((z_size, 2, 2) + ffn_pack[i].shape))
+
+    along = jnp.arange(rows)
+    tables = rot_tables(jnp.concatenate([side * rows + along, (1 - side) * rows + along]))
+    query, key, value, mine, theirs, lse = self_forward(place, first_all, wq, tables)
+    mixed = swap(theirs, "half")
+
+    my_cond = cond_tokens[seq].reshape(cond_slots, z_size, 2, cond_shard)
+    swapped = jnp.where(core == 1, my_cond[:, :, ::-1], my_cond)
+    my_cond = swapped.transpose(0, 2, 1, 3).reshape(cond_slots, cond_width)
+    my_cond = jnp.pad(my_cond, ((0, SLOTS - cond_slots), (0, 0)))
+    (top_across,) = across(top_grads)
+    (their_top_across,) = across(their_top)
+    cross_key, cross_value = cond_forward(place, my_cond, squares[2])
+    x1, second, cross_query, cross_mixed, x2, third = middle_forward(
+        place, mine_in, mine, mixed, gains, cross_key, cross_value, squares,
+        (top_across, their_top_across),
+    )
+    their_third = swap(third, "half")
+    (third_across,) = across(third)
+    (their_third_across,) = across(their_third)
+    ffn_weights[0] = hold(ffn_weights[0], (their_third_across, third_across))
+    sums, ways, after = (), [], ()
+    for i in range(CHUNKS):
+        *sums, gown, gother = ffn(
+            place,
+            (third, their_third),
+            (third_across, their_third_across),
+            (top_grads, their_top),
+            (top_across, their_top_across),
+            ffn_weights[i],
+            TILE,
+            sums,
+            after,
+        )
+        arrived = [way.got for way in ways]
+        if arrived:
+            gother = hold(gother, arrived)
+        ways.append(Way(gown, gother, False, ("seq", near, far)))
+        if i < CHUNKS - 1:
+            after = tuple(way.step() for way in ways)
+    ymine, ytheirs, dmine, dtheirs = sums
+    d_received = swap(hold(dtheirs, arrived), "half")
+
+    after = [way.step() for way in ways]
+    dx1, e2, dquery, dkey, dvalue, e1, dmine, dtheirs = middle_backward(
+        place, dmine, d_received, top_grads, x2, x1, gains,
+        cross_query, cross_key, cross_value, squares, after,
+    )
+    dtheirs = swap(dtheirs, "half")
+    y_received = swap(hold(ytheirs, (dx1,)), "half")
+    aown, aother, bown, bother, dcond = middle_weights(
+        place, e1, mine, mixed, second, dquery, my_cond, dkey, dvalue, e2, cross_mixed, squares[2]
+    )
+    arrived = [way.got for way in ways] + [dtheirs]
+    aother, bother = hold(aother, arrived), hold(bother, arrived)
+    dcond = hold(dcond, arrived)
+    first_way = Way(aown, aother, True, ("half", "seq", near, far))
+    second_way = Way(bown, bother, True, ("seq", "half", near, far))
+    qkv_grads = []
+    pairs = 2 * pairs_here
+    after = [dcond, y_received] + [way.step() for way in ways if way.order]
+    running = None
+    for first, several in ((0, 2), (2, pairs - 2)):
+        gown, gother, *sums = self_backward(
+            place, query, key, value, mine, theirs, dmine, dtheirs, lse, tables, first_across,
+            wq, first, several, running, first > 0, after,
+        )
+        full = (2, 2, 2, shard, gown.shape[-1])
+        qkv_grads.append((gown.reshape(full), gother.reshape(full)))
+        running = sums[0]
+        if first == 0:
+            arrived = [way.got for way in ways] + [first_way.got, second_way.got]
+            running = hold(running, arrived)
+            after = [way.step(late=(running,)) for way in ways if way.order]
+            after += [first_way.step(late=(running,)), second_way.step(late=(running,))]
+    rmine, rtheirs = sums
+    rtheirs = hold(rtheirs, (first_way.got, second_way.got, ways[-1].got))
+    gain_columns = [g.astype(F32).reshape(shard, 1) for g in (norm1_gain, norm2_gain, norm3_gain)]
+    grad_gate_up, grad_down, gain_third = finish_ffn(
+        gate_up_flat, gain_columns[2], [array for way in ways for array in way.end()]
+    )
+    grad_gate_up = grad_gate_up.reshape(shard, 2, hidden_cols)
+    (
+        block_out, grad_input, grad_out, grad_cq, grad_ckv, grad_co, grad_qkv, gain_grads,
+    ) = scatter_last(
+        rmine, rtheirs, jnp.concatenate(gain_columns[:2], axis=1),
+        qkv_weight.reshape(shard, 3 * head_cols), cross_q_weight, gain_third,
+        x2, ymine, y_received, turn, mine_in, gains, dx1,
+        [
+            tuple(a.reshape((2, 2, 2) + a.shape[-2:]) for a in (way.here, way.got))
+            for way in (first_way, second_way)
+        ],
+        qkv_grads,
+    )
+    grad_ckv = grad_ckv.reshape(2, cond_shard, head_cols).transpose(1, 0, 2)
+    grad_qkv = grad_qkv.reshape(shard, 3, head_cols)
+
+    dcond = dcond[:cond_slots].reshape(cond_slots, 2, z_size, cond_shard)
+    dcond = jnp.where(core == 1, dcond[:, ::-1], dcond).transpose(0, 2, 1, 3)
+    dcond = dcond.reshape(cond_slots, 2, 2, cond_width // 4)
+    cond_keep = lax.dynamic_index_in_dim(dcond, side, 2, keepdims=False)
+    cond_send = lax.dynamic_index_in_dim(dcond, 1 - side, 2, keepdims=False)
+    dcond = cond_keep + swap(cond_send, "half")
+    cond_keep = lax.dynamic_index_in_dim(dcond, seq, 1, keepdims=False)
+    cond_send = lax.dynamic_index_in_dim(dcond, 1 - seq, 1, keepdims=False)
+    cond_got = swap(cond_send, "seq")
+    grad_cond = jnp.stack(
+        [jnp.where(seq == 1, cond_got, cond_keep), jnp.where(seq == 1, cond_keep, cond_got)]
+    )
+
+    gain_grads = gain_grads[:, :3].T
+    return (
+        block_out,
+        grad_input,
+        grad_cond,
+        gain_grads[0],
+        gain_grads[1],
+        gain_grads[2],
+        grad_qkv,
+        grad_out,
+        grad_cq,
+        grad_ckv,
+        grad_co,
+        grad_gate_up,
+        grad_down,
+    )
+
+
+def pair_solution(mesh, sequences):
+    dp, tensor = mesh.devices.shape
+    finer = Mesh(mesh.devices.reshape(dp, sequences, tensor // sequences), ("dp", "seq", "half"))
+    every = ("dp", "seq", "half")
+    both = ("seq", "half")
+    return jax.shard_map(
+        pair_body,
+        mesh=finer,
+        in_specs=(
+            P(every, None),
+            P("dp", None, None),
+            P("dp"),
+            P("dp"),
+            P("dp"),
+            P("dp"),
+            P("dp", None, both),
+            P(both, "dp"),
+            P("dp", both),
+            P("dp", None, both),
+            P(both, "dp"),
+            P("dp", None, both),
+            P(both, "dp"),
+            P(every, None),
+        ),
+        out_specs=(
+            P(every, None),
+            P(every, None),
+            P("dp", None, both),
+            P("dp"),
+            P("dp"),
+            P("dp"),
+            P("dp", None, both),
+            P(both, "dp"),
+            P("dp", both),
+            P("dp", None, both),
+            P(both, "dp"),
+            P("dp", None, both),
+            P(both, "dp"),
+        ),
+        check_vma=False,
+    )
+
+
+CHUNKS = 3
+FLOPS = 1.15e9
+TILE = 256
+SLOTS = 256
+
+
+def solution(mesh):
+    dp, tensor = mesh.devices.shape
+
+    def run(*args):
+        block_in, cond_tokens, qkv, down = args[0], args[1], args[6], args[12]
+        sequences = cond_tokens.shape[0] // dp
+        fits = (
+            sequences == 2
+            and tensor == 4
+            and dp == 8
+            and qkv.shape[2] % (tensor * 128) == 0
+            and (qkv.shape[0] // dp) % 64 == 0
+            and down.shape[0] % (tensor * CHUNKS * TILE) == 0
+            and qkv.shape[0] == 2 * cond_tokens.shape[2]
+            and qkv.shape[2] == qkv.shape[0]
+            and cond_tokens.shape[1] <= SLOTS
+            and block_in.shape[0] == 1024 * cond_tokens.shape[0]
+        )
+        if fits:
+            return pair_solution(mesh, sequences)(*args)
+        return general_solution(mesh)(*args)
+
+    return run

time: 2260 us -> 967 us (0.43)
  waiting for transfers between devices: 1390 us -> 145 us
  Pallas kernels: 0 us -> 723 us
  matrix products: 388 us -> 0 us
  local copies, waits for them, and re-layouts: 265 us -> 54.9 us
  other arithmetic: 102 us -> 4.33 us
  blocking collectives: 70.4 us -> 0 us
    reduce_scatter x12 -> x0, waiting for transfers between devices: 872 us -> none  [the longest x3 358 us: project_out(): lax.psum_scatter(jnp.dot(mixed_all, weight, preferred_element_type=jnp.fl...]
    pallas_call x0 -> x41, Pallas kernels: none -> 723 us  [the longest x26 413 us: call(): pl.pallas_call(without_after, **how, out_shape=[shape for _, shape in out...]
    all_gather x13 -> x3, waiting for transfers between devices: 518 us -> 0.02 us  [pair_body(): gathered = lax.all_gather(ffn_pack[i], ('dp', 'seq'))]
    dot_general x49 -> x0, matrix products: 388 us -> none  [the longest x7 83.3 us: times_transposed(): lax.dot_general(left, right, (((1,), (1,)), ((), ())), preferred_element_...]
    ppermute x0 -> x23, waiting for transfers between devices: none -> 144 us  [swap(): lax.ppermute(array, axis, [(i, i ^ bit) for i in range(lax.axis_size(axis...]
    dynamic_update_slice x8 -> x1, local copies, waits for them, and re-layouts: 115 us -> 0.44 us  [pair_body(): lax.dynamic_update_slice(jnp.zeros((8, width), F32), gains, (0, dp * shard))]
    unnamed x2 -> x0, blocking collectives: 61.3 us -> none
    convert_element_type x17 -> x2, other arithmetic: 60.6 us -> 0.02 us  [the longest x1 0.01 us: pair_body(): gains = jnp.stack([norm1_gain, norm2_gain, norm3_gain]).astype(F32)]
  transfers between devices with their start and end apart: 27 -> 26, of which waited for: 22 -> 9; matrix products, arithmetic and copies ran while one was open for 27% -> 3% of each run, Pallas kernels for 0% -> 43%
where the time goes in v2:
time: 967 us; the launch traced here: 961 us
  Pallas kernels  723 us (75%)
  waiting for transfers between devices  145 us (15%)
  local copies, waits for them, and re-layouts  54.9 us (6%)
  starting transfers between devices  18.3 us (2%)
  between operations  14.8 us (2%)
    pallas_call x26, Pallas kernels, call(): pl.pallas_call(without_after, **how, out_shape=[shape for _, shape in out...  413 us
    pallas_call x1, Pallas kernels, gather_first(): pl.pallas_call(gather_kernel, in_specs=[anywhere, anywhere] + [vmem] * 5,...  182 us
    ppermute x23, waiting for transfers between devices, swap(): lax.ppermute(array, axis, [(i, i ^ bit) for i in range(lax.axis_size(axis...  144 us
    pallas_call x1, Pallas kernels, scatter_last(): pl.pallas_call(functools.partial(scatter_kernel, len(queries)), in_specs=...  128 us
    unnamed x76, local copies, waits for them, and re-layouts  24.6 us
  transfers between devices with their start and end apart: 26, of which 9 were waited for; matrix products, arithmetic and copies ran while one was open for 3% of the time, Pallas kernels for 43%

profile of v2, /device:TPU:0, one launch (start us, length us, event | category | flops | bytes accessed | tf_op | source)
XLA Modules:
  0.0 960.7 jit_solution(12414707698060326735)
XLA Ops:
  10.5 1.2 copy.158
  11.7 1.2 copy.127.down_ref
  15.1 182.3 %gather_first.1 = (bf16[2,2,2,2,192,1152]{5,4,3,2,1,0:T(8,128)(2,1)}, bf16[2,2,2,2,2,192,384]{6,5,4,3,2,1,0:T(8,128)(2,1)}, bf16[2,2,2,2,2,192,384]{6,5,4,3,2,1,...) custom-call(bf16[192,1152]{1,0:T(8,128)(2,1)} %pad_maximum_fusion.1., ...), custom_call_target="tpu_custom_call" | custom-call | tf_op jit(solution)/shard_map/gather_first/pallas_call | solution.py:653
  198.5 1.9 fusion.1
  200.5 1.7 concatenate.31.refs_5_.refs_10_
  202.3 1.7 concatenate.32.refs_6_.refs_11_
  204.6 1.7 concatenate.30.refs_4_.refs_9_
  206.4 1.3 stack.44.refs_0_
  207.6 36.9 %self_forward.1 = (bf16[1024,768]{1,0:T(8,128)(2,1)}, bf16[1024,768]{1,0:T(8,128)(2,1)}, bf16[1024,768]{1,0:T(8,128)(2,1)}, bf16[512,768]{1,0:T(8,128)(2,1)}, bf...) custom-call(s32[6]{0:T(128)} %stack.44.refs_0_, bf16[1024,1536]{1,0:T(8,128)(2,1)} %get-tuple-element.113.refs_1_, ...), custom_call_target="tpu_custom_call" | custom-call | flops 48299999232 | tf_op jit(solution)/shard_map/self_forward/pallas_call | solution.py:438
  244.5 2.0 collective-permute-start
  246.5 1.2 dynamic-slice_reduce_fusion
  248.0 3.1 rev.6
  251.1 3.1 across.4.refs_13_.refs_7_
  254.2 3.0 across.5.refs_14_.refs_8_
  258.6 6.3 cond_forward.1
  265.8 26.3 %middle_forward.1 = (f32[512,1536]{1,0:T(8,128)}, bf16[512,1536]{1,0:T(8,128)(2,1)}, bf16[512,1536]{1,0:T(8,128)(2,1)}, bf16[512,1536]{1,0:T(8,128)(2,1)}, f32[5...) custom-call(s32[6]{0:T(128)} %stack.44.refs_0_, bf16[512,1536]{1,0:T(8,128)(2,1)} %get-tuple-element.120.refs_1_.rows_ref, ...), custom_call_target="tpu_custom_call" | custom-call | flops 29899999232 | tf_op jit(solution)/shard_map/middle_forward/pallas_call | solution.py:438
  292.1 1.7 collective-permute-start.1
  293.8 3.0 across.6.refs_2_.refs_3_
  296.9 31.8 %collective-permute-done.1.refs_0_.refs_2_ = bf16[512,1536]{1,0:T(8,128)(2,1)S(1)} collective-permute-done((bf16[512,1536]{1,0:T(8,128)(2,1)}, bf16[512,1536]{1,0:T(8,128)(2,1)S(1)}, u32[]{:S(2)}, u32[]{:S(2)}) %collective-permute-start.1) | collective-permute-done | bytes 1572896 | tf_op jit(solution)/shard_map/ppermute | solution.py:1520
  328.7 1.2 copy-done.26
  329.9 3.1 across.7.refs_1_.refs_4_
  333.0 42.0 %feed_forward.3 = (bf16[512,1536]{1,0:T(8,128)(2,1)}, bf16[512,1536]{1,0:T(8,128)(2,1)}, bf16[512,1536]{1,0:T(8,128)(2,1)}, bf16[512,1536]{1,0:T(8,128)(2,1)}, b...) custom-call(s32[6]{0:T(128)} %stack.44.refs_0_, bf16[512,1536]{1,0:T(8,128)(2,1)} %get-tuple-element.130.refs_0_.refs_1_, ...), custom_call_target="tpu_custom_call" | custom-call | flops 41400000512 | tf_op jit(solution)/shard_map/feed_forward/pallas_call | solution.py:438
  375.0 8.2 collective-permute-done.2
  383.2 7.0 fold.11
  390.2 44.7 %feed_forward.4 = (bf16[512,1536]{1,0:T(8,128)(2,1)}, bf16[512,1536]{1,0:T(8,128)(2,1)}, bf16[512,1536]{1,0:T(8,128)(2,1)}, bf16[512,1536]{1,0:T(8,128)(2,1)}, b...) custom-call(s32[6]{0:T(128)} %stack.44.refs_0_, bf16[512,1536]{1,0:T(8,128)(2,1)} %get-tuple-element.130.refs_0_.refs_1_, ...), custom_call_target="tpu_custom_call" | custom-call | flops 41400000512 | tf_op jit(solution)/shard_map/feed_forward/pallas_call | solution.py:438
  434.9 34.1 %collective-permute-done.3.refs_1_ = bf16[1,1,2,2,192,1536]{5,4,3,2,1,0:T(8,128)(2,1)S(1)} collective-permute-done((bf16[1,1,2,2,192,1536]{5,4,3,2,1,0:T(8,128)(2,1)}, bf16[1,1,2,2,192,1536]{5,4,3,2,1,0:T(8,128)(2,1)S(1)}, u32[]{:S(2)}, u32[]{:S(2)}) %collective-permute-start.3) | collective-permute-done | bytes 2359328 | tf_op jit(solution)/shard_map/ppermute | solution.py:1520
  469.0 1.4 copy-done.5
  470.4 4.2 fold.12
  474.8 3.9 collective-permute-done.4
  478.6 6.9 fold.13
  485.8 44.0 %feed_forward.5 = (bf16[512,1536]{1,0:T(8,128)(2,1)}, bf16[512,1536]{1,0:T(8,128)(2,1)}, bf16[512,1536]{1,0:T(8,128)(2,1)}, bf16[512,1536]{1,0:T(8,128)(2,1)}, b...) custom-call(s32[6]{0:T(128)} %stack.44.refs_0_, bf16[512,1536]{1,0:T(8,128)(2,1)} %get-tuple-element.130.refs_0_.refs_1_, ...), custom_call_target="tpu_custom_call" | custom-call | flops 41400000512 | tf_op jit(solution)/shard_map/feed_forward/pallas_call | solution.py:438
  529.8 9.2 collective-permute-done.6.refs_2_
  539.1 1.4 copy-done.3
  540.5 1.2 collective-permute-start.7
  541.6 3.4 fold.14
  545.1 4.2 fold.15
  549.3 3.5 collective-permute-start.11
  552.9 7.1 fold.16
  560.0 17.5 %collective-permute-done.7.refs_2_ = bf16[512,1536]{1,0:T(8,128)(2,1)S(1)} collective-permute-done((bf16[512,1536]{1,0:T(8,128)(2,1)}, bf16[512,1536]{1,0:T(8,128)(2,1)S(1)}, u32[]{:S(2)}, u32[]{:S(2)}) %collective-permute-start.7) | collective-permute-done | bytes 1572896 | tf_op jit(solution)/shard_map/ppermute | solution.py:1520
  577.5 1.1 copy-done.27
  578.7 38.2 %middle_backward.1 = (f32[512,1536]{1,0:T(8,128)}, bf16[512,1536]{1,0:T(8,128)(2,1)}, bf16[512,1536]{1,0:T(8,128)(2,1)}, bf16[256,1536]{1,0:T(8,128)(2,1)}, bf16...) custom-call(s32[6]{0:T(128)} %stack.44.refs_0_, ...), custom_call_target="tpu_custom_call" | custom-call | flops 46000001024 | tf_op jit(solution)/shard_map/middle_backward/pallas_call | solution.py:438
  616.9 1.2 collective-permute-start.9
  619.2 22.8 %middle_weights.1 = (bf16[2,2,768,768]{3,2,1,0:T(8,128)(2,1)}, bf16[2,2,768,768]{3,2,1,0:T(8,128)(2,1)}, bf16[2,2,768,768]{3,2,1,0:T(8,128)(2,1)}, bf16[2,2,768,768]{3,2,1,0:T(8,128)(2,1)}, f32[256,768]{1,0:T(8,128)}) custom-call(s32[6]{0:T(128)} %stack.44.refs_0_, bf16[512,1536]{1,0:T(8,128)(2,1)} %get-tuple-element.166.refs_1_, ...), custom_call_target="tpu_custom_call" | custom-call | flops 25300000768 | tf_op jit(solution)/shard_map/middle_weights/pallas_call | solution.py:438
  642.0 28.9 %collective-permute-done.12.refs_3_ = bf16[1,1,2,2,192,1536]{5,4,3,2,1,0:T(8,128)(2,1)S(1)} collective-permute-done((bf16[1,1,2,2,192,1536]{5,4,3,2,1,0:T(8,128)(2,1)}, bf16[1,1,2,2,192,1536]{5,4,3,2,1,0:T(8,128)(2,1)S(1)}, u32[]{:S(2)}, u32[]{:S(2)}) %collective-permute-start.12) | collective-permute-done | bytes 2359328 | tf_op jit(solution)/shard_map/ppermute | solution.py:1520
  670.9 1.4 copy-done.2
  677.1 1.9 rev.7
  680.6 3.5 fold.17
  684.1 4.3 fold.18
  688.8 3.2 collective-permute-start.15
  692.6 26.7 %self_backward.2 = (bf16[2,768,384]{2,1,0:T(8,128)(2,1)}, bf16[2,768,384]{2,1,0:T(8,128)(2,1)}, f32[1024,1536]{1,0:T(8,128)}) custom-call(s32[6]{0:T(128)} %stack.44.refs_0_, bf16[1024,768]{1,0:T(8,128)(2,1)} %get-tuple-element.115.refs_1_, bf16[1024,768]{1,0:T(8,128)(2,1)} %get-tuple-element.116.refs_2_, bf16[1024,768]{1,0:T(8,128)(2,1)} %get-tuple-element.117.refs_3_, ...), custom_call_target="tpu_custom_call" | custom-call | flops 29899999232 | tf_op jit(solution)/shard_map/self_backward/pallas_call | solution.py:438
  720.2 10.2 %collective-permute-done.15 = bf16[1,1,2,1,192,1536]{5,4,2,3,1,0:T(8,128)(2,1)S(1)} collective-permute-done((bf16[1,1,2,1,192,1536]{5,4,2,3,1,0:T(8,128)(2,1)}, bf16[1,1,2,1,192,1536]{5,4,2,3,1,0:T(8,128)(2,1)S(1)}, u32[]{:S(2)}, u32[]{:S(2)}) %collective-permute-start.15) | collective-permute-done | bytes 1179680 | tf_op jit(solution)/shard_map/ppermute | solution.py:1520
  731.5 3.4 fold.19
  734.9 8.6 fold.21
  744.0 8.6 fold.20
  753.7 47.2 %self_backward.3 = (bf16[2,768,768]{2,1,0:T(8,128)(2,1)}, bf16[2,768,768]{2,1,0:T(8,128)(2,1)}, bf16[512,1536]{1,0:T(8,128)(2,1)}, bf16[512,1536]{1,0:T(8,128)(2,1)}) custom-call(s32[6]{0:T(128)} %stack.44.refs_0_, bf16[1024,768]{1,0:T(8,128)(2,1)} %get-tuple-element.115.refs_1_, bf16[1024,768]{1,0:T(8,128)(2,1)} %get-tuple-element.116.refs_2_, ...), custom_call_target="tpu_custom_call" | custom-call | flops 59799998464 | tf_op jit(solution)/shard_map/self_backward/pallas_call | solution.py:438
  801.7 4.7 finish_ffn.1
  806.5 4.4 reshape.318
  810.9 2.9 copy.152
  813.8 1.4 copy-done.8
  815.3 127.8 %scatter_last.1 = (bf16[512,1536]{1,0:T(8,128)(2,1)}, f32[512,1536]{1,0:T(8,128)}, f32[384,192]{1,0:T(8,128)}, f32[192,384]{1,0:T(8,128)}, f32[192,384]{1,0:T(8,...) custom-call(bf16[512,1536]{1,0:T(8,128)(2,1)} %get-tuple-element.191.dx_ref, ...), custom_call_target="tpu_custom_call" | custom-call | tf_op jit(solution)/shard_map/scatter_last/pallas_call | solution.py:1499
  943.1 2.2 copy.165
  948.9 1.1 copy.185
  950.0 1.3 copy-done.9
  951.4 1.7 copy.186
  (161 shorter events, 27.6 us)
Async XLA Ops:
  7.2 239.3 %copy-start = (bf16[2,130,768]{2,0,1:T(2,128)(2,1)S(1)}, bf16[2,130,768]{2,0,1:T(2,128)(2,1)}, u32[]{:S(2)}) copy-start(bf16[2,130,768]{2,0,1:T(2,128)(2,1)} %param.15) | copy-start | bytes 1198084
  7.2 3.3 copy-start.12
  7.2 325.8 %all-gather.11.cloned.1.call-start = ((), (), s32[]{:S(2)}) async-start(), calls=%async_computation.2 | async-start | bytes 10027008 | tf_op jit(solution)/shard_map/all_gather | solution.py:1622
  9.3 2.4 copy-start.16
  10.5 2.3 copy-start.24
  11.7 2.5 copy-start.13
  11.7 2.5 copy-start.22
  11.7 2.5 copy-start.23
  13.4 1.7 copy-start.21
  197.4 192.8 %all-gather.9.cloned.1.call-start = ((), (), s32[]{:S(2)}) async-start(), calls=%async_computation.1 | async-start | bytes 10027008 | tf_op jit(solution)/shard_map/all_gather | solution.py:1622
  198.2 287.7 %all-gather.7.cloned.1.call-start = ((), (), s32[]{:S(2)}) async-start(), calls=%async_computation | async-start | bytes 10027008 | tf_op jit(solution)/shard_map/all_gather | solution.py:1622
  202.3 1.7 copy-start.29
  244.5 20.4 %collective-permute-start = (bf16[512,768]{1,0:T(8,128)(2,1)}, bf16[512,768]{1,0:T(8,128)(2,1)S(1)}, u32[]{:S(2)}, u32[]{:S(2)}) collective-permute-start(bf16[512,768]{1,0:T(8,128)(2,1)} %get-tuple-element.119.refs_5_), channel_id=1, source_target_pairs={{0,1},{1,0},{2,3},{3,2},{4,5},{5,4},{6,7},{7,6},{8,9},{9,8},{10,11... | collective-permute-start | bytes 2359304 | tf_op jit(solution)/shard_map/ppermute | solution.py:1520
  264.9 0.9 copy-start.28
  292.1 36.6 %collective-permute-start.1 = (bf16[512,1536]{1,0:T(8,128)(2,1)}, bf16[512,1536]{1,0:T(8,128)(2,1)S(1)}, u32[]{:S(2)}, u32[]{:S(2)}) collective-permute-start(bf16[512,1536]{1,0:T(8,128)(2,1)} %get-tuple-element.130.refs_0_.refs_1_), channel_id=1, source_target_pairs={{0,1},{1,0},{2,3},{3,2},{4,5},{5,4},{6,7},{7,6},{8,9},{9,8},{10,11... | collective-permute-start | bytes 4718600 | tf_op jit(solution)/shard_map/ppermute | solution.py:1520
  328.7 1.2 copy-start.26
  374.9 8.3 collective-permute-start.2
  390.2 78.8 %collective-permute-start.3 = (bf16[1,1,2,2,192,1536]{5,4,3,2,1,0:T(8,128)(2,1)}, bf16[1,1,2,2,192,1536]{5,4,3,2,1,0:T(8,128)(2,1)S(1)}, u32[]{:S(2)}, u32[]{:S(2)}) collective-permute-start(bf16[1,1,2,2,192,1536]{5,4,3,2,1,0:T(8,128)(2,1)} %bitcast.244), channel_id=1, source_target_pairs={{0,2},{2,0},{1,3},{3,1},{4,6},{6,4},{5,7},{7,5},{8,10},{10,8},{9,1... | collective-permute-start | bytes 7077896 | tf_op jit(solution)/shard_map/ppermute | solution.py:1520
  469.0 1.4 copy-start.5
  470.4 8.3 collective-permute-start.4
  474.6 55.2 %collective-permute-start.5 = (bf16[1,1,2,1,192,1536]{5,4,3,2,1,0:T(8,128)(2,1)}, bf16[1,1,2,1,192,1536]{5,4,3,2,1,0:T(8,128)(2,1)S(1)}, u32[]{:S(2)}, u32[]{:S(2)}) collective-permute-start(bf16[1,1,2,1,192,1536]{5,4,3,2,1,0:T(8,128)(2,1)} %bitcast.247), channel_id=1, source_target_pairs={{0,8},{4,12},{8,0},{12,4},{16,24},{20,28},{24,16},{28,20},{1,9},{5... | collective-permute-start | bytes 3538952 | tf_op jit(solution)/shard_map/ppermute | solution.py:1520
  485.6 53.5 %collective-permute-start.6 = (bf16[1,1,2,2,192,1536]{5,4,3,2,1,0:T(8,128)(2,1)}, bf16[1,1,2,2,192,1536]{5,4,3,2,1,0:T(8,128)(2,1)S(1)}, u32[]{:S(2)}, u32[]{:S(2)}) collective-permute-start(bf16[1,1,2,2,192,1536]{5,4,3,2,1,0:T(8,128)(2,1)} %bitcast.243), channel_id=1, source_target_pairs={{0,2},{2,0},{1,3},{3,1},{4,6},{6,4},{5,7},{7,5},{8,10},{10,8},{9,1... | collective-permute-start | bytes 7077896 | tf_op jit(solution)/shard_map/ppermute | solution.py:1520
  529.8 9.2 copy-start.6
  539.1 1.4 copy-start.3
  540.5 12.4 %collective-permute-start.8 = (bf16[2,768,1536]{2,1,0:T(8,128)(2,1)}, bf16[2,768,1536]{2,1,0:T(8,128)(2,1)}, u32[]{:S(2)}, u32[]{:S(2)}) collective-permute-start(bf16[2,768,1536]{2,1,0:T(8,128)(2,1)} %hold.16), channel_id=1, source_target_pairs={{0,4},{4,0},{8,12},{12,8},{16,20},{20,16},{24,28},{28,24},{1,5},{5... | collective-permute-start | bytes 14155784 | tf_op jit(solution)/shard_map/ppermute | solution.py:1520
  540.5 37.0 %collective-permute-start.7 = (bf16[512,1536]{1,0:T(8,128)(2,1)}, bf16[512,1536]{1,0:T(8,128)(2,1)S(1)}, u32[]{:S(2)}, u32[]{:S(2)}) collective-permute-start(bf16[512,1536]{1,0:T(8,128)(2,1)} %hold.15), channel_id=1, source_target_pairs={{0,1},{1,0},{2,3},{3,2},{4,5},{5,4},{6,7},{7,6},{8,9},{9,8},{10,11... | collective-permute-start | bytes 4718600 | tf_op jit(solution)/shard_map/ppermute | solution.py:1520
  545.1 96.9 %collective-permute-start.10 = (bf16[1,1,1,1,192,1536]{5,4,3,2,1,0:T(8,128)(2,1)}, bf16[1,1,1,1,192,1536]{5,4,3,2,1,0:T(8,128)(2,1)}, u32[]{:S(2)}, u32[]{:S(2)}) collective-permute-start(bf16[1,1,1,1,192,1536]{5,4,3,2,1,0:T(8,128)(2,1)} %bitcast.252), channel_id=1, source_target_pairs={{0,16},{4,20},{8,24},{12,28},{16,0},{20,4},{24,8},{28,12},{1,17},{... | collective-permute-start | bytes 1769480 | tf_op jit(solution)/shard_map/ppermute | solution.py:1520
  549.3 92.6 %collective-permute-start.11 = (bf16[1,1,2,1,192,1536]{5,4,3,2,1,0:T(8,128)(2,1)}, bf16[1,1,2,1,192,1536]{5,4,3,2,1,0:T(8,128)(2,1)S(1)}, u32[]{:S(2)}, u32[]{:S(2)}) collective-permute-start(bf16[1,1,2,1,192,1536]{5,4,3,2,1,0:T(8,128)(2,1)} %bitcast.245), channel_id=1, source_target_pairs={{0,8},{4,12},{8,0},{12,4},{16,24},{20,28},{24,16},{28,20},{1,9},{5... | collective-permute-start | bytes 3538952 | tf_op jit(solution)/shard_map/ppermute | solution.py:1520
  577.5 1.1 copy-start.27
  616.9 25.1 %collective-permute-start.9 = (bf16[512,768]{1,0:T(8,128)(2,1)}, bf16[512,768]{1,0:T(8,128)(2,1)}, u32[]{:S(2)}, u32[]{:S(2)}) collective-permute-start(bf16[512,768]{1,0:T(8,128)(2,1)} %get-tuple-element.163), channel_id=1, source_target_pairs={{0,1},{1,0},{2,3},{3,2},{4,5},{5,4},{6,7},{7,6},{8,9},{9,8},{10,11... | collective-permute-start | bytes 2359304 | tf_op jit(solution)/shard_map/ppermute | solution.py:1520
  618.0 52.8 %collective-permute-start.12 = (bf16[1,1,2,2,192,1536]{5,4,3,2,1,0:T(8,128)(2,1)}, bf16[1,1,2,2,192,1536]{5,4,3,2,1,0:T(8,128)(2,1)S(1)}, u32[]{:S(2)}, u32[]{:S(2)}) collective-permute-start(bf16[1,1,2,2,192,1536]{5,4,3,2,1,0:T(8,128)(2,1)} %bitcast.240), channel_id=1, source_target_pairs={{0,2},{2,0},{1,3},{3,1},{4,6},{6,4},{5,7},{7,5},{8,10},{10,8},{9,1... | collective-permute-start | bytes 7077896 | tf_op jit(solution)/shard_map/ppermute | solution.py:1520
  618.3 73.7 %collective-permute-start.13 = (bf16[512,1536]{1,0:T(8,128)(2,1)}, bf16[512,1536]{1,0:T(8,128)(2,1)}, u32[]{:S(2)}, u32[]{:S(2)}) collective-permute-start(bf16[512,1536]{1,0:T(8,128)(2,1)} %hold.18), channel_id=1, source_target_pairs={{0,1},{1,0},{2,3},{3,2},{4,5},{5,4},{6,7},{7,6},{8,9},{9,8},{10,11... | collective-permute-start | bytes 4718600 | tf_op jit(solution)/shard_map/ppermute | solution.py:1520
  642.0 28.9 %copy-start.4 = (bf16[1,1,2,1,192,1536]{5,4,3,2,1,0:T(8,128)(2,1)}, bf16[1,1,2,1,192,1536]{5,4,3,2,1,0:T(8,128)(2,1)S(1)}, u32[]{:S(2)}) copy-start(bf16[1,1,2,1,192,1536]{5,4,3,2,1,0:T(8,128)(2,1)S(1)} %collective-permute-done.11.refs_2_) | copy-start | bytes 3538948
  670.9 1.4 copy-start.2
  672.3 58.2 %collective-permute-start.17 = (bf16[2,2,768,768]{3,2,1,0:T(8,128)(2,1)}, bf16[2,2,768,768]{3,2,1,0:T(8,128)(2,1)}, u32[]{:S(2)}, u32[]{:S(2)}) collective-permute-start(bf16[2,2,768,768]{3,2,1,0:T(8,128)(2,1)} %hold.20), channel_id=1, source_target_pairs={{0,4},{4,0},{8,12},{12,8},{16,20},{20,16},{24,28},{28,24},{1,5},{5... | collective-permute-start | bytes 14155784 | tf_op jit(solution)/shard_map/ppermute | solution.py:1520
  672.3 0.7 copy-start.30
  672.3 0.7 copy-start.31
  672.3 0.7 copy-start.32
  672.3 1.4 copy-start.10
  672.3 58.2 %collective-permute-start.16 = (bf16[2,2,768,768]{3,2,1,0:T(8,128)(2,1)}, bf16[2,2,768,768]{3,2,1,0:T(8,128)(2,1)}, u32[]{:S(2)}, u32[]{:S(2)}) collective-permute-start(bf16[2,2,768,768]{3,2,1,0:T(8,128)(2,1)} %hold.19), channel_id=1, source_target_pairs={{0,4},{4,0},{8,12},{12,8},{16,20},{20,16},{24,28},{28,24},{1,5},{5... | collective-permute-start | bytes 14155784 | tf_op jit(solution)/shard_map/ppermute | solution.py:1520
  679.7 9.1 collective-permute-start.21
  684.1 36.2 %collective-permute-start.14 = (bf16[1,1,1,1,192,1536]{5,4,3,2,1,0:T(8,128)(2,1)}, bf16[1,1,1,1,192,1536]{5,4,3,2,1,0:T(8,128)(2,1)S(1)}, u32[]{:S(2)}, u32[]{:S(2)}) collective-permute-start(bf16[1,1,1,1,192,1536]{5,4,3,2,1,0:T(8,128)(2,1)} %bitcast.255), channel_id=1, source_target_pairs={{0,16},{4,20},{8,24},{12,28},{16,0},{20,4},{24,8},{28,12},{1,17},{... | collective-permute-start | bytes 1769480 | tf_op jit(solution)/shard_map/ppermute | solution.py:1520
  688.8 41.6 %collective-permute-start.15 = (bf16[1,1,2,1,192,1536]{5,4,2,3,1,0:T(8,128)(2,1)}, bf16[1,1,2,1,192,1536]{5,4,2,3,1,0:T(8,128)(2,1)S(1)}, u32[]{:S(2)}, u32[]{:S(2)}) collective-permute-start(bf16[1,1,2,1,192,1536]{5,4,2,3,1,0:T(8,128)(2,1)} %bitcast.246), channel_id=1, source_target_pairs={{0,8},{4,12},{8,0},{12,4},{16,24},{20,28},{24,16},{28,20},{1,9},{5... | collective-permute-start | bytes 3538952 | tf_op jit(solution)/shard_map/ppermute | solution.py:1520
  692.1 27.3 %collective-permute-start.22 = (f32[130,192]{1,0:T(8,128)S(1)}, f32[130,192]{1,0:T(8,128)S(1)}, u32[]{:S(2)}, u32[]{:S(2)}) collective-permute-start(f32[130,192]{1,0:T(8,128)S(1)} %dynamic-slice_bitcast_fusion.1), channel_id=1, source_target_pairs={{0,2},{2,0},{1,3},{3,1},{4,6},{6,4},{5,7},{7,5},{8,10},{10,8},{9,1... | collective-permute-start | bytes 299528 | tf_op jit(solution)/shard_map/ppermute | solution.py:1520
  720.2 10.2 %copy-start.14 = (bf16[1,1,1,1,192,1536]{5,4,3,2,1,0:T(8,128)(2,1)}, bf16[1,1,1,1,192,1536]{5,4,3,2,1,0:T(8,128)(2,1)S(1)}, u32[]{:S(2)}) copy-start(bf16[1,1,1,1,192,1536]{5,4,3,2,1,0:T(8,128)(2,1)S(1)} %collective-permute-done.14.refs_2_) | copy-start | bytes 1769476
  730.5 1.0 copy-start.7
  734.9 66.0 %collective-permute-start.20 = (bf16[1,1,1,1,192,1536]{5,4,3,2,1,0:T(8,128)(2,1)}, bf16[1,1,1,1,192,1536]{5,4,3,2,1,0:T(8,128)(2,1)S(1)}, u32[]{:S(2)}, u32[]{:S(2)}) collective-permute-start(bf16[1,1,1,1,192,1536]{5,4,3,2,1,0:T(8,128)(2,1)} %bitcast.256), channel_id=1, source_target_pairs={{0,16},{4,20},{8,24},{12,28},{16,0},{20,4},{24,8},{28,12},{1,17},{... | collective-permute-start | bytes 1769480 | tf_op jit(solution)/shard_map/ppermute | solution.py:1520
  743.5 70.3 %collective-permute-start.19 = (bf16[2,1,2,2,192,768]{5,4,3,2,0,1:T(8,128)(2,1)}, bf16[2,1,2,2,192,768]{5,4,3,2,0,1:T(8,128)(2,1)S(1)}, u32[]{:S(2)}, u32[]{:S(2)}) collective-permute-start(bf16[2,1,2,2,192,768]{5,4,3,2,0,1:T(8,128)(2,1)} %bitcast.241), channel_id=1, source_target_pairs={{0,2},{2,0},{1,3},{3,1},{4,6},{6,4},{5,7},{7,5},{8,10},{10,8},{9,1... | collective-permute-start | bytes 7077896 | tf_op jit(solution)/shard_map/ppermute | solution.py:1520
  752.5 61.3 %collective-permute-start.18 = (bf16[1,2,2,2,192,768]{5,4,3,2,1,0:T(8,128)(2,1)}, bf16[1,2,2,2,192,768]{5,4,3,2,1,0:T(8,128)(2,1)}, u32[]{:S(2)}, u32[]{:S(2)}) collective-permute-start(bf16[1,2,2,2,192,768]{5,4,3,2,1,0:T(8,128)(2,1)} %bitcast.242), channel_id=1, source_target_pairs={{0,1},{1,0},{2,3},{3,2},{4,5},{5,4},{6,7},{7,6},{8,9},{9,8},{10,11... | collective-permute-start | bytes 7077896 | tf_op jit(solution)/shard_map/ppermute | solution.py:1520
  800.9 0.8 copy-start.15
  813.8 1.5 copy-start.8
  943.1 2.3 copy-start.20
  943.1 3.2 copy-start.18
  943.1 4.1 copy-start.17
  943.1 4.9 copy-start.25
  945.4 3.6 copy-start.11
  948.9 2.5 copy-start.9
  951.4 1.7 copy-start.19
  951.4 2.4 copy-start.1
Sparse Core Ops, SparseCore 0:
  197.5 81.4 all-gather.10
  281.3 79.5 all-gather.8
  363.2 105.1 all-gather.6

commit v3 on v2

--- a/solution.py
+++ b/solution.py
@@ -19,6 +19,7 @@
 NN = (((1,), (0,)), ((), ()))
 NT = (((1,), (1,)), ((), ()))
 VMEM_BYTES = 60 << 20
+DP, TENSOR = "dp", "tensor"
 
 
 def layer_norm(values, gain):
@@ -125,7 +126,7 @@
 ):
     local_rows = block_in.shape[0]
     model_width = block_in.shape[1]
-    group_rows = local_rows * lax.axis_size("tensor")
+    group_rows = local_rows * lax.axis_size(TENSOR)
     seq_here = cond_tokens.shape[0]
     seq_length = group_rows // seq_here
     cond_slots = cond_tokens.shape[1]
@@ -134,16 +135,16 @@
     heads_here = head_cols // HD
     hidden_here = down_weight.shape[0]
     gain_one, gain_two, gain_three, w_qkv, w_out, w_cq, w_ckv, w_co, w_gu, w_down = (
-        lax.all_gather(norm1_gain, "dp", axis=0, tiled=True),
-        lax.all_gather(norm2_gain, "dp", axis=0, tiled=True),
-        lax.all_gather(norm3_gain, "dp", axis=0, tiled=True),
-        lax.all_gather(qkv_weight, "dp", axis=0, tiled=True),
-        lax.all_gather(attn_out_weight, "dp", axis=1, tiled=True),
-        lax.all_gather(cross_q_weight, "dp", axis=0, tiled=True),
-        lax.all_gather(cross_kv_weight, "dp", axis=0, tiled=True),
-        lax.all_gather(cross_out_weight, "dp", axis=1, tiled=True),
-        lax.all_gather(gate_up_weight, "dp", axis=0, tiled=True),
-        lax.all_gather(down_weight, "dp", axis=1, tiled=True),
+        lax.all_gather(norm1_gain, DP, axis=0, tiled=True),
+        lax.all_gather(norm2_gain, DP, axis=0, tiled=True),
+        lax.all_gather(norm3_gain, DP, axis=0, tiled=True),
+        lax.all_gather(qkv_weight, DP, axis=0, tiled=True),
+        lax.all_gather(attn_out_weight, DP, axis=1, tiled=True),
+        lax.all_gather(cross_q_weight, DP, axis=0, tiled=True),
+        lax.all_gather(cross_kv_weight, DP, axis=0, tiled=True),
+        lax.all_gather(cross_out_weight, DP, axis=1, tiled=True),
+        lax.all_gather(gate_up_weight, DP, axis=0, tiled=True),
+        lax.all_gather(down_weight, DP, axis=1, tiled=True),
     )
     quarter = HD // 4
     positions = (jnp.arange(group_rows) % seq_length).astype(jnp.float32)
@@ -158,22 +159,22 @@
         return array.reshape((seq_here, seq_length) + array.shape[1:])
 
     def spread_rows(local_part):
-        return lax.all_gather(local_part, "tensor", axis=0, tiled=True)
+        return lax.all_gather(local_part, TENSOR, axis=0, tiled=True)
 
     def project_out(mixed_all, weight):
         return lax.psum_scatter(
             jnp.dot(mixed_all, weight, preferred_element_type=jnp.float32),
-            "tensor",
+            TENSOR,
             scatter_dimension=0,
             tiled=True,
         )
 
     def spread_grads(local_part):
-        return lax.all_gather(local_part, "tensor", axis=0, tiled=True)
+        return lax.all_gather(local_part, TENSOR, axis=0, tiled=True)
 
     def gather_back(grad_all, weight):
         return lax.psum_scatter(
-            times_transposed(grad_all, weight), "tensor", scatter_dimension=0, tiled=True
+            times_transposed(grad_all, weight), TENSOR, scatter_dimension=0, tiled=True
         )
 
     def self_forward(seq_parts):
@@ -239,16 +240,16 @@
     hidden = gated(gate_vals, up_vals).astype(jnp.bfloat16)
     block_out = (after_cross + project_out(hidden, w_down)).astype(jnp.bfloat16)
     gain_one, gain_two, gain_three, w_qkv, w_out, w_cq, w_ckv, w_co, w_gu, w_down = (
-        lax.all_gather(norm1_gain, "dp", axis=0, tiled=True),
-        lax.all_gather(norm2_gain, "dp", axis=0, tiled=True),
-        lax.all_gather(norm3_gain, "dp", axis=0, tiled=True),
-        lax.all_gather(qkv_weight, "dp", axis=0, tiled=True),
-        lax.all_gather(attn_out_weight, "dp", axis=1, tiled=True),
-        lax.all_gather(cross_q_weight, "dp", axis=0, tiled=True),
-        lax.all_gather(cross_kv_weight, "dp", axis=0, tiled=True),
-        lax.all_gather(cross_out_weight, "dp", axis=1, tiled=True),
-        lax.all_gather(gate_up_weight, "dp", axis=0, tiled=True),
-        lax.all_gather(down_weight, "dp", axis=1, tiled=True),
+        lax.all_gather(norm1_gain, DP, axis=0, tiled=True),
+        lax.all_gather(norm2_gain, DP, axis=0, tiled=True),
+        lax.all_gather(norm3_gain, DP, axis=0, tiled=True),
+        lax.all_gather(qkv_weight, DP, axis=0, tiled=True),
+        lax.all_gather(attn_out_weight, DP, axis=1, tiled=True),
+        lax.all_gather(cross_q_weight, DP, axis=0, tiled=True),
+        lax.all_gather(cross_kv_weight, DP, axis=0, tiled=True),
+        lax.all_gather(cross_out_weight, DP, axis=1, tiled=True),
+        lax.all_gather(gate_up_weight, DP, axis=0, tiled=True),
+        lax.all_gather(down_weight, DP, axis=1, tiled=True),
     )
     gain_first = gain_one.astype(jnp.float32)
     gain_second = gain_two.astype(jnp.float32)
@@ -293,7 +294,7 @@
     cond_partial = times_transposed(
         grad_cross_kv, w_ckv.reshape(cond_width, 2 * head_cols)
     ).reshape(seq_here, cond_slots, cond_width)
-    grad_cond = lax.psum_scatter(cond_partial, "tensor", scatter_dimension=2, tiled=True)
+    grad_cond = lax.psum_scatter(cond_partial, TENSOR, scatter_dimension=2, tiled=True)
     grad_second = gather_back(grad_cross_query, w_cq)
     norm_out, norm_pull = jax.vjp(layer_norm, after_self, gain_second)
     part_rows, grad_gain_second = norm_pull(grad_second)
@@ -325,18 +326,18 @@
     part_rows, grad_gain_first = norm_pull(grad_first)
     grad_input = grad_self_rows + part_rows
     owned = (
-        lax.psum_scatter(grad_gain_first, "dp", scatter_dimension=0, tiled=True),
-        lax.psum_scatter(grad_gain_second, "dp", scatter_dimension=0, tiled=True),
-        lax.psum_scatter(grad_gain_third, "dp", scatter_dimension=0, tiled=True),
-        lax.psum_scatter(grad_qkv_weight, "dp", scatter_dimension=0, tiled=True),
-        lax.psum_scatter(grad_out_weight, "dp", scatter_dimension=1, tiled=True),
-        lax.psum_scatter(grad_cq_weight, "dp", scatter_dimension=0, tiled=True),
-        lax.psum_scatter(grad_ckv_weight, "dp", scatter_dimension=0, tiled=True),
-        lax.psum_scatter(grad_co_weight, "dp", scatter_dimension=1, tiled=True),
-        lax.psum_scatter(grad_gu_weight, "dp", scatter_dimension=0, tiled=True),
-        lax.psum_scatter(grad_down, "dp", scatter_dimension=1, tiled=True),
-    )
-    gain_grads = lax.psum((owned[0], owned[1], owned[2]), "tensor")
+        lax.psum_scatter(grad_gain_first, DP, scatter_dimension=0, tiled=True),
+        lax.psum_scatter(grad_gain_second, DP, scatter_dimension=0, tiled=True),
+        lax.psum_scatter(grad_gain_third, DP, scatter_dimension=0, tiled=True),
+        lax.psum_scatter(grad_qkv_weight, DP, scatter_dimension=0, tiled=True),
+        lax.psum_scatter(grad_out_weight, DP, scatter_dimension=1, tiled=True),
+        lax.psum_scatter(grad_cq_weight, DP, scatter_dimension=0, tiled=True),
+        lax.psum_scatter(grad_ckv_weight, DP, scatter_dimension=0, tiled=True),
+        lax.psum_scatter(grad_co_weight, DP, scatter_dimension=1, tiled=True),
+        lax.psum_scatter(grad_gu_weight, DP, scatter_dimension=0, tiled=True),
+        lax.psum_scatter(grad_down, DP, scatter_dimension=1, tiled=True),
+    )
+    gain_grads = lax.psum((owned[0], owned[1], owned[2]), TENSOR)
     return (
         block_out,
         grad_input,
@@ -359,35 +360,35 @@
         general_body,
         mesh=mesh,
         in_specs=(
-            P(("dp", "tensor"), None),
-            P("dp", None, None),
-            P("dp"),
-            P("dp"),
-            P("dp"),
-            P("dp"),
-            P("dp", None, "tensor"),
-            P("tensor", "dp"),
-            P("dp", "tensor"),
-            P("dp", None, "tensor"),
-            P("tensor", "dp"),
-            P("dp", None, "tensor"),
-            P("tensor", "dp"),
-            P(("dp", "tensor"), None),
+            P((DP, TENSOR), None),
+            P(DP, None, None),
+            P(DP),
+            P(DP),
+            P(DP),
+            P(DP),
+            P(DP, None, TENSOR),
+            P(TENSOR, DP),
+            P(DP, TENSOR),
+            P(DP, None, TENSOR),
+            P(TENSOR, DP),
+            P(DP, None, TENSOR),
+            P(TENSOR, DP),
+            P((DP, TENSOR), None),
         ),
         out_specs=(
-            P(("dp", "tensor"), None),
-            P(("dp", "tensor"), None),
-            P("dp", None, "tensor"),
-            P("dp"),
-            P("dp"),
-            P("dp"),
-            P("dp", None, "tensor"),
-            P("tensor", "dp"),
-            P("dp", "tensor"),
-            P("dp", None, "tensor"),
-            P("tensor", "dp"),
-            P("dp", None, "tensor"),
-            P("tensor", "dp"),
+            P((DP, TENSOR), None),
+            P((DP, TENSOR), None),
+            P(DP, None, TENSOR),
+            P(DP),
+            P(DP),
+            P(DP),
+            P(DP, None, TENSOR),
+            P(TENSOR, DP),
+            P(DP, TENSOR),
+            P(DP, None, TENSOR),
+            P(TENSOR, DP),
+            P(DP, None, TENSOR),
+            P(TENSOR, DP),
         ),
         check_vma=False,
     )
@@ -513,36 +514,35 @@
     ) * scale
 
 
-def first_norm(mine_ref, theirs_ref, gains_ref, out_ref, across_ref):
-    rows = mine_ref.shape[0]
+def first_norm(ref, base, gains_ref, out_ref, across_ref):
     step = 256
-    for ref, base in ((mine_ref, 0), (theirs_ref, rows)):
-        for at in range(0, rows, step):
-            normal, _ = normalize(ref[at : at + step, :].astype(F32))
-            out = (normal * gains_ref[0:1, :]).astype(BF)
-            out_ref[base + at : base + at + step, :] = out
-            across_ref[:, base + at : base + at + step] = jnp.transpose(out)
-
-
-QKV_CHAINS = (("z2", "z1", "y", "c"), ("z2", "y", "z1", "c"))
+    for at in range(0, ref.shape[0], step):
+        normal, _ = normalize(ref[at : at + step, :].astype(F32))
+        out = (normal * gains_ref[0:1, :]).astype(BF)
+        out_ref[base + at : base + at + step, :] = out
+        across_ref[:, base + at : base + at + step] = jnp.transpose(out)
+
+
+QKV_CHAINS = (("z2", "y", "z1", "c"), ("z1", "z2", "y", "c"))
 SQUARE_CHAINS = (
-    ("z2", "z1", "y", "x", "c"),
+    ("x", "z1", "y", "z2", "c"),
+    ("z2", "y", "x", "z1", "c"),
     ("z2", "z1", "x", "y", "c"),
-    ("z2", "x", "y", "z1", "c"),
-    ("z2", "z1", "y", "x", "c"),
+    ("y", "z2", "z1", "x", "c"),
 )
 AXES = ("z2", "z1", "c", "y", "x")
 STEPS = (
-    "Q0.0", "Q1.0", "S0.0", "Q1.1", "S1.0", "in", "S2.0", "S3.0", "Q0.1", "S0.1", "top",
-    "Q0.2", "Q1.2", "S2.1", "S1.1", "S0.2", "S3.1", "Q0.3", "Q1.3", "S1.2", "S2.2", "S3.2",
-    "S0.3", "S2.3", "S1.3", "S0.4", "S2.4", "S3.3", "S1.4", "S3.4",
+    "S0.0", "S3.0", "g0", "S2.0", "S1.0", "Q1.0", "g1", "tops", "S1.1", "Q0.0", "g2", "norm",
+    "S0.1", "S3.1", "Q0.1", "in", "S2.1", "norms", "S1.2", "S0.2", "Q1.1", "pack", "S2.2",
+    "S3.2", "Q1.2", "Q1.3", "Q0.2", "Q0.3", "S3.3", "S2.3", "S3.4", "S0.3", "S2.4", "S1.3",
+    "S0.4", "S1.4",
 )
 
 
 def gather_kernel(
     qkv_ref, square_ref, gains_ref, rows_ref, tops_ref, gu_ref, down_ref,
     wq_ref, w0_ref, w1_ref, w2_ref, w3_ref,
-    mine_ref, theirs_ref, tops_out, their_tops_ref, gains_out, first_ref, across_ref, turn_ref,
+    mine_ref, theirs_ref, tops_out, gains_out, first_ref, across_ref, turn_ref,
     *rest,
 ):
     *pack_refs, sum_ref, slot_ref, sends, receives, local_sems = rest
@@ -606,42 +606,58 @@
         return send(region(name, step), region(name, step), order[step])
 
     flying = {}
-    for name in chains:
-        flying[name] = begin(name, 0)
+    for event in STEPS:
+        if event.endswith(".0"):
+            flying[event[:2]] = begin(event[:2], 0)
     odd = here["c"] == 1
     turn_ref[...] = unravel(qkv_ref.shape[0])
     turn = turn_ref[...]
     mine_ref[...] = put_in_order(rows_ref[...], turn, odd).astype(BF)
-    swaps = {"in": send(mine_ref, theirs_ref, "x")}
-    tops_out[...] = put_in_order(tops_ref[...], turn, odd).astype(BF)
+    their_rows = send(mine_ref, theirs_ref, "x")
     sum_ref[...] = gains_ref[...]
-    for at, axis in enumerate(("c", "z1", "z2")):
-        copy = send(sum_ref, slot_ref.at[at], axis)
-        copy.wait()
-        sum_ref[...] += slot_ref[at]
-    gains_out[...] = put_in_order(sum_ref[...].astype(BF), turn, odd)
-    hidden = down_ref.shape[0]
+    gain_axes = ("c", "z1", "z2")
+    gain_copy = send(sum_ref, slot_ref.at[0], gain_axes[0])
+
+    for event in STEPS:
+        if event[0] == "g":
+            at = int(event[1])
+            gain_copy.wait()
+            sum_ref[...] += slot_ref[at]
+            if at < 2:
+                gain_copy = send(sum_ref, slot_ref.at[at + 1], gain_axes[at + 1])
+            else:
+                gains_out[...] = put_in_order(sum_ref[...].astype(BF), turn, odd)
+            continue
+        if event == "tops":
+            tops_out[...] = put_in_order(tops_ref[...], turn, odd).astype(BF)
+            continue
+        if event == "pack":
+            pack_parts(gu_ref, down_ref, pack_refs)
+            continue
+        if event == "norm":
+            first_norm(mine_ref, 0, gains_out, first_ref, across_ref)
+            continue
+        if event == "norms":
+            first_norm(theirs_ref, theirs_ref.shape[0], gains_out, first_ref, across_ref)
+            continue
+        if event == "in":
+            their_rows.wait()
+            continue
+        name, step = event.split(".")
+        flying[name].wait()
+        if int(step) + 1 < len(chains[name][4]):
+            flying[name] = begin(name, int(step) + 1)
+
+
+def pack_parts(gu_ref, down_ref, pack_refs):
+    hidden = down_ref.shape[1]
     tiles = hidden // len(pack_refs) // TILE
     for i, pack_ref in enumerate(pack_refs):
         for j in range(tiles):
             at, low = 3 * j * TILE, (i * tiles + j) * TILE
             pack_ref[:, at : at + TILE] = gu_ref[:, low : low + TILE]
             pack_ref[:, at + TILE : at + 2 * TILE] = gu_ref[:, hidden + low : hidden + low + TILE]
-            pack_ref[:, at + 2 * TILE : at + 3 * TILE] = jnp.transpose(
-                down_ref[low : low + TILE, :]
-            )
-
-    for event in STEPS:
-        if event in ("in", "top"):
-            swaps[event].wait()
-            if event == "in":
-                swaps["top"] = send(tops_out, their_tops_ref, "x")
-                first_norm(mine_ref, theirs_ref, gains_out, first_ref, across_ref)
-            continue
-        name, step = event.split(".")
-        flying[name].wait()
-        if int(step) + 1 < len(chains[name][4]):
-            flying[name] = begin(name, int(step) + 1)
+            pack_ref[:, at + 2 * TILE : at + 3 * TILE] = down_ref[:, low : low + TILE]
 
 
 def gather_first(qkv, square, gains, rows, tops, gate_up, down):
@@ -649,17 +665,17 @@
     shard = qkv.shape[0]
     wide = square.shape[1] // 4
     count, width = rows.shape
-    copies = 4 * 2 + 5 * 4 + 2 + 3
+    copies = 4 * 2 + 5 * 4 + 1 + 3
     return pl.pallas_call(
         gather_kernel,
         in_specs=[anywhere, anywhere] + [vmem] * 5,
-        out_specs=[anywhere] * 5 + [vmem] * (8 + CHUNKS),
+        out_specs=[anywhere] * 5 + [vmem] * (7 + CHUNKS),
         out_shape=[shaped((2, 2, 2, 2) + qkv.shape, BF)]
         + [shaped((2, 2, 2, 2, 2, shard, wide), BF)] * 4
-        + [shaped(rows.shape, BF)] * 4
+        + [shaped(rows.shape, BF)] * 3
         + [shaped(gains.shape, F32), shaped((2 * count, width), BF), shaped((width, 2 * count), BF)]
         + [shaped((4 * shard, 4 * shard), BF)]
-        + [shaped((shard, 3 * down.shape[0] // CHUNKS), BF)] * CHUNKS,
+        + [shaped((shard, 3 * down.shape[1] // CHUNKS), BF)] * CHUNKS,
         scratch_shapes=[
             pltpu.VMEM(gains.shape, F32),
             pltpu.VMEM((3,) + gains.shape, F32),
@@ -713,15 +729,15 @@
 
 def rot_tables(positions):
     quarter = HD // 4
-    inverse = 10000.0 ** (-jnp.arange(quarter).astype(F32) / quarter)
+    feature = jnp.arange(2 * HD) % HD
+    inverse = 10000.0 ** (-(feature % quarter).astype(F32) / quarter)
     angle_grid = positions.astype(F32)[:, None] * inverse[None, :]
     cosine, sine = jnp.cos(angle_grid), jnp.sin(angle_grid)
-    rest = jnp.zeros((positions.shape[0], 2 * quarter), F32)
-    none = jnp.zeros_like(sine)
+    first, second = (feature < quarter)[None], ((feature // quarter) == 1)[None]
     return (
-        jnp.concatenate([cosine, cosine, rest + 1.0] * 2, axis=1),
-        jnp.concatenate([none, sine, rest] * 2, axis=1),
-        jnp.concatenate([-sine, none, rest] * 2, axis=1),
+        jnp.where(first | second, cosine, 1.0),
+        jnp.where(second, sine, 0.0),
+        jnp.where(first, -sine, 0.0),
     )
 
 
@@ -898,8 +914,9 @@
 
 def ffn_kernel(
     tile, carried, place_ref, mine_ref, theirs_ref, fmine_ref, ftheirs_ref,
-    tmine_ref, ttheirs_ref, gmine_ref, gtheirs_ref, own_ref, other_ref, *rest,
+    tmine_ref, ttheirs_ref, gmine_ref, gtheirs_ref, *rest,
 ):
+    weight_refs, rest = rest[: len(rest) - 4 * carried - 8], rest[len(rest) - 4 * carried - 8 :]
     starts, rest = rest[: 4 * carried], rest[4 * carried :]
     ymine_ref, ytheirs_ref, dmine_ref, dtheirs_ref, gown_ref, gother_ref, y_ref, d_ref = rest
     rows, width = mine_ref.shape
@@ -918,8 +935,13 @@
             y_ref[...] = jnp.zeros_like(y_ref)
             d_ref[...] = jnp.zeros_like(d_ref)
 
-    own = own_ref[...].reshape(half, 3 * tile)
-    other = other_ref[...].reshape(half, 3 * tile)
+    if len(weight_refs) == 2:
+        own, other = (ref[...] for ref in weight_refs)
+    else:
+        nearer = pl.program_id(0) < pl.num_programs(0) // 2
+        own = jnp.where(nearer, weight_refs[0][...], weight_refs[1][...])
+        other = jnp.where(nearer, weight_refs[2][...], weight_refs[3][...])
+    own, other = own.reshape(half, 3 * tile), other.reshape(half, 3 * tile)
     hidden_parts, dgate_up_parts = [], []
     for part, (ref, top_ref) in enumerate(((mine_ref, tmine_ref), (theirs_ref, ttheirs_ref))):
         gate_up = dot(ref[:, :half], own[:, :both]) + dot(ref[:, half:], other[:, :both])
@@ -955,15 +977,20 @@
 
 def ffn(place, rows, flipped, tops, tops_flipped, weights, tile, starts=(), after=()):
     count, width = rows[0].shape
-    zs, _, groups, shard, wide = weights.shape
+    several = isinstance(weights, list)
+    zs, shard, wide = weights[0].shape if several else (weights.shape[:1] + weights.shape[3:])
     half = zs * shard
     tiles = wide // (3 * tile)
-    own_block = pl.BlockSpec(
-        (zs, 1, 1, shard, 3 * tile), lambda p, s: (0, s[0], p // tiles, 0, p % tiles)
-    )
-    other_block = pl.BlockSpec(
-        (zs, 1, 1, shard, 3 * tile), lambda p, s: (0, 1 - s[0], p // tiles, 0, p % tiles)
-    )
+    groups = 2
+    if several:
+        near = pl.BlockSpec((zs, shard, 3 * tile), lambda p, s: (0, 0, jnp.minimum(p, tiles - 1)))
+        far = pl.BlockSpec((zs, shard, 3 * tile), lambda p, s: (0, 0, jnp.maximum(p - tiles, 0)))
+        matrices = list(zip((near, far, near, far), weights))
+    else:
+        shape = (zs, 1, 1, shard, 3 * tile)
+        own = pl.BlockSpec(shape, lambda p, s: (0, s[0], p // tiles, 0, p % tiles))
+        other = pl.BlockSpec(shape, lambda p, s: (0, 1 - s[0], p // tiles, 0, p % tiles))
+        matrices = [(own, weights), (other, weights)]
     block = pl.BlockSpec((1, half, 3 * tile), lambda p, s: (p // tiles, 0, p % tiles))
     out = shaped((groups, half, wide), BF)
     once, fixed = whole((count, width)), whole((width, count))
@@ -972,7 +999,7 @@
         (groups * tiles,),
         [(once, a) for a in rows] + [(fixed, a) for a in flipped]
         + [(once, a) for a in tops] + [(fixed, a) for a in tops_flipped]
-        + [(own_block, weights), (other_block, weights)] + [(once, a) for a in starts],
+        + matrices + [(once, a) for a in starts],
         [(once, shaped((count, width), BF))] * 4 + [(block, out)] * 2,
         "feed_forward", 9 * groups * tiles,
         scratch=[pltpu.VMEM((2, count, width), F32)] * 2,
@@ -1281,7 +1308,7 @@
         + [(full, e2), (block, mixed), (own, square), (other, square)]
         + [(pair, a) for a in (mine, theirs) for pair in pairs],
         [(out, shaped(out_shape, BF))] * 4 + [(whole(cond.shape), shaped(cond.shape, F32))],
-        "middle_weights", 22,
+        "middle_weights", 5,
         scratch=[pltpu.VMEM((width, rows), BF)] * 3 + [pltpu.VMEM((cond.shape[1], slots), BF)],
         after=after,
         scalars=place,
@@ -1313,12 +1340,11 @@
     return [array.reshape(left) for array in results]
 
 
-def finish_ffn_kernel(weight_ref, gain_ref, *refs):
-    *sources, gu_ref, down_ref, norm_ref = refs
+def finish_ffn(weight_ref, sources, gu_ref, down_ref):
     chunks = len(sources) // 2
     tiles = sources[0].shape[1] // (3 * TILE)
     hidden = chunks * tiles * TILE
-    total = jnp.zeros((gain_ref.shape[0], 1), F32)
+    total = jnp.zeros((weight_ref.shape[0], 1), F32)
     for i in range(chunks):
         keep, got = sources[2 * i], sources[2 * i + 1]
         for j in range(tiles):
@@ -1330,32 +1356,31 @@
                 part = grads[:, kind * TILE : (kind + 1) * TILE]
                 gu_ref[:, cut] = part
                 total += jnp.sum(part * weight_ref[:, cut].astype(F32), axis=1, keepdims=True)
-            down_ref[target : target + TILE, :] = jnp.transpose(grads[:, 2 * TILE :])
-    norm_ref[...] = total / gain_ref[...]
-
-
-def finish_ffn(weight, gain, sources):
-    shard, wide = weight.shape
-    return call(
-        finish_ffn_kernel, (1,),
-        [(whole(weight.shape), weight), (whole(gain.shape), gain)]
-        + [(whole(a.shape), a) for a in sources],
-        [
-            (whole(weight.shape), shaped(weight.shape, F32)),
-            (whole((wide // 2, shard)), shaped((wide // 2, shard), F32)),
-            (whole(gain.shape), shaped(gain.shape, F32)),
-        ],
-        "finish_ffn", 5,
-    )
+            down_ref[:, target : target + TILE] = grads[:, 2 * TILE :]
+    return total
+
+
+SUM_CHAINS = {
+    "A": ("z1", "y", "z2"),
+    "B": ("x", "z2", "z1"),
+    "Q0": ("z2", "y", "z1"),
+    "Q1": ("y", "z1", "z2"),
+}
+SUM_STEPS = (
+    "Q0.0", "Q1.0", "out", "A.1", "B.1", "Q0.1", "Q1.1", "A.2", "Q0.2", "B.2", "in", "Q1.2",
+)
 
 
 def scatter_kernel(
-    queries, dx_ref, their_dx_ref, gain_ref, qkv_weight, query_weight, third_ref,
-    x2_ref, y_ref, y_got_ref, turn_ref, rows_ref, gains_ref, dx1_ref, *refs,
+    queries, their_dx_ref, *refs,
 ):
+    few = 12 + 2 * CHUNKS
+    sources, refs, fetched = refs[:few], refs[few : len(refs) - few], refs[len(refs) - few :]
+    dx_ref, gain_ref, qkv_weight, query_weight, ffn_weight, x2_ref, y_ref = fetched[:7]
+    y_got_ref, turn_ref, rows_ref, gains_ref, dx1_ref, *ffn_refs = fetched[7:]
     inputs, refs = refs[: 4 + 2 * queries], refs[4 + 2 * queries :]
-    outs, refs = refs[:8], refs[8:]
-    block_ref, dinput_ref, out_ref, cq_ref, ckv_ref, co_ref, qkv_ref, norm_ref = outs
+    outs, refs = refs[:10], refs[10:]
+    block_ref, dinput_ref, out_ref, cq_ref, ckv_ref, co_ref, qkv_ref, norm_ref = outs[:8]
     dx_slot, norm_slot, refs = refs[0], refs[1], refs[2:]
     works, slots, refs = refs[: 2 + queries], refs[2 + queries : 5 * (2 + queries)], refs[5 * (2 + queries) :]
     sends, receives, local_sems = refs
@@ -1394,7 +1419,6 @@
     def add(target, source):
         target[...] = (target[...].astype(F32) + source[...].astype(F32)).astype(BF)
 
-    dx_copy = send(their_dx_ref, dx_slot, "x")
     names = ["A", "B"] + ["Q%d" % i for i in range(queries)]
     work = dict(zip(names, works))
     slot = {name: slots[4 * i : 4 * i + 4] for i, name in enumerate(names)}
@@ -1408,56 +1432,56 @@
     for i, name in enumerate("AB"):
         flying[name] = [load(inputs[2 * i], work[name]), load(inputs[2 * i + 1], slot[name][0])]
 
-    def part(name, step):
-        ref, mine = work[name], here[first[name]]
-        if step == 0:
-            return ref.at[mine], ref.at[1 - mine]
-        if step == 1:
-            return ref.at[mine, :, here["z1"]], ref.at[mine, :, 1 - here["z1"]]
-        return ref.at[mine, here["z2"], here["z1"]], ref.at[mine, 1 - here["z2"], here["z1"]]
+    def part(name, step, goes):
+        index = [slice(None)] * 3
+        for at, axis in enumerate(SUM_CHAINS[name][: step + 1]):
+            place = {"z2": 1, "z1": 2}.get(axis, 0)
+            index[place] = 1 - here[axis] if goes and at == step else here[axis]
+        return work[name].at[tuple(index)]
 
     def advance(name, step):
         for copy in flying[name]:
             copy.wait()
-        keep = work[name] if step == 0 else part(name, step - 1)[0]
-        add(keep, slot[name][step])
-        axis = (first[name], "z1", "z2")[step]
-        flying[name] = [send(part(name, step)[1], slot[name][step + 1], axis)]
+        add(work[name] if step == 0 else part(name, step - 1, False), slot[name][step])
+        target = slot[name][step + 1]
+        flying[name] = [send(part(name, step, True), target, SUM_CHAINS[name][step])]
 
     def end(name):
         for copy in flying[name]:
             copy.wait()
-        return part(name, 2)[0][...].astype(F32) + slot[name][3][...].astype(F32)
+        return part(name, 2, False)[...].astype(F32) + slot[name][3][...].astype(F32)
 
     odd = here["c"] == 1
-    for name in ("A", "B") + tuple(names[2:]):
-        advance(name, 0)
-    total = x2_ref[...] + (y_ref[...].astype(F32) + y_got_ref[...].astype(F32))
-    block_ref[...] = put_back(total.astype(BF).astype(F32), turn_ref[...], odd, 1).astype(BF)
-    advance("A", 1)
-    dx_copy.wait()
-    normal, scale = normalize(rows_ref[...].astype(F32))
-    grads = dx_ref[...].astype(F32) + dx_slot[...].astype(F32)
-    total = dx1_ref[...] + normalize_back(grads, gains_ref[0:1, :], normal, scale)
-    dinput_ref[...] = put_back(total, turn_ref[...], odd, 2)
-    advance("A", 2)
-    advance(names[2], 1)
-    advance("B", 1)
-    for name in names[3:]:
-        advance(name, 1)
-    advance(names[2], 2)
-    advance("B", 2)
-    for name in names[3:]:
-        advance(name, 2)
+    fetches = [load(source, target) for source, target in zip(sources, fetched)]
+    advance("A", 0)
+    advance("B", 0)
+    dx_copy = send(their_dx_ref, dx_slot, "x")
+    for event in SUM_STEPS:
+        if event == "out":
+            for copy in fetches:
+                copy.wait()
+            total = x2_ref[...] + (y_ref[...].astype(F32) + y_got_ref[...].astype(F32))
+            total = total.astype(BF).astype(F32)
+            block_ref[...] = put_back(total, turn_ref[...], odd, 1).astype(BF)
+            third = finish_ffn(ffn_weight, ffn_refs, *outs[8:])
+        elif event == "in":
+            dx_copy.wait()
+            normal, scale = normalize(rows_ref[...].astype(F32))
+            grads = dx_ref[...].astype(F32) + dx_slot[...].astype(F32)
+            total = dx1_ref[...] + normalize_back(grads, gains_ref[0:1, :], normal, scale)
+            dinput_ref[...] = put_back(total, turn_ref[...], odd, 2)
+        else:
+            name, step = event.split(".")
+            advance(name, int(step))
 
     wide = cq_ref.shape[1]
     grads = end("A")
-    out_ref[...] = jnp.transpose(grads[:, :wide])
+    out_ref[...] = grads[:, :wide]
     cq_ref[...] = grads[:, wide:]
     second = jnp.sum(grads[:, wide:] * query_weight[...].astype(F32), axis=1, keepdims=True)
     grads = end("B")
     ckv_ref[...] = grads[:, :wide]
-    co_ref[...] = jnp.transpose(grads[:, wide:])
+    co_ref[...] = grads[:, wide:]
     total = jnp.zeros(second.shape, F32)
     j = 0
     for name in names[2:]:
@@ -1466,14 +1490,14 @@
             for kind in range(3):
                 cut = slice(kind * wide + j * 128, kind * wide + (j + 1) * 128)
                 piece = grads[:, at + kind * 128 : at + (kind + 1) * 128]
-                qkv_ref[:, cut] = piece
+                qkv_ref[kind, :, j * 128 : (j + 1) * 128] = piece
                 total += jnp.sum(piece * qkv_weight[:, cut].astype(F32), axis=1, keepdims=True)
             j += 1
     lane = iota(norm_ref.shape, 1)
     norm_ref[...] = jnp.where(
         lane == 0,
         total / gain_ref[:, 0:1],
-        jnp.where(lane == 1, second / gain_ref[:, 1:2], jnp.where(lane == 2, third_ref[...], 0.0)),
+        jnp.where(lane == 1, second / gain_ref[:, 1:2], jnp.where(lane == 2, third / gain_ref[:, 2:3], 0.0)),
     )
     for at, axis in enumerate(("y", "x")):
         send(norm_ref, norm_slot.at[at], axis).wait()
@@ -1481,24 +1505,24 @@
 
 
 def scatter_last(
-    dx, their_dx, gain_columns, qkv_weight, query_weight, third, x2, y, y_got, turn, rows, gains,
+    dx, their_dx, gain_columns, qkv_weight, query_weight, ffn_weight, ffn_sums, x2, y, y_got, turn, rows, gains,
     dx1, squares, queries,
 ):
     anywhere, vmem = pl.BlockSpec(memory_space=pl.ANY), pl.BlockSpec(memory_space=pltpu.VMEM)
     shard, wide = query_weight.shape
     shapes = [a.shape for a, _ in squares] + [a.shape for a, _ in queries]
     assert all(shape[:3] == (2, 2, 2) for shape in shapes)
-    few = [dx, their_dx, gain_columns, qkv_weight, query_weight, third, x2, y, y_got, turn, rows]
-    few += [gains, dx1]
+    few = [dx, gain_columns, qkv_weight, query_weight, ffn_weight, x2, y, y_got, turn, rows]
+    few += [gains, dx1, *ffn_sums]
     many = [a for pair in (*squares, *queries) for a in pair]
-    outs = [(x2.shape, BF), (x2.shape, F32), ((wide, shard), F32), ((shard, wide), F32)]
-    outs += [((shard, wide), F32), ((wide, shard), F32), ((shard, 3 * wide), F32)]
-    outs += [((shard, 128), F32)]
+    outs = [(x2.shape, BF), (x2.shape, F32), ((shard, wide), F32), ((shard, wide), F32)]
+    outs += [((shard, wide), F32), ((shard, wide), F32), ((3, shard, wide), F32)]
+    outs += [((shard, 128), F32), (ffn_weight.shape, F32), ((shard, ffn_weight.shape[1] // 2), F32)]
     slots = [pltpu.VMEM(shape[at:], BF) for shape in shapes for at in range(4)]
     copies = 1 + 2 + len(queries) * 4 + len(squares) * 3
     return pl.pallas_call(
         functools.partial(scatter_kernel, len(queries)),
-        in_specs=[vmem] * len(few) + [anywhere] * len(many),
+        in_specs=[anywhere] * (1 + len(few) + len(many)),
         out_specs=[vmem] * len(outs),
         out_shape=[shaped(*out) for out in outs],
         scratch_shapes=[pltpu.VMEM(rows.shape, BF), pltpu.VMEM((2, shard, 128), F32)]
@@ -1507,13 +1531,14 @@
         + [
             pltpu.SemaphoreType.DMA((copies,)),
             pltpu.SemaphoreType.DMA((copies,)),
-            pltpu.SemaphoreType.DMA((4 + len(queries),)),
-        ],
+            pltpu.SemaphoreType.DMA((4 + len(queries) + len(few),)),
+        ]
+        + [pltpu.VMEM(a.shape, a.dtype) for a in few],
         compiler_params=pltpu.CompilerParams(
-            vmem_limit_bytes=VMEM_BYTES, collective_id=1, has_side_effects=True
+            vmem_limit_bytes=63 << 20, collective_id=1, has_side_effects=True
         ),
         name="scatter_last",
-    )(*few, *many)
+    )(their_dx, *few, *many)
 
 
 def swap(array, axis, bit=1):
@@ -1557,13 +1582,55 @@
         z_bits.append(bit)
         bit //= 2
 
-    places = {"half": 0, "seq": 1}
-    steps = {"half": ("half", 1, 2), "seq": ("seq", 1, 1)}
+    qkv_pack = jnp.concatenate(
+        [
+            qkv_weight[:, :, j * 128 : (j + 1) * 128].reshape(shard, 384)
+            for j in range(pairs_here)
+        ],
+        axis=1,
+    )
+    square_pack = jnp.concatenate(
+        [
+            attn_out_weight.T,
+            cross_q_weight,
+            cross_kv_weight.transpose(1, 0, 2).reshape(shard, head_cols),
+            cross_out_weight.T,
+        ],
+        axis=1,
+    )
+    gains = jnp.stack([norm1_gain, norm2_gain, norm3_gain]).astype(F32)
+    gains = lax.dynamic_update_slice(jnp.zeros((8, width), F32), gains, (0, dp * shard))
+    places = {"half": 0, "seq": 1, "own": 1}
+    steps = {"half": ("half", 1, 2), "seq": ("seq", 1, 1), "own": ("seq", 1, 6)}
     for at, bit in enumerate(z_bits):
         name = "z%d" % bit
         places[name] = 2 + at
         steps[name] = ("dp", 2 * bit, 4 + at)
     far, near = "z%d" % z_bits[0], "z%d" % z_bits[-1]
+
+    gate_up_flat = gate_up_weight.reshape(shard, 2 * hidden_cols)
+    (
+        wq, w0, w1, w2, w3, mine_in, theirs_in, top_grads, gains, first_all, first_across, turn,
+        *packs,
+    ) = gather_first(
+        qkv_pack, square_pack, gains, block_in, out_cotangent, gate_up_flat, down_weight.T
+    )
+    wq = wq.reshape((z_size, 2, 2) + qkv_pack.shape)
+    squares = [w.reshape((z_size, 2, 2, 2, shard, head_cols)) for w in (w0, w1, w2, w3)]
+    place = jnp.stack([core, seq, side, cond_count[seq], z // 2, z % 2, 0 * z]).astype(jnp.int32)
+    their_top = swap(top_grads, "half")
+    ffn_weights = []
+    for pack in packs[:-1]:
+        gathered = lax.all_gather(pack, ("dp", "seq"))
+        ffn_weights.append(gathered.reshape((z_size, 2, 2) + pack.shape))
+
+    def over(array, name, after):
+        axis, bit, which = steps[name]
+        array = hold(array, after)
+        got, upper = swap(array, axis, bit), place[which] == 1
+        return jnp.stack([jnp.where(upper, got, array), jnp.where(upper, array, got)], axis=-3)
+
+    slab = over(packs[-1], far, (gains,))
 
     class Way:
         def __init__(self, own, other, wide, order):
@@ -1589,60 +1656,29 @@
             shape = self.here.shape[-2:]
             return [self.here.reshape(shape), self.got.reshape(shape)]
 
-    qkv_pack = jnp.concatenate(
-        [
-            qkv_weight[:, :, j * 128 : (j + 1) * 128].reshape(shard, 384)
-            for j in range(pairs_here)
-        ],
-        axis=1,
-    )
-    square_pack = jnp.concatenate(
-        [
-            attn_out_weight.T,
-            cross_q_weight,
-            cross_kv_weight.transpose(1, 0, 2).reshape(shard, head_cols),
-            cross_out_weight.T,
-        ],
-        axis=1,
-    )
-    gains = jnp.stack([norm1_gain, norm2_gain, norm3_gain]).astype(F32)
-    gains = lax.dynamic_update_slice(jnp.zeros((8, width), F32), gains, (0, dp * shard))
-    gate_up_flat = gate_up_weight.reshape(shard, 2 * hidden_cols)
-    (
-        wq, w0, w1, w2, w3, mine_in, theirs_in, top_grads, their_top, gains, first_all,
-        first_across, turn, *ffn_pack,
-    ) = gather_first(
-        qkv_pack, square_pack, gains, block_in, out_cotangent, gate_up_flat, down_weight
-    )
-    wq = wq.reshape((z_size, 2, 2) + qkv_pack.shape)
-    squares = [w.reshape((z_size, 2, 2, 2, shard, head_cols)) for w in (w0, w1, w2, w3)]
-    place = jnp.stack([core, seq, side, cond_count[seq], z // 2, z % 2]).astype(jnp.int32)
-    ffn_weights = []
-    for i in range(CHUNKS):
-        gathered = lax.all_gather(ffn_pack[i], ("dp", "seq"))
-        ffn_weights.append(gathered.reshape((z_size, 2, 2) + ffn_pack[i].shape))
-
     along = jnp.arange(rows)
     tables = rot_tables(jnp.concatenate([side * rows + along, (1 - side) * rows + along]))
     query, key, value, mine, theirs, lse = self_forward(place, first_all, wq, tables)
+    theirs = hold(theirs, (their_top,))
+    slab = over(slab, near, (lse,))
     mixed = swap(theirs, "half")
 
-    my_cond = cond_tokens[seq].reshape(cond_slots, z_size, 2, cond_shard)
+    my_cond = hold(cond_tokens[seq], (theirs,)).reshape(cond_slots, z_size, 2, cond_shard)
     swapped = jnp.where(core == 1, my_cond[:, :, ::-1], my_cond)
     my_cond = swapped.transpose(0, 2, 1, 3).reshape(cond_slots, cond_width)
     my_cond = jnp.pad(my_cond, ((0, SLOTS - cond_slots), (0, 0)))
-    (top_across,) = across(top_grads)
-    (their_top_across,) = across(their_top)
+    top_across, their_top_across = across(hold(top_grads, (theirs,)), their_top)
     cross_key, cross_value = cond_forward(place, my_cond, squares[2])
     x1, second, cross_query, cross_mixed, x2, third = middle_forward(
         place, mine_in, mine, mixed, gains, cross_key, cross_value, squares,
         (top_across, their_top_across),
     )
+    slab = slab.reshape((z_size,) + slab.shape[2:])
     their_third = swap(third, "half")
     (third_across,) = across(third)
     (their_third_across,) = across(their_third)
     ffn_weights[0] = hold(ffn_weights[0], (their_third_across, third_across))
-    sums, ways, after = (), [], ()
+    sums, ways, after = (), [], (slab,)
     for i in range(CHUNKS):
         *sums, gown, gother = ffn(
             place,
@@ -1655,16 +1691,21 @@
             sums,
             after,
         )
-        arrived = [way.got for way in ways]
-        if arrived:
+        if i == 0:
+            slab = hold(slab, (sums[2],))
+            far_slab = swap(slab, "seq")
+            slabs = [slab, far_slab]
+            ffn_weights.append(slabs + [swap(s, "dp", 1) for s in slabs])
+        else:
+            arrived = [far_slab if i == 1 else ways[0].got]
             gother = hold(gother, arrived)
-        ways.append(Way(gown, gother, False, ("seq", near, far)))
+        ways.append(Way(gown, gother, False, ("own" if i == CHUNKS - 1 else "seq", near, far)))
         if i < CHUNKS - 1:
-            after = tuple(way.step() for way in ways)
+            after = (ways[i].step(((far_slab, ways[0].got)[i],)),)
     ymine, ytheirs, dmine, dtheirs = sums
     d_received = swap(hold(dtheirs, arrived), "half")
 
-    after = [way.step() for way in ways]
+    after = [ways[0].step(), ways[2].step()]
     dx1, e2, dquery, dkey, dvalue, e1, dmine, dtheirs = middle_backward(
         place, dmine, d_received, top_grads, x2, x1, gains,
         cross_query, cross_key, cross_value, squares, after,
@@ -1676,12 +1717,11 @@
     )
     arrived = [way.got for way in ways] + [dtheirs]
     aother, bother = hold(aother, arrived), hold(bother, arrived)
-    dcond = hold(dcond, arrived)
     first_way = Way(aown, aother, True, ("half", "seq", near, far))
     second_way = Way(bown, bother, True, ("seq", "half", near, far))
     qkv_grads = []
     pairs = 2 * pairs_here
-    after = [dcond, y_received] + [way.step() for way in ways if way.order]
+    after = [aother] + [way.step() for way in ways if way.order]
     running = None
     for first, several in ((0, 2), (2, pairs - 2)):
         gown, gother, *sums = self_backward(
@@ -1692,22 +1732,21 @@
         qkv_grads.append((gown.reshape(full), gother.reshape(full)))
         running = sums[0]
         if first == 0:
-            arrived = [way.got for way in ways] + [first_way.got, second_way.got]
+            arrived = [way.got for way in ways] + [first_way.got, second_way.got, y_received]
             running = hold(running, arrived)
+            dcond = hold(dcond, (running,))
             after = [way.step(late=(running,)) for way in ways if way.order]
             after += [first_way.step(late=(running,)), second_way.step(late=(running,))]
     rmine, rtheirs = sums
     rtheirs = hold(rtheirs, (first_way.got, second_way.got, ways[-1].got))
     gain_columns = [g.astype(F32).reshape(shard, 1) for g in (norm1_gain, norm2_gain, norm3_gain)]
-    grad_gate_up, grad_down, gain_third = finish_ffn(
-        gate_up_flat, gain_columns[2], [array for way in ways for array in way.end()]
-    )
-    grad_gate_up = grad_gate_up.reshape(shard, 2, hidden_cols)
     (
         block_out, grad_input, grad_out, grad_cq, grad_ckv, grad_co, grad_qkv, gain_grads,
+        grad_gate_up, grad_down,
     ) = scatter_last(
-        rmine, rtheirs, jnp.concatenate(gain_columns[:2], axis=1),
-        qkv_weight.reshape(shard, 3 * head_cols), cross_q_weight, gain_third,
+        rmine, rtheirs, jnp.concatenate(gain_columns, axis=1),
+        qkv_weight.reshape(shard, 3 * head_cols), cross_q_weight,
+        gate_up_flat, [array for way in ways for array in way.end()],
         x2, ymine, y_received, turn, mine_in, gains, dx1,
         [
             tuple(a.reshape((2, 2, 2) + a.shape[-2:]) for a in (way.here, way.got))
@@ -1716,7 +1755,8 @@
         qkv_grads,
     )
     grad_ckv = grad_ckv.reshape(2, cond_shard, head_cols).transpose(1, 0, 2)
-    grad_qkv = grad_qkv.reshape(shard, 3, head_cols)
+    grad_qkv = grad_qkv.transpose(1, 0, 2)
+    grad_gate_up = grad_gate_up.reshape(shard, 2, hidden_cols)
 
     dcond = dcond[:cond_slots].reshape(cond_slots, 2, z_size, cond_shard)
     dcond = jnp.where(core == 1, dcond[:, ::-1], dcond).transpose(0, 2, 1, 3)
@@ -1740,12 +1780,12 @@
         gain_grads[1],
         gain_grads[2],
         grad_qkv,
-        grad_out,
+        grad_out.T,
         grad_cq,
         grad_ckv,
-        grad_co,
+        grad_co.T,
         grad_gate_up,
-        grad_down,
+        grad_down.T,
     )
 
 
@@ -1795,7 +1835,7 @@
 CHUNKS = 3
 FLOPS = 1.15e9
 TILE = 256
-SLOTS = 256
+SLOTS = 144
 
 
 def solution(mesh):

time: 967 us -> 898 us (0.929)
  Pallas kernels: 723 us -> 672 us
  waiting for transfers between devices: 145 us -> 126 us
  local copies, waits for them, and re-layouts: 54.9 us -> 40.7 us
  starting transfers between devices: 18.3 us -> 28.5 us
    ppermute x23 -> x29, waiting for transfers between devices: 144 us -> 120 us  [swap(): lax.ppermute(array, axis, [(i, i ^ bit) for i in range(lax.axis_size(axis...]
    pallas_call x1, Pallas kernels: 128 us -> 107 us  [scatter_last(): pl.pallas_call(functools.partial(scatter_kernel, len(queries)), in_specs=...]
    pallas_call x1, Pallas kernels: 182 us -> 163 us  [gather_first(): pl.pallas_call(gather_kernel, in_specs=[anywhere, anywhere] + [vmem] * 5,...]
    pallas_call x26 -> x24, Pallas kernels: 413 us -> 402 us  [call(): pl.pallas_call(without_after, **how, out_shape=[shape for _, shape in out...]
    ppermute x23 -> x29, starting transfers between devices: 17.9 us -> 28.2 us  [swap(): lax.ppermute(array, axis, [(i, i ^ bit) for i in range(lax.axis_size(axis...]
    unnamed x76 -> x84, local copies, waits for them, and re-layouts: 24.6 us -> 20.1 us
  transfers between devices with their start and end apart: 26 -> 31, of which waited for: 9 -> 11; matrix products, arithmetic and copies ran while one was open for 3% -> 2% of each run, Pallas kernels for 43% -> 45%
where the time goes in v3:
time: 898 us; the launch traced here: 892 us
  Pallas kernels  672 us (75%)
  waiting for transfers between devices  126 us (14%)
  local copies, waits for them, and re-layouts  40.7 us (5%)
  starting transfers between devices  28.5 us (3%)
  between operations  15 us (2%)
  other arithmetic  9.19 us (1%)
    pallas_call x24, Pallas kernels, call(): pl.pallas_call(without_after, **how, out_shape=[shape for _, shape in out...  402 us
    pallas_call x1, Pallas kernels, gather_first(): pl.pallas_call(gather_kernel, in_specs=[anywhere, anywhere] + [vmem] * 5,...  163 us
    ppermute x29, waiting for transfers between devices, swap(): lax.ppermute(array, axis, [(i, i ^ bit) for i in range(lax.axis_size(axis...  120 us
    pallas_call x1, Pallas kernels, scatter_last(): pl.pallas_call(functools.partial(scatter_kernel, len(queries)), in_specs=...  107 us
    ppermute x29, starting transfers between devices, swap(): lax.ppermute(array, axis, [(i, i ^ bit) for i in range(lax.axis_size(axis...  28.2 us
    unnamed x84, local copies, waits for them, and re-layouts  20.1 us
  transfers between devices with their start and end apart: 31, of which 11 were waited for; matrix products, arithmetic and copies ran while one was open for 2% of the time, Pallas kernels for 45%

profile of v3, /device:TPU:0, one launch (start us, length us, event | category | flops | bytes accessed | tf_op | source)
XLA Modules:
  0.0 891.7 jit_solution(6270104785411221858)
XLA Ops:
  9.3 1.1 slice_bitcast_fusion.2
  10.5 1.2 copy.152
  13.9 163.1 %gather_first.1 = (bf16[2,2,2,2,192,1152]{5,4,3,2,1,0:T(8,128)(2,1)}, bf16[2,2,2,2,2,192,384]{6,5,4,3,2,1,0:T(8,128)(2,1)}, bf16[2,2,2,2,2,192,384]{6,5,4,3,2,1,...) custom-call(bf16[192,1152]{1,0:T(8,128)(2,1)} %pad_maximum_fusion.3., ...), custom_call_target="tpu_custom_call" | custom-call | tf_op jit(solution)/shard_map/gather_first/pallas_call | solution.py:669
  177.3 1.6 collective-permute-start
  178.9 3.4 collective-permute-start.3
  183.0 3.3 fusion.2
  186.3 1.2 stack.62.refs_0_
  187.5 37.2 %self_forward.1 = (bf16[1024,768]{1,0:T(8,128)(2,1)}, bf16[1024,768]{1,0:T(8,128)(2,1)}, bf16[1024,768]{1,0:T(8,128)(2,1)}, bf16[512,768]{1,0:T(8,128)(2,1)}, bf...) custom-call(s32[7]{0:T(128)} %stack.62.refs_0_, bf16[1024,1536]{1,0:T(8,128)(2,1)} %get-tuple-element.113.refs_1_, ...), custom_call_target="tpu_custom_call" | custom-call | flops 48299999232 | tf_op jit(solution)/shard_map/self_forward/pallas_call | solution.py:439
  224.8 1.1 copy.165.refs_0_
  227.7 1.1 select_bitcast_fusion.3
  228.9 1.2 pad_maximum_fusion.1.refs_0_
  230.9 1.4 reshape.301
  233.4 5.3 cond_forward.1
  238.8 4.1 across.3
  242.8 6.8 collective-permute-done.1.refs_3_.refs_14_.refs_15_.refs_16_
  250.6 26.4 %middle_forward.1 = (f32[512,1536]{1,0:T(8,128)}, bf16[512,1536]{1,0:T(8,128)(2,1)}, bf16[512,1536]{1,0:T(8,128)(2,1)}, bf16[512,1536]{1,0:T(8,128)(2,1)}, f32[5...) custom-call(s32[7]{0:T(128)} %stack.62.refs_0_, bf16[512,1536]{1,0:T(8,128)(2,1)} %get-tuple-element.121.refs_1_.refs_9_, ...), custom_call_target="tpu_custom_call" | custom-call | flops 29899999232 | tf_op jit(solution)/shard_map/middle_forward/pallas_call | solution.py:439
  277.7 17.5 %collective-permute-done.4 = bf16[2,192,1536]{2,1,0:T(8,128)(2,1)S(1)} collective-permute-done((bf16[2,192,1536]{2,1,0:T(8,128)(2,1)}, bf16[2,192,1536]{2,1,0:T(8,128)(2,1)S(1)}, u32[]{:S(2)}, u32[]{:S(2)}) %collective-permute-start.4) | collective-permute-done | bytes 1179680 | tf_op jit(solution)/shard_map/ppermute | solution.py:1545
  295.6 1.6 copy.129
  297.2 3.0 across.4.refs_2_.refs_3_
  300.2 12.1 %collective-permute-done.2.refs_0_.refs_2_ = bf16[512,1536]{1,0:T(8,128)(2,1)} collective-permute-done((bf16[512,1536]{1,0:T(8,128)(2,1)}, bf16[512,1536]{1,0:T(8,128)(2,1)}, u32[]{:S(2)}, u32[]{:S(2)}) %collective-permute-start.2) | collective-permute-done | bytes 1572896 | tf_op jit(solution)/shard_map/ppermute | solution.py:1545
  312.4 3.0 across.5.refs_1_.refs_4_
  315.4 42.3 %feed_forward.3 = (bf16[512,1536]{1,0:T(8,128)(2,1)}, bf16[512,1536]{1,0:T(8,128)(2,1)}, bf16[512,1536]{1,0:T(8,128)(2,1)}, bf16[512,1536]{1,0:T(8,128)(2,1)}, b...) custom-call(s32[7]{0:T(128)} %stack.62.refs_0_, bf16[512,1536]{1,0:T(8,128)(2,1)} %get-tuple-element.131.refs_0_.refs_1_, ...), custom_call_target="tpu_custom_call" | custom-call | flops 41400000512 | tf_op jit(solution)/shard_map/feed_forward/pallas_call | solution.py:439
  357.8 1.6 collective-permute-start.5
  359.5 6.6 collective-permute-done.8
  366.1 7.1 fold.11
  373.2 6.6 all-gather.7.cloned.1.call-done
  379.8 43.7 %feed_forward.4 = (bf16[512,1536]{1,0:T(8,128)(2,1)}, bf16[512,1536]{1,0:T(8,128)(2,1)}, bf16[512,1536]{1,0:T(8,128)(2,1)}, bf16[512,1536]{1,0:T(8,128)(2,1)}, b...) custom-call(s32[7]{0:T(128)} %stack.62.refs_0_, bf16[512,1536]{1,0:T(8,128)(2,1)} %get-tuple-element.131.refs_0_.refs_1_, ...), custom_call_target="tpu_custom_call" | custom-call | flops 41400000512 | tf_op jit(solution)/shard_map/feed_forward/pallas_call | solution.py:439
  424.7 7.1 collective-permute-done.9
  431.8 7.0 fold.12
  438.8 44.7 %feed_forward.5 = (bf16[512,1536]{1,0:T(8,128)(2,1)}, bf16[512,1536]{1,0:T(8,128)(2,1)}, bf16[512,1536]{1,0:T(8,128)(2,1)}, bf16[512,1536]{1,0:T(8,128)(2,1)}, b...) custom-call(s32[7]{0:T(128)} %stack.62.refs_0_, bf16[512,1536]{1,0:T(8,128)(2,1)} %get-tuple-element.131.refs_0_.refs_1_, ...), custom_call_target="tpu_custom_call" | custom-call | flops 41400000512 | tf_op jit(solution)/shard_map/feed_forward/pallas_call | solution.py:439
  483.6 1.4 copy-done.2
  485.2 2.1 collective-permute-start.11
  487.4 4.3 fold.13
  491.6 2.3 collective-permute-start.14
  494.0 7.3 fold.14
  501.3 2.1 collective-permute-start.16
  503.4 19.1 %collective-permute-done.11.refs_2_ = bf16[512,1536]{1,0:T(8,128)(2,1)} collective-permute-done((bf16[512,1536]{1,0:T(8,128)(2,1)}, bf16[512,1536]{1,0:T(8,128)(2,1)}, u32[]{:S(2)}, u32[]{:S(2)}) %collective-permute-start.11) | collective-permute-done | bytes 1572896 | tf_op jit(solution)/shard_map/ppermute | solution.py:1545
  522.5 34.7 %middle_backward.1 = (f32[512,1536]{1,0:T(8,128)}, bf16[512,1536]{1,0:T(8,128)(2,1)}, bf16[512,1536]{1,0:T(8,128)(2,1)}, bf16[144,1536]{1,0:T(8,128)(2,1)}, bf16...) custom-call(s32[7]{0:T(128)} %stack.62.refs_0_, ...), custom_call_target="tpu_custom_call" | custom-call | flops 46000001024 | tf_op jit(solution)/shard_map/middle_backward/pallas_call | solution.py:439
  557.2 1.7 collective-permute-start.13
  559.0 21.6 %middle_weights.1 = (bf16[2,2,768,768]{3,2,1,0:T(8,128)(2,1)}, bf16[2,2,768,768]{3,2,1,0:T(8,128)(2,1)}, bf16[2,2,768,768]{3,2,1,0:T(8,128)(2,1)}, bf16[2,2,768,768]{3,2,1,0:T(8,128)(2,1)}, f32[144,768]{1,0:T(8,128)}) custom-call(s32[7]{0:T(128)} %stack.62.refs_0_, bf16[512,1536]{1,0:T(8,128)(2,1)} %get-tuple-element.163.refs_1_, ...), custom_call_target="tpu_custom_call" | custom-call | flops 5750000128 | tf_op jit(solution)/shard_map/middle_weights/pallas_call | solution.py:439
  580.6 17.0 %collective-permute-done.16.refs_3_ = bf16[1,1,2,2,192,1536]{5,4,3,2,1,0:T(8,128)(2,1)S(1)} collective-permute-done((bf16[1,1,2,2,192,1536]{5,4,3,2,1,0:T(8,128)(2,1)}, bf16[1,1,2,2,192,1536]{5,4,3,2,1,0:T(8,128)(2,1)S(1)}, u32[]{:S(2)}, u32[]{:S(2)}) %collective-permute-start.16) | collective-permute-done | bytes 2359328 | tf_op jit(solution)/shard_map/ppermute | solution.py:1545
  597.6 1.4 copy-done.3
  599.5 3.6 fold.15
  603.1 1.0 collective-permute-start.17
  605.8 4.2 fold.16
  610.0 1.7 collective-permute-start.18
  612.0 4.2 fold.17
  616.2 15.8 %collective-permute-done.17.refs_1_ = bf16[1,1,1,1,192,1536]{5,4,3,2,1,0:T(8,128)(2,1)S(1)} collective-permute-done((bf16[1,1,1,1,192,1536]{5,4,3,2,1,0:T(8,128)(2,1)}, bf16[1,1,1,1,192,1536]{5,4,3,2,1,0:T(8,128)(2,1)S(1)}, u32[]{:S(2)}, u32[]{:S(2)}) %collective-permute-start.17) | collective-permute-done | bytes 589856 | tf_op jit(solution)/shard_map/ppermute | solution.py:1545
  632.0 26.6 %self_backward.2 = (bf16[2,768,384]{2,1,0:T(8,128)(2,1)}, bf16[2,768,384]{2,1,0:T(8,128)(2,1)}, f32[1024,1536]{1,0:T(8,128)}) custom-call(s32[7]{0:T(128)} %stack.62.refs_0_, bf16[1024,768]{1,0:T(8,128)(2,1)} %get-tuple-element.115.refs_1_, bf16[1024,768]{1,0:T(8,128)(2,1)} %get-tuple-element.116.refs_2_, bf16[1024,768]{1,0:T(8,128)(2,1)} %get-tuple-element.117.refs_3_, ...), custom_call_target="tpu_custom_call" | custom-call | flops 29899999232 | tf_op jit(solution)/shard_map/self_backward/pallas_call | solution.py:439
  658.7 17.0 %collective-permute-done.19 = bf16[1,1,2,1,192,1536]{5,4,2,3,1,0:T(8,128)(2,1)S(1)} collective-permute-done((bf16[1,1,2,1,192,1536]{5,4,2,3,1,0:T(8,128)(2,1)}, bf16[1,1,2,1,192,1536]{5,4,2,3,1,0:T(8,128)(2,1)S(1)}, u32[]{:S(2)}, u32[]{:S(2)}) %collective-permute-start.19) | collective-permute-done | bytes 1179680 | tf_op jit(solution)/shard_map/ppermute | solution.py:1545
  678.4 1.9 rev.7
  681.8 8.6 fold.21
  690.8 8.6 fold.20
  699.3 1.3 collective-permute-start.23
  700.7 3.4 fold.19
  704.1 3.6 fold.18
  707.7 2.9 collective-permute-start.26
  711.6 1.8 collective-permute-start.28
  713.4 47.3 %self_backward.3 = (bf16[2,768,768]{2,1,0:T(8,128)(2,1)}, bf16[2,768,768]{2,1,0:T(8,128)(2,1)}, bf16[512,1536]{1,0:T(8,128)(2,1)}, bf16[512,1536]{1,0:T(8,128)(2,1)}) custom-call(s32[7]{0:T(128)} %stack.62.refs_0_, bf16[1024,768]{1,0:T(8,128)(2,1)} %get-tuple-element.115.refs_1_, bf16[1024,768]{1,0:T(8,128)(2,1)} %get-tuple-element.116.refs_2_, ...), custom_call_target="tpu_custom_call" | custom-call | flops 59799998464 | tf_op jit(solution)/shard_map/self_backward/pallas_call | solution.py:439
  763.2 106.9 %scatter_last.1 = (bf16[512,1536]{1,0:T(8,128)(2,1)}, f32[512,1536]{1,0:T(8,128)}, f32[192,384]{1,0:T(8,128)}, f32[192,384]{1,0:T(8,128)}, f32[192,384]{1,0:T(8,...) custom-call(bf16[512,1536]{1,0:T(8,128)(2,1)} %hold.42.their_dx_ref,, ...), custom_call_target="tpu_custom_call" | custom-call | tf_op jit(solution)/shard_map/scatter_last/pallas_call | solution.py:1523
  870.1 4.3 reshape.362
  876.3 1.1 copy.192
  877.4 1.3 copy-done.10
  878.7 1.7 copy.193
  (183 shorter events, 29.2 us)
Async XLA Ops:
  7.2 218.8 %copy-start = (bf16[2,130,768]{2,0,1:T(2,128)(2,1)S(1)}, bf16[2,130,768]{2,0,1:T(2,128)(2,1)}, u32[]{:S(2)}) copy-start(bf16[2,130,768]{2,0,1:T(2,128)(2,1)} %param.15) | copy-start | bytes 1198084
  7.2 3.3 copy-start.19
  7.2 308.2 %all-gather.5.cloned.1.call-start = ((), (), s32[]{:S(2)}) async-start(), calls=%async_computation | async-start | bytes 10027008 | tf_op jit(solution)/shard_map/all_gather | solution.py:1624
  9.3 2.4 copy-start.30
  10.5 2.6 copy-start.22
  10.5 2.6 copy-start.28
  10.5 2.5 copy-start.29
  12.3 1.7 copy-start.27
  177.0 5.4 copy-start.32
  177.1 202.7 %all-gather.7.cloned.1.call-start = ((), (), s32[]{:S(2)}) async-start(), calls=%async_computation.1 | async-start | bytes 10027008 | tf_op jit(solution)/shard_map/all_gather | solution.py:1624
  177.3 53.0 %collective-permute-start = (bf16[512,1536]{1,0:T(8,128)(2,1)}, bf16[512,1536]{1,0:T(8,128)(2,1)}, u32[]{:S(2)}, u32[]{:S(2)}) collective-permute-start(bf16[512,1536]{1,0:T(8,128)(2,1)} %get-tuple-element.120.refs_5_.refs_3_), channel_id=1, source_target_pairs={{0,1},{1,0},{2,3},{3,2},{4,5},{5,4},{6,7},{7,6},{8,9},{9,8},{10,11... | collective-permute-start | bytes 4718600 | tf_op jit(solution)/shard_map/ppermute | solution.py:1545
  178.9 48.9 %collective-permute-start.3 = (bf16[192,1536]{1,0:T(8,128)(2,1)}, bf16[192,1536]{1,0:T(8,128)(2,1)}, u32[]{:S(2)}, u32[]{:S(2)}) collective-permute-start(bf16[192,1536]{1,0:T(8,128)(2,1)} %hold.25), channel_id=1, source_target_pairs={{0,16},{4,20},{8,24},{12,28},{16,0},{20,4},{24,8},{28,12},{1,17},{... | collective-permute-start | bytes 1769480 | tf_op jit(solution)/shard_map/ppermute | solution.py:1545
  187.5 37.2 %copy-start.17 = (bf16[512,1536]{1,0:T(8,128)(2,1)S(1)}, bf16[512,1536]{1,0:T(8,128)(2,1)}, u32[]{:S(2)}) copy-start(bf16[512,1536]{1,0:T(8,128)(2,1)} %get-tuple-element.120.refs_5_.refs_3_) | copy-start | bytes 4718596
  224.8 2.9 copy-start.11
  230.0 65.2 %collective-permute-start.4 = (bf16[2,192,1536]{2,1,0:T(8,128)(2,1)}, bf16[2,192,1536]{2,1,0:T(8,128)(2,1)S(1)}, u32[]{:S(2)}, u32[]{:S(2)}) collective-permute-start(bf16[2,192,1536]{2,1,0:T(8,128)(2,1)} %hold.26), channel_id=1, source_target_pairs={{0,8},{4,12},{8,0},{12,4},{16,24},{20,28},{24,16},{28,20},{1,9},{5... | collective-permute-start | bytes 3538952 | tf_op jit(solution)/shard_map/ppermute | solution.py:1545
  230.3 19.4 %collective-permute-start.1 = (bf16[512,768]{1,0:T(8,128)(2,1)}, bf16[512,768]{1,0:T(8,128)(2,1)S(1)}, u32[]{:S(2)}, u32[]{:S(2)}) collective-permute-start(bf16[512,768]{1,0:T(8,128)(2,1)} %hold.22.refs_1_.refs_5_), channel_id=1, source_target_pairs={{0,1},{1,0},{2,3},{3,2},{4,5},{5,4},{6,7},{7,6},{8,9},{9,8},{10,11... | collective-permute-start | bytes 2359304 | tf_op jit(solution)/shard_map/ppermute | solution.py:1545
  250.6 44.7 %copy-start.7 = (bf16[2,192,1536]{2,1,0:T(8,128)(2,1)S(1)}, bf16[2,192,1536]{2,1,0:T(8,128)(2,1)}, u32[]{:S(2)}) copy-start(bf16[2,192,1536]{2,1,0:T(8,128)(2,1)} %hold.26) | copy-start | bytes 3538948
  276.9 35.5 %collective-permute-start.2 = (bf16[512,1536]{1,0:T(8,128)(2,1)}, bf16[512,1536]{1,0:T(8,128)(2,1)}, u32[]{:S(2)}, u32[]{:S(2)}) collective-permute-start(bf16[512,1536]{1,0:T(8,128)(2,1)} %get-tuple-element.131.refs_0_.refs_1_), channel_id=1, source_target_pairs={{0,1},{1,0},{2,3},{3,2},{4,5},{5,4},{6,7},{7,6},{8,9},{9,8},{10,11... | collective-permute-start | bytes 4718600 | tf_op jit(solution)/shard_map/ppermute | solution.py:1545
  357.8 8.3 collective-permute-start.8
  357.8 65.7 %collective-permute-start.5 = (bf16[4,192,1536]{2,1,0:T(8,128)(2,1)}, bf16[4,192,1536]{2,1,0:T(8,128)(2,1)}, u32[]{:S(2)}, u32[]{:S(2)}) collective-permute-start(bf16[4,192,1536]{2,1,0:T(8,128)(2,1)} %hold.28.refs_9_), channel_id=1, source_target_pairs={{0,2},{2,0},{1,3},{3,1},{4,6},{6,4},{5,7},{7,5},{8,10},{10,8},{9,1... | collective-permute-start | bytes 7077896 | tf_op jit(solution)/shard_map/ppermute | solution.py:1545
  423.5 8.3 collective-permute-start.9
  423.9 15.0 %collective-permute-start.6 = (bf16[4,192,1536]{2,1,0:T(8,128)(2,1)}, bf16[4,192,1536]{2,1,0:T(8,128)(2,1)}, u32[]{:S(2)}, u32[]{:S(2)}) collective-permute-start(bf16[4,192,1536]{2,1,0:T(8,128)(2,1)} %hold.28.refs_9_), channel_id=1, source_target_pairs={{0,4},{4,0},{8,12},{12,8},{16,20},{20,16},{24,28},{28,24},{1,5},{5... | collective-permute-start | bytes 7077896 | tf_op jit(solution)/shard_map/ppermute | solution.py:1545
  424.1 14.7 %collective-permute-start.7 = (bf16[4,192,1536]{2,1,0:T(8,128)(2,1)}, bf16[4,192,1536]{2,1,0:T(8,128)(2,1)}, u32[]{:S(2)}, u32[]{:S(2)}) collective-permute-start(bf16[4,192,1536]{2,1,0:T(8,128)(2,1)} %collective-permute-done.5.refs_1_.refs_10_), channel_id=1, source_target_pairs={{0,4},{4,0},{8,12},{12,8},{16,20},{20,16},{24,28},{28,24},{1,5},{5... | collective-permute-start | bytes 7077896 | tf_op jit(solution)/shard_map/ppermute | solution.py:1545
  424.4 59.2 %collective-permute-start.10 = (bf16[1,1,2,2,192,1536]{5,4,3,2,1,0:T(8,128)(2,1)}, bf16[1,1,2,2,192,1536]{5,4,3,2,1,0:T(8,128)(2,1)S(1)}, u32[]{:S(2)}, u32[]{:S(2)}) collective-permute-start(bf16[1,1,2,2,192,1536]{5,4,3,2,1,0:T(8,128)(2,1)} %hold.30), channel_id=1, source_target_pairs={{0,2},{2,0},{1,3},{3,1},{4,6},{6,4},{5,7},{7,5},{8,10},{10,8},{9,1... | collective-permute-start | bytes 7077896 | tf_op jit(solution)/shard_map/ppermute | solution.py:1545
  483.6 1.4 copy-start.2
  485.0 9.0 %collective-permute-start.12 = (bf16[2,768,1536]{2,1,0:T(8,128)(2,1)}, bf16[2,768,1536]{2,1,0:T(8,128)(2,1)}, u32[]{:S(2)}, u32[]{:S(2)}) collective-permute-start(bf16[2,768,1536]{2,1,0:T(8,128)(2,1)} %hold.32), channel_id=1, source_target_pairs={{0,4},{4,0},{8,12},{12,8},{16,20},{20,16},{24,28},{28,24},{1,5},{5... | collective-permute-start | bytes 14155784 | tf_op jit(solution)/shard_map/ppermute | solution.py:1545
  485.2 37.3 %collective-permute-start.11 = (bf16[512,1536]{1,0:T(8,128)(2,1)}, bf16[512,1536]{1,0:T(8,128)(2,1)}, u32[]{:S(2)}, u32[]{:S(2)}) collective-permute-start(bf16[512,1536]{1,0:T(8,128)(2,1)} %hold.31), channel_id=1, source_target_pairs={{0,1},{1,0},{2,3},{3,2},{4,5},{5,4},{6,7},{7,6},{8,9},{9,8},{10,11... | collective-permute-start | bytes 4718600 | tf_op jit(solution)/shard_map/ppermute | solution.py:1545
  491.6 88.9 %collective-permute-start.14 = (bf16[1,1,2,1,192,1536]{5,4,3,2,1,0:T(8,128)(2,1)}, bf16[1,1,2,1,192,1536]{5,4,3,2,1,0:T(8,128)(2,1)S(1)}, u32[]{:S(2)}, u32[]{:S(2)}) collective-permute-start(bf16[1,1,2,1,192,1536]{5,4,3,2,1,0:T(8,128)(2,1)} %bitcast.262), channel_id=1, source_target_pairs={{0,8},{4,12},{8,0},{12,4},{16,24},{20,28},{24,16},{28,20},{1,9},{5... | collective-permute-start | bytes 3538952 | tf_op jit(solution)/shard_map/ppermute | solution.py:1545
  494.0 86.6 %collective-permute-start.15 = (bf16[1,1,2,2,192,1536]{5,4,3,2,1,0:T(8,128)(2,1)}, bf16[1,1,2,2,192,1536]{5,4,3,2,1,0:T(8,128)(2,1)}, u32[]{:S(2)}, u32[]{:S(2)}) collective-permute-start(bf16[1,1,2,2,192,1536]{5,4,3,2,1,0:T(8,128)(2,1)} %hold.33), channel_id=1, source_target_pairs={{0,2},{2,0},{1,3},{3,1},{4,6},{6,4},{5,7},{7,5},{8,10},{10,8},{9,1... | collective-permute-start | bytes 7077896 | tf_op jit(solution)/shard_map/ppermute | solution.py:1545
  501.3 96.3 %collective-permute-start.16 = (bf16[1,1,2,2,192,1536]{5,4,3,2,1,0:T(8,128)(2,1)}, bf16[1,1,2,2,192,1536]{5,4,3,2,1,0:T(8,128)(2,1)S(1)}, u32[]{:S(2)}, u32[]{:S(2)}) collective-permute-start(bf16[1,1,2,2,192,1536]{5,4,3,2,1,0:T(8,128)(2,1)} %bitcast.261), channel_id=1, source_target_pairs={{0,2},{2,0},{1,3},{3,1},{4,6},{6,4},{5,7},{7,5},{8,10},{10,8},{9,1... | collective-permute-start | bytes 7077896 | tf_op jit(solution)/shard_map/ppermute | solution.py:1545
  557.2 23.3 %collective-permute-start.13 = (bf16[512,768]{1,0:T(8,128)(2,1)}, bf16[512,768]{1,0:T(8,128)(2,1)}, u32[]{:S(2)}, u32[]{:S(2)}) collective-permute-start(bf16[512,768]{1,0:T(8,128)(2,1)} %get-tuple-element.161), channel_id=1, source_target_pairs={{0,1},{1,0},{2,3},{3,2},{4,5},{5,4},{6,7},{7,6},{8,9},{9,8},{10,11... | collective-permute-start | bytes 2359304 | tf_op jit(solution)/shard_map/ppermute | solution.py:1545
  580.6 17.0 %copy-start.4 = (bf16[1,1,2,1,192,1536]{5,4,3,2,1,0:T(8,128)(2,1)}, bf16[1,1,2,1,192,1536]{5,4,3,2,1,0:T(8,128)(2,1)S(1)}, u32[]{:S(2)}) copy-start(bf16[1,1,2,1,192,1536]{5,4,3,2,1,0:T(8,128)(2,1)S(1)} %collective-permute-done.14.refs_1_) | copy-start | bytes 3538948
  597.6 1.4 copy-start.3
  599.0 76.7 %collective-permute-start.21 = (bf16[2,2,768,768]{3,2,1,0:T(8,128)(2,1)}, bf16[2,2,768,768]{3,2,1,0:T(8,128)(2,1)}, u32[]{:S(2)}, u32[]{:S(2)}) collective-permute-start(bf16[2,2,768,768]{3,2,1,0:T(8,128)(2,1)} %hold.35), channel_id=1, source_target_pairs={{0,4},{4,0},{8,12},{12,8},{16,20},{20,16},{24,28},{28,24},{1,5},{5... | collective-permute-start | bytes 14155784 | tf_op jit(solution)/shard_map/ppermute | solution.py:1545
  599.0 76.7 %collective-permute-start.20 = (bf16[2,2,768,768]{3,2,1,0:T(8,128)(2,1)}, bf16[2,2,768,768]{3,2,1,0:T(8,128)(2,1)}, u32[]{:S(2)}, u32[]{:S(2)}) collective-permute-start(bf16[2,2,768,768]{3,2,1,0:T(8,128)(2,1)} %hold.34.refs_15_), channel_id=1, source_target_pairs={{0,4},{4,0},{8,12},{12,8},{16,20},{20,16},{24,28},{28,24},{1,5},{5... | collective-permute-start | bytes 14155784 | tf_op jit(solution)/shard_map/ppermute | solution.py:1545
  599.5 4.7 copy-start.33
  599.5 4.7 copy-start.34
  599.5 4.7 copy-start.35
  599.5 4.7 copy-start.16
  603.1 28.9 %collective-permute-start.17 = (bf16[1,1,1,1,192,1536]{5,4,3,2,1,0:T(8,128)(2,1)}, bf16[1,1,1,1,192,1536]{5,4,3,2,1,0:T(8,128)(2,1)S(1)}, u32[]{:S(2)}, u32[]{:S(2)}) collective-permute-start(bf16[1,1,1,1,192,1536]{5,4,3,2,1,0:T(8,128)(2,1)} %bitcast.267), channel_id=1, source_target_pairs={{0,16},{4,20},{8,24},{12,28},{16,0},{20,4},{24,8},{28,12},{1,17},{... | collective-permute-start | bytes 1769480 | tf_op jit(solution)/shard_map/ppermute | solution.py:1545
  610.0 48.6 %collective-permute-start.18 = (bf16[1,1,2,1,192,1536]{5,4,2,3,1,0:T(8,128)(2,1)}, bf16[1,1,2,1,192,1536]{5,4,2,3,1,0:T(8,128)(2,1)S(1)}, u32[]{:S(2)}, u32[]{:S(2)}) collective-permute-start(bf16[1,1,2,1,192,1536]{5,4,2,3,1,0:T(8,128)(2,1)} %bitcast.263), channel_id=1, source_target_pairs={{0,8},{4,12},{8,0},{12,4},{16,24},{20,28},{24,16},{28,20},{1,9},{5... | collective-permute-start | bytes 3538952 | tf_op jit(solution)/shard_map/ppermute | solution.py:1545
  611.7 47.0 %collective-permute-start.22 = (bf16[512,1536]{1,0:T(8,128)(2,1)}, bf16[512,1536]{1,0:T(8,128)(2,1)}, u32[]{:S(2)}, u32[]{:S(2)}) collective-permute-start(bf16[512,1536]{1,0:T(8,128)(2,1)} %hold.36), channel_id=1, source_target_pairs={{0,1},{1,0},{2,3},{3,2},{4,5},{5,4},{6,7},{7,6},{8,9},{9,8},{10,11... | collective-permute-start | bytes 4718600 | tf_op jit(solution)/shard_map/ppermute | solution.py:1545
  632.0 26.6 %copy-start.12 = (bf16[1,1,1,1,192,1536]{5,4,3,2,1,0:T(8,128)(2,1)}, bf16[1,1,1,1,192,1536]{5,4,3,2,1,0:T(8,128)(2,1)S(1)}, u32[]{:S(2)}) copy-start(bf16[1,1,1,1,192,1536]{5,4,3,2,1,0:T(8,128)(2,1)S(1)} %collective-permute-done.17.refs_1_) | copy-start | bytes 1769476
  632.0 43.7 %collective-permute-start.19 = (bf16[1,1,2,1,192,1536]{5,4,2,3,1,0:T(8,128)(2,1)}, bf16[1,1,2,1,192,1536]{5,4,2,3,1,0:T(8,128)(2,1)S(1)}, u32[]{:S(2)}, u32[]{:S(2)}) collective-permute-start(bf16[1,1,2,1,192,1536]{5,4,2,3,1,0:T(8,128)(2,1)} %bitcast.264), channel_id=1, source_target_pairs={{0,8},{4,12},{8,0},{12,4},{16,24},{20,28},{24,16},{28,20},{1,9},{5... | collective-permute-start | bytes 3538952 | tf_op jit(solution)/shard_map/ppermute | solution.py:1545
  658.7 17.0 %copy-start.5 = (bf16[1,1,2,1,192,1536]{5,4,2,3,1,0:T(8,128)(2,1)}, bf16[1,1,2,1,192,1536]{5,4,2,3,1,0:T(8,128)(2,1)S(1)}, u32[]{:S(2)}) copy-start(bf16[1,1,2,1,192,1536]{5,4,2,3,1,0:T(8,128)(2,1)S(1)} %collective-permute-done.18) | copy-start | bytes 3538948
  675.7 1.0 copy-start.6
  681.1 29.5 %collective-permute-start.27 = (f32[130,2,192]{2,0,1:T(8,128)S(1)}, f32[130,2,192]{2,0,1:T(8,128)}, u32[]{:S(2)}, u32[]{:S(2)}) collective-permute-start(f32[130,2,192]{2,0,1:T(8,128)S(1)} %dynamic-slice_bitcast_fusion), channel_id=1, source_target_pairs={{0,1},{1,0},{2,3},{3,2},{4,5},{5,4},{6,7},{7,6},{8,9},{9,8},{10,11... | collective-permute-start | bytes 599048 | tf_op jit(solution)/shard_map/ppermute | solution.py:1545
  690.5 71.2 %collective-permute-start.24 = (bf16[2,1,2,2,192,768]{5,4,3,2,0,1:T(8,128)(2,1)}, bf16[2,1,2,2,192,768]{5,4,3,2,0,1:T(8,128)(2,1)S(1)}, u32[]{:S(2)}, u32[]{:S(2)}) collective-permute-start(bf16[2,1,2,2,192,768]{5,4,3,2,0,1:T(8,128)(2,1)} %bitcast.259), channel_id=1, source_target_pairs={{0,2},{2,0},{1,3},{3,1},{4,6},{6,4},{5,7},{7,5},{8,10},{10,8},{9,1... | collective-permute-start | bytes 7077896 | tf_op jit(solution)/shard_map/ppermute | solution.py:1545
  699.3 62.3 %collective-permute-start.23 = (bf16[1,2,2,2,192,768]{5,4,3,2,1,0:T(8,128)(2,1)}, bf16[1,2,2,2,192,768]{5,4,3,2,1,0:T(8,128)(2,1)}, u32[]{:S(2)}, u32[]{:S(2)}) collective-permute-start(bf16[1,2,2,2,192,768]{5,4,3,2,1,0:T(8,128)(2,1)} %bitcast.260), channel_id=1, source_target_pairs={{0,1},{1,0},{2,3},{3,2},{4,5},{5,4},{6,7},{7,6},{8,9},{9,8},{10,11... | collective-permute-start | bytes 7077896 | tf_op jit(solution)/shard_map/ppermute | solution.py:1545
  704.1 57.5 %collective-permute-start.25 = (bf16[1,1,1,1,192,1536]{5,4,3,2,1,0:T(8,128)(2,1)}, bf16[1,1,1,1,192,1536]{5,4,3,2,1,0:T(8,128)(2,1)S(1)}, u32[]{:S(2)}, u32[]{:S(2)}) collective-permute-start(bf16[1,1,1,1,192,1536]{5,4,3,2,1,0:T(8,128)(2,1)} %bitcast.266), channel_id=1, source_target_pairs={{0,16},{4,20},{8,24},{12,28},{16,0},{20,4},{24,8},{28,12},{1,17},{... | collective-permute-start | bytes 1769480 | tf_op jit(solution)/shard_map/ppermute | solution.py:1545
  704.1 6.5 copy-start.15
  707.7 55.6 %collective-permute-start.26 = (bf16[1,1,1,1,192,1536]{5,4,3,2,1,0:T(8,128)(2,1)}, bf16[1,1,1,1,192,1536]{5,4,3,2,1,0:T(8,128)(2,1)}, u32[]{:S(2)}, u32[]{:S(2)}) collective-permute-start(bf16[1,1,1,1,192,1536]{5,4,3,2,1,0:T(8,128)(2,1)} %bitcast.265), channel_id=1, source_target_pairs={{0,16},{4,20},{8,24},{12,28},{16,0},{20,4},{24,8},{28,12},{1,17},{... | collective-permute-start | bytes 1769480 | tf_op jit(solution)/shard_map/ppermute | solution.py:1545
  711.6 49.1 %collective-permute-start.28 = (f32[130,192]{1,0:T(8,128)S(1)}, f32[130,192]{1,0:T(8,128)S(1)}, u32[]{:S(2)}, u32[]{:S(2)}) collective-permute-start(f32[130,192]{1,0:T(8,128)S(1)} %dynamic-slice_bitcast_fusion.1), channel_id=1, source_target_pairs={{0,2},{2,0},{1,3},{3,1},{4,6},{6,4},{5,7},{7,5},{8,10},{10,8},{9,1... | collective-permute-start | bytes 299528 | tf_op jit(solution)/shard_map/ppermute | solution.py:1545
  761.6 1.6 copy-start.8
  870.1 4.4 copy-start.26
  870.1 5.3 copy-start.31
  870.1 6.2 copy-start.18
  876.3 2.5 copy-start.10
  878.7 1.8 copy-start.21
  878.7 2.7 copy-start.25
  880.5 1.6 copy-start.24
  880.5 2.4 copy-start.23
  880.5 3.1 copy-start.20
  882.2 2.5 copy-start.1
  (3 other events, 2.5 us)
Sparse Core Ops, SparseCore 0:
  177.2 116.7 all-gather.4
  296.2 83.5 all-gather.6

commit v4 on v3

--- a/solution.py
+++ b/solution.py
@@ -1699,23 +1699,24 @@
         else:
             arrived = [far_slab if i == 1 else ways[0].got]
             gother = hold(gother, arrived)
-        ways.append(Way(gown, gother, False, ("own" if i == CHUNKS - 1 else "seq", near, far)))
+        order = (near, "own", far) if i == CHUNKS - 1 else ("seq", near, far)
+        ways.append(Way(gown, gother, False, order))
         if i < CHUNKS - 1:
             after = (ways[i].step(((far_slab, ways[0].got)[i],)),)
     ymine, ytheirs, dmine, dtheirs = sums
     d_received = swap(hold(dtheirs, arrived), "half")
 
     after = [ways[0].step(), ways[2].step()]
+    y_received = swap(hold(ytheirs, (d_received, *after)), "half")
     dx1, e2, dquery, dkey, dvalue, e1, dmine, dtheirs = middle_backward(
         place, dmine, d_received, top_grads, x2, x1, gains,
         cross_query, cross_key, cross_value, squares, after,
     )
     dtheirs = swap(dtheirs, "half")
-    y_received = swap(hold(ytheirs, (dx1,)), "half")
     aown, aother, bown, bother, dcond = middle_weights(
         place, e1, mine, mixed, second, dquery, my_cond, dkey, dvalue, e2, cross_mixed, squares[2]
     )
-    arrived = [way.got for way in ways] + [dtheirs]
+    arrived = [way.got for way in ways] + [dtheirs, y_received]
     aother, bother = hold(aother, arrived), hold(bother, arrived)
     first_way = Way(aown, aother, True, ("half", "seq", near, far))
     second_way = Way(bown, bother, True, ("seq", "half", near, far))
@@ -1732,7 +1733,7 @@
         qkv_grads.append((gown.reshape(full), gother.reshape(full)))
         running = sums[0]
         if first == 0:
-            arrived = [way.got for way in ways] + [first_way.got, second_way.got, y_received]
+            arrived = [way.got for way in ways] + [first_way.got, second_way.got]
             running = hold(running, arrived)
             dcond = hold(dcond, (running,))
             after = [way.step(late=(running,)) for way in ways if way.order]

time: 898 us -> 861 us (0.959)
  waiting for transfers between devices: 126 us -> 87.5 us
    ppermute x29, waiting for transfers between devices: 120 us -> 80.6 us  [swap(): lax.ppermute(array, axis, [(i, i ^ bit) for i in range(lax.axis_size(axis...]
  transfers between devices with their start and end apart: 31 -> 31, of which waited for: 11 -> 9; matrix products, arithmetic and copies ran while one was open for 2% -> 2% of each run, Pallas kernels for 45% -> 47%
where the time goes in v4:
time: 861 us; the launch traced here: 854 us
  Pallas kernels  672 us (78%)
  waiting for transfers between devices  87.5 us (10%)
  local copies, waits for them, and re-layouts  41.4 us (5%)
  starting transfers between devices  29.4 us (3%)
  between operations  15 us (2%)
  other arithmetic  9.19 us (1%)
    pallas_call x24, Pallas kernels, call(): pl.pallas_call(without_after, **how, out_shape=[shape for _, shape in out...  401 us
    pallas_call x1, Pallas kernels, gather_first(): pl.pallas_call(gather_kernel, in_specs=[anywhere, anywhere] + [vmem] * 5,...  163 us
    pallas_call x1, Pallas kernels, scatter_last(): pl.pallas_call(functools.partial(scatter_kernel, len(queries)), in_specs=...  107 us
    ppermute x29, waiting for transfers between devices, swap(): lax.ppermute(array, axis, [(i, i ^ bit) for i in range(lax.axis_size(axis...  80.6 us
    ppermute x29, starting transfers between devices, swap(): lax.ppermute(array, axis, [(i, i ^ bit) for i in range(lax.axis_size(axis...  29.1 us
    unnamed x84, local copies, waits for them, and re-layouts  20.9 us
  transfers between devices with their start and end apart: 31, of which 9 were waited for; matrix products, arithmetic and copies ran while one was open for 2% of the time, Pallas kernels for 47%

profile of v4, /device:TPU:0, one launch (start us, length us, event | category | flops | bytes accessed | tf_op | source)
XLA Modules:
  0.0 854.1 jit_solution(882887892721886213)
XLA Ops:
  9.3 1.1 slice_bitcast_fusion.2
  10.5 1.2 copy.144
  13.9 163.1 %gather_first.1 = (bf16[2,2,2,2,192,1152]{5,4,3,2,1,0:T(8,128)(2,1)}, bf16[2,2,2,2,2,192,384]{6,5,4,3,2,1,0:T(8,128)(2,1)}, bf16[2,2,2,2,2,192,384]{6,5,4,3,2,1,...) custom-call(bf16[192,1152]{1,0:T(8,128)(2,1)} %pad_maximum_fusion.3., ...), custom_call_target="tpu_custom_call" | custom-call | tf_op jit(solution)/shard_map/gather_first/pallas_call | solution.py:669
  177.3 1.6 collective-permute-start
  178.9 3.4 collective-permute-start.3
  183.0 3.3 fusion.2
  186.3 1.2 stack.62.refs_0_
  187.5 37.2 %self_forward.1 = (bf16[1024,768]{1,0:T(8,128)(2,1)}, bf16[1024,768]{1,0:T(8,128)(2,1)}, bf16[1024,768]{1,0:T(8,128)(2,1)}, bf16[512,768]{1,0:T(8,128)(2,1)}, bf...) custom-call(s32[7]{0:T(128)} %stack.62.refs_0_, bf16[1024,1536]{1,0:T(8,128)(2,1)} %get-tuple-element.113.refs_1_, ...), custom_call_target="tpu_custom_call" | custom-call | flops 48299999232 | tf_op jit(solution)/shard_map/self_forward/pallas_call | solution.py:439
  224.8 1.1 copy.157.refs_0_
  227.7 1.1 select_bitcast_fusion.3
  228.9 1.2 pad_maximum_fusion.1.refs_0_
  230.9 1.4 reshape.301
  233.5 5.4 cond_forward.1
  238.8 4.0 across.3
  242.8 6.9 collective-permute-done.1.refs_3_.refs_14_.refs_15_.refs_16_
  250.6 26.4 %middle_forward.1 = (f32[512,1536]{1,0:T(8,128)}, bf16[512,1536]{1,0:T(8,128)(2,1)}, bf16[512,1536]{1,0:T(8,128)(2,1)}, bf16[512,1536]{1,0:T(8,128)(2,1)}, f32[5...) custom-call(s32[7]{0:T(128)} %stack.62.refs_0_, bf16[512,1536]{1,0:T(8,128)(2,1)} %get-tuple-element.121.refs_1_.refs_9_, ...), custom_call_target="tpu_custom_call" | custom-call | flops 29899999232 | tf_op jit(solution)/shard_map/middle_forward/pallas_call | solution.py:439
  277.7 17.5 %collective-permute-done.4 = bf16[2,192,1536]{2,1,0:T(8,128)(2,1)S(1)} collective-permute-done((bf16[2,192,1536]{2,1,0:T(8,128)(2,1)}, bf16[2,192,1536]{2,1,0:T(8,128)(2,1)S(1)}, u32[]{:S(2)}, u32[]{:S(2)}) %collective-permute-start.4) | collective-permute-done | bytes 1179680 | tf_op jit(solution)/shard_map/ppermute | solution.py:1545
  295.7 1.6 copy.123
  297.2 3.0 across.4.refs_2_.refs_3_
  300.2 12.1 %collective-permute-done.2.refs_0_.refs_2_ = bf16[512,1536]{1,0:T(8,128)(2,1)} collective-permute-done((bf16[512,1536]{1,0:T(8,128)(2,1)}, bf16[512,1536]{1,0:T(8,128)(2,1)}, u32[]{:S(2)}, u32[]{:S(2)}) %collective-permute-start.2) | collective-permute-done | bytes 1572896 | tf_op jit(solution)/shard_map/ppermute | solution.py:1545
  312.4 3.0 across.5.refs_1_.refs_4_
  315.4 42.3 %feed_forward.3 = (bf16[512,1536]{1,0:T(8,128)(2,1)}, bf16[512,1536]{1,0:T(8,128)(2,1)}, bf16[512,1536]{1,0:T(8,128)(2,1)}, bf16[512,1536]{1,0:T(8,128)(2,1)}, b...) custom-call(s32[7]{0:T(128)} %stack.62.refs_0_, bf16[512,1536]{1,0:T(8,128)(2,1)} %get-tuple-element.131.refs_0_.refs_1_, ...), custom_call_target="tpu_custom_call" | custom-call | flops 41400000512 | tf_op jit(solution)/shard_map/feed_forward/pallas_call | solution.py:439
  357.8 1.6 collective-permute-start.5
  359.4 6.6 collective-permute-done.8
  366.0 7.0 fold.11
  373.0 6.9 all-gather.7.cloned.1.call-done
  379.9 43.7 %feed_forward.4 = (bf16[512,1536]{1,0:T(8,128)(2,1)}, bf16[512,1536]{1,0:T(8,128)(2,1)}, bf16[512,1536]{1,0:T(8,128)(2,1)}, bf16[512,1536]{1,0:T(8,128)(2,1)}, b...) custom-call(s32[7]{0:T(128)} %stack.62.refs_0_, bf16[512,1536]{1,0:T(8,128)(2,1)} %get-tuple-element.131.refs_0_.refs_1_, ...), custom_call_target="tpu_custom_call" | custom-call | flops 41400000512 | tf_op jit(solution)/shard_map/feed_forward/pallas_call | solution.py:439
  424.6 7.3 collective-permute-done.9
  431.9 7.0 fold.12
  438.9 44.5 %feed_forward.5 = (bf16[512,1536]{1,0:T(8,128)(2,1)}, bf16[512,1536]{1,0:T(8,128)(2,1)}, bf16[512,1536]{1,0:T(8,128)(2,1)}, bf16[512,1536]{1,0:T(8,128)(2,1)}, b...) custom-call(s32[7]{0:T(128)} %stack.62.refs_0_, bf16[512,1536]{1,0:T(8,128)(2,1)} %get-tuple-element.131.refs_0_.refs_1_, ...), custom_call_target="tpu_custom_call" | custom-call | flops 41400000512 | tf_op jit(solution)/shard_map/feed_forward/pallas_call | solution.py:439
  483.5 1.4 copy-done.2
  485.2 2.1 collective-permute-start.11
  487.3 4.3 fold.13
  491.6 2.3 collective-permute-start.14
  493.9 7.3 fold.14
  501.2 21.2 %collective-permute-done.11.refs_2_.refs_1_ = bf16[512,1536]{1,0:T(8,128)(2,1)} collective-permute-done((bf16[512,1536]{1,0:T(8,128)(2,1)}, bf16[512,1536]{1,0:T(8,128)(2,1)}, u32[]{:S(2)}, u32[]{:S(2)}) %collective-permute-start.11) | collective-permute-done | bytes 1572896 | tf_op jit(solution)/shard_map/ppermute | solution.py:1545
  522.4 1.7 collective-permute-start.17
  524.1 2.3 collective-permute-start.16
  526.5 34.7 %middle_backward.1 = (f32[512,1536]{1,0:T(8,128)}, bf16[512,1536]{1,0:T(8,128)(2,1)}, bf16[512,1536]{1,0:T(8,128)(2,1)}, bf16[144,1536]{1,0:T(8,128)(2,1)}, bf16...) custom-call(s32[7]{0:T(128)} %stack.62.refs_0_, ...), custom_call_target="tpu_custom_call" | custom-call | flops 46000001024 | tf_op jit(solution)/shard_map/middle_backward/pallas_call | solution.py:439
  561.4 21.5 %middle_weights.1 = (bf16[2,2,768,768]{3,2,1,0:T(8,128)(2,1)}, bf16[2,2,768,768]{3,2,1,0:T(8,128)(2,1)}, bf16[2,2,768,768]{3,2,1,0:T(8,128)(2,1)}, bf16[2,2,768,768]{3,2,1,0:T(8,128)(2,1)}, f32[144,768]{1,0:T(8,128)}) custom-call(s32[7]{0:T(128)} %stack.62.refs_0_, bf16[512,1536]{1,0:T(8,128)(2,1)} %get-tuple-element.163.refs_1_, ...), custom_call_target="tpu_custom_call" | custom-call | flops 5750000128 | tf_op jit(solution)/shard_map/middle_weights/pallas_call | solution.py:439
  587.5 3.4 fold.15
  591.6 4.2 fold.16
  595.8 2.0 collective-permute-start.19
  597.8 4.2 fold.17
  602.0 26.6 %self_backward.2 = (bf16[2,768,384]{2,1,0:T(8,128)(2,1)}, bf16[2,768,384]{2,1,0:T(8,128)(2,1)}, f32[1024,1536]{1,0:T(8,128)}) custom-call(s32[7]{0:T(128)} %stack.62.refs_0_, bf16[1024,768]{1,0:T(8,128)(2,1)} %get-tuple-element.115.refs_1_, bf16[1024,768]{1,0:T(8,128)(2,1)} %get-tuple-element.116.refs_2_, bf16[1024,768]{1,0:T(8,128)(2,1)} %get-tuple-element.117.refs_3_, ...), custom_call_target="tpu_custom_call" | custom-call | flops 29899999232 | tf_op jit(solution)/shard_map/self_backward/pallas_call | solution.py:439
  628.7 8.2 collective-permute-done.19
  637.0 1.0 copy-done.5
  638.4 1.0 slice.32
  640.1 1.9 rev.7
  642.7 1.8 collective-permute-start.27
  644.6 8.6 %fold.21 = (bf16[2,1,4,192,768]{4,3,2,1,0:T(8,128)(2,1)}, bf16[2,1,4,192,768]{4,3,2,1,0:T(8,128)(2,1)}) custom-call(s32[7]{0:T(128)} %stack.62.refs_0_, bf16[2,2,4,192,768]{4,3,2,1,0:T(8,128)(2,1)} %bitcast.156, bf16[2,2,4,192,768]{4,3,2,1,0:T(8,128)(2,1)} %bitcast.71.refs_2_.refs_4_, bf16[2,2,4,192,768]{4,3,2,1,0:T(8,128)(2,1)} %bitcast.157, ...), custom_call_target="tpu_custom_call" | custom-call | flops 3527147520 | tf_op jit(solution)/shard_map/fold/pallas_call | solution.py:439
  653.1 8.6 %fold.20 = (bf16[1,1,8,192,768]{4,3,2,1,0:T(8,128)(2,1)}, bf16[1,1,8,192,768]{4,3,2,1,0:T(8,128)(2,1)}) custom-call(s32[7]{0:T(128)} %stack.62.refs_0_, bf16[1,2,8,192,768]{4,3,2,1,0:T(8,128)(2,1)} %bitcast.153, bf16[1,2,8,192,768]{4,3,2,1,0:T(8,128)(2,1)} %bitcast.67.refs_2_.refs_4_, bf16[1,2,8,192,768]{4,3,2,1,0:T(8,128)(2,1)} %bitcast.154, ...), custom_call_target="tpu_custom_call" | custom-call | flops 3527147520 | tf_op jit(solution)/shard_map/fold/pallas_call | solution.py:439
  662.4 3.4 fold.19
  665.8 3.6 fold.18
  669.4 2.9 collective-permute-start.26
  672.3 1.0 bitcast_add_fusion
  673.3 2.1 collective-permute-start.28
  675.4 47.3 %self_backward.3 = (bf16[2,768,768]{2,1,0:T(8,128)(2,1)}, bf16[2,768,768]{2,1,0:T(8,128)(2,1)}, bf16[512,1536]{1,0:T(8,128)(2,1)}, bf16[512,1536]{1,0:T(8,128)(2,1)}) custom-call(s32[7]{0:T(128)} %stack.62.refs_0_, bf16[1024,768]{1,0:T(8,128)(2,1)} %get-tuple-element.115.refs_1_, bf16[1024,768]{1,0:T(8,128)(2,1)} %get-tuple-element.116.refs_2_, ...), custom_call_target="tpu_custom_call" | custom-call | flops 59799998464 | tf_op jit(solution)/shard_map/self_backward/pallas_call | solution.py:439
  725.2 107.3 %scatter_last.1 = (bf16[512,1536]{1,0:T(8,128)(2,1)}, f32[512,1536]{1,0:T(8,128)}, f32[192,384]{1,0:T(8,128)}, f32[192,384]{1,0:T(8,128)}, f32[192,384]{1,0:T(8,...) custom-call(bf16[512,1536]{1,0:T(8,128)(2,1)} %hold.42.their_dx_ref,, ...), custom_call_target="tpu_custom_call" | custom-call | tf_op jit(solution)/shard_map/scatter_last/pallas_call | solution.py:1523
  832.6 4.3 reshape.362
  838.7 1.1 copy.184
  839.9 1.3 copy-done.10
  841.2 1.7 copy.185
  846.0 1.0 copy.190
  (183 shorter events, 27.9 us)
Async XLA Ops:
  7.2 218.8 %copy-start = (bf16[2,130,768]{2,0,1:T(2,128)(2,1)S(1)}, bf16[2,130,768]{2,0,1:T(2,128)(2,1)}, u32[]{:S(2)}) copy-start(bf16[2,130,768]{2,0,1:T(2,128)(2,1)} %param.15) | copy-start | bytes 1198084
  7.2 3.3 copy-start.19
  7.2 308.2 %all-gather.5.cloned.1.call-start = ((), (), s32[]{:S(2)}) async-start(), calls=%async_computation | async-start | bytes 10027008 | tf_op jit(solution)/shard_map/all_gather | solution.py:1624
  9.3 2.4 copy-start.30
  10.5 2.6 copy-start.22
  10.5 2.6 copy-start.28
  10.5 2.5 copy-start.29
  12.3 1.7 copy-start.27
  177.0 5.4 copy-start.32
  177.1 202.8 %all-gather.7.cloned.1.call-start = ((), (), s32[]{:S(2)}) async-start(), calls=%async_computation.1 | async-start | bytes 10027008 | tf_op jit(solution)/shard_map/all_gather | solution.py:1624
  177.3 53.0 %collective-permute-start = (bf16[512,1536]{1,0:T(8,128)(2,1)}, bf16[512,1536]{1,0:T(8,128)(2,1)}, u32[]{:S(2)}, u32[]{:S(2)}) collective-permute-start(bf16[512,1536]{1,0:T(8,128)(2,1)} %get-tuple-element.120.refs_5_.refs_3_), channel_id=1, source_target_pairs={{0,1},{1,0},{2,3},{3,2},{4,5},{5,4},{6,7},{7,6},{8,9},{9,8},{10,11... | collective-permute-start | bytes 4718600 | tf_op jit(solution)/shard_map/ppermute | solution.py:1545
  178.9 48.9 %collective-permute-start.3 = (bf16[192,1536]{1,0:T(8,128)(2,1)}, bf16[192,1536]{1,0:T(8,128)(2,1)}, u32[]{:S(2)}, u32[]{:S(2)}) collective-permute-start(bf16[192,1536]{1,0:T(8,128)(2,1)} %hold.25), channel_id=1, source_target_pairs={{0,16},{4,20},{8,24},{12,28},{16,0},{20,4},{24,8},{28,12},{1,17},{... | collective-permute-start | bytes 1769480 | tf_op jit(solution)/shard_map/ppermute | solution.py:1545
  187.5 37.3 %copy-start.17 = (bf16[512,1536]{1,0:T(8,128)(2,1)S(1)}, bf16[512,1536]{1,0:T(8,128)(2,1)}, u32[]{:S(2)}) copy-start(bf16[512,1536]{1,0:T(8,128)(2,1)} %get-tuple-element.120.refs_5_.refs_3_) | copy-start | bytes 4718596
  224.8 2.9 copy-start.11
  230.0 65.2 %collective-permute-start.4 = (bf16[2,192,1536]{2,1,0:T(8,128)(2,1)}, bf16[2,192,1536]{2,1,0:T(8,128)(2,1)S(1)}, u32[]{:S(2)}, u32[]{:S(2)}) collective-permute-start(bf16[2,192,1536]{2,1,0:T(8,128)(2,1)} %hold.26), channel_id=1, source_target_pairs={{0,8},{4,12},{8,0},{12,4},{16,24},{20,28},{24,16},{28,20},{1,9},{5... | collective-permute-start | bytes 3538952 | tf_op jit(solution)/shard_map/ppermute | solution.py:1545
  230.3 19.4 %collective-permute-start.1 = (bf16[512,768]{1,0:T(8,128)(2,1)}, bf16[512,768]{1,0:T(8,128)(2,1)S(1)}, u32[]{:S(2)}, u32[]{:S(2)}) collective-permute-start(bf16[512,768]{1,0:T(8,128)(2,1)} %hold.22.refs_1_.refs_5_), channel_id=1, source_target_pairs={{0,1},{1,0},{2,3},{3,2},{4,5},{5,4},{6,7},{7,6},{8,9},{9,8},{10,11... | collective-permute-start | bytes 2359304 | tf_op jit(solution)/shard_map/ppermute | solution.py:1545
  249.7 0.9 copy-start.9
  250.6 44.7 %copy-start.7 = (bf16[2,192,1536]{2,1,0:T(8,128)(2,1)S(1)}, bf16[2,192,1536]{2,1,0:T(8,128)(2,1)}, u32[]{:S(2)}) copy-start(bf16[2,192,1536]{2,1,0:T(8,128)(2,1)} %hold.26) | copy-start | bytes 3538948
  276.9 35.5 %collective-permute-start.2 = (bf16[512,1536]{1,0:T(8,128)(2,1)}, bf16[512,1536]{1,0:T(8,128)(2,1)}, u32[]{:S(2)}, u32[]{:S(2)}) collective-permute-start(bf16[512,1536]{1,0:T(8,128)(2,1)} %get-tuple-element.131.refs_0_.refs_1_), channel_id=1, source_target_pairs={{0,1},{1,0},{2,3},{3,2},{4,5},{5,4},{6,7},{7,6},{8,9},{9,8},{10,11... | collective-permute-start | bytes 4718600 | tf_op jit(solution)/shard_map/ppermute | solution.py:1545
  357.7 8.3 collective-permute-start.8
  357.8 65.8 %collective-permute-start.5 = (bf16[4,192,1536]{2,1,0:T(8,128)(2,1)}, bf16[4,192,1536]{2,1,0:T(8,128)(2,1)}, u32[]{:S(2)}, u32[]{:S(2)}) collective-permute-start(bf16[4,192,1536]{2,1,0:T(8,128)(2,1)} %hold.28.refs_9_), channel_id=1, source_target_pairs={{0,2},{2,0},{1,3},{3,1},{4,6},{6,4},{5,7},{7,5},{8,10},{10,8},{9,1... | collective-permute-start | bytes 7077896 | tf_op jit(solution)/shard_map/ppermute | solution.py:1545
  423.6 8.3 collective-permute-start.9
  423.9 15.0 %collective-permute-start.6 = (bf16[4,192,1536]{2,1,0:T(8,128)(2,1)}, bf16[4,192,1536]{2,1,0:T(8,128)(2,1)}, u32[]{:S(2)}, u32[]{:S(2)}) collective-permute-start(bf16[4,192,1536]{2,1,0:T(8,128)(2,1)} %hold.28.refs_9_), channel_id=1, source_target_pairs={{0,4},{4,0},{8,12},{12,8},{16,20},{20,16},{24,28},{28,24},{1,5},{5... | collective-permute-start | bytes 7077896 | tf_op jit(solution)/shard_map/ppermute | solution.py:1545
  424.2 14.7 %collective-permute-start.7 = (bf16[4,192,1536]{2,1,0:T(8,128)(2,1)}, bf16[4,192,1536]{2,1,0:T(8,128)(2,1)}, u32[]{:S(2)}, u32[]{:S(2)}) collective-permute-start(bf16[4,192,1536]{2,1,0:T(8,128)(2,1)} %collective-permute-done.5.refs_1_.refs_10_), channel_id=1, source_target_pairs={{0,4},{4,0},{8,12},{12,8},{16,20},{20,16},{24,28},{28,24},{1,5},{5... | collective-permute-start | bytes 7077896 | tf_op jit(solution)/shard_map/ppermute | solution.py:1545
  424.5 59.0 %collective-permute-start.10 = (bf16[1,1,2,2,192,1536]{5,4,3,2,1,0:T(8,128)(2,1)}, bf16[1,1,2,2,192,1536]{5,4,3,2,1,0:T(8,128)(2,1)S(1)}, u32[]{:S(2)}, u32[]{:S(2)}) collective-permute-start(bf16[1,1,2,2,192,1536]{5,4,3,2,1,0:T(8,128)(2,1)} %hold.30), channel_id=1, source_target_pairs={{0,2},{2,0},{1,3},{3,1},{4,6},{6,4},{5,7},{7,5},{8,10},{10,8},{9,1... | collective-permute-start | bytes 7077896 | tf_op jit(solution)/shard_map/ppermute | solution.py:1545
  483.5 1.4 copy-start.2
  484.9 9.0 %collective-permute-start.12 = (bf16[2,768,1536]{2,1,0:T(8,128)(2,1)}, bf16[2,768,1536]{2,1,0:T(8,128)(2,1)}, u32[]{:S(2)}, u32[]{:S(2)}) collective-permute-start(bf16[2,768,1536]{2,1,0:T(8,128)(2,1)} %hold.32), channel_id=1, source_target_pairs={{0,4},{4,0},{8,12},{12,8},{16,20},{20,16},{24,28},{28,24},{1,5},{5... | collective-permute-start | bytes 14155784 | tf_op jit(solution)/shard_map/ppermute | solution.py:1545
  485.2 37.2 %collective-permute-start.11 = (bf16[512,1536]{1,0:T(8,128)(2,1)}, bf16[512,1536]{1,0:T(8,128)(2,1)}, u32[]{:S(2)}, u32[]{:S(2)}) collective-permute-start(bf16[512,1536]{1,0:T(8,128)(2,1)} %hold.31), channel_id=1, source_target_pairs={{0,1},{1,0},{2,3},{3,2},{4,5},{5,4},{6,7},{7,6},{8,9},{9,8},{10,11... | collective-permute-start | bytes 4718600 | tf_op jit(solution)/shard_map/ppermute | solution.py:1545
  491.6 91.4 %collective-permute-start.14 = (bf16[1,1,2,1,192,1536]{5,4,3,2,1,0:T(8,128)(2,1)}, bf16[1,1,2,1,192,1536]{5,4,3,2,1,0:T(8,128)(2,1)S(1)}, u32[]{:S(2)}, u32[]{:S(2)}) collective-permute-start(bf16[1,1,2,1,192,1536]{5,4,3,2,1,0:T(8,128)(2,1)} %bitcast.262), channel_id=1, source_target_pairs={{0,8},{4,12},{8,0},{12,4},{16,24},{20,28},{24,16},{28,20},{1,9},{5... | collective-permute-start | bytes 3538952 | tf_op jit(solution)/shard_map/ppermute | solution.py:1545
  493.9 89.1 %collective-permute-start.15 = (bf16[1,1,2,2,192,1536]{5,4,3,2,1,0:T(8,128)(2,1)}, bf16[1,1,2,2,192,1536]{5,4,3,2,1,0:T(8,128)(2,1)S(1)}, u32[]{:S(2)}, u32[]{:S(2)}) collective-permute-start(bf16[1,1,2,2,192,1536]{5,4,3,2,1,0:T(8,128)(2,1)} %hold.33), channel_id=1, source_target_pairs={{0,2},{2,0},{1,3},{3,1},{4,6},{6,4},{5,7},{7,5},{8,10},{10,8},{9,1... | collective-permute-start | bytes 7077896 | tf_op jit(solution)/shard_map/ppermute | solution.py:1545
  522.4 60.6 %collective-permute-start.17 = (bf16[512,1536]{1,0:T(8,128)(2,1)}, bf16[512,1536]{1,0:T(8,128)(2,1)}, u32[]{:S(2)}, u32[]{:S(2)}) collective-permute-start(bf16[512,1536]{1,0:T(8,128)(2,1)} %hold.34), channel_id=1, source_target_pairs={{0,1},{1,0},{2,3},{3,2},{4,5},{5,4},{6,7},{7,6},{8,9},{9,8},{10,11... | collective-permute-start | bytes 4718600 | tf_op jit(solution)/shard_map/ppermute | solution.py:1545
  524.1 58.9 %collective-permute-start.16 = (bf16[1,2,2,1,192,1536]{5,4,3,2,1,0:T(8,128)(2,1)}, bf16[1,2,2,1,192,1536]{5,4,3,2,1,0:T(8,128)(2,1)}, u32[]{:S(2)}, u32[]{:S(2)}) collective-permute-start(bf16[1,2,2,1,192,1536]{5,4,3,2,1,0:T(8,128)(2,1)} %bitcast.261), channel_id=1, source_target_pairs={{0,8},{4,12},{8,0},{12,4},{16,24},{20,28},{24,16},{28,20},{1,9},{5... | collective-permute-start | bytes 7077896 | tf_op jit(solution)/shard_map/ppermute | solution.py:1545
  561.1 21.9 %collective-permute-start.13 = (bf16[512,768]{1,0:T(8,128)(2,1)}, bf16[512,768]{1,0:T(8,128)(2,1)}, u32[]{:S(2)}, u32[]{:S(2)}) collective-permute-start(bf16[512,768]{1,0:T(8,128)(2,1)} %get-tuple-element.161), channel_id=1, source_target_pairs={{0,1},{1,0},{2,3},{3,2},{4,5},{5,4},{6,7},{7,6},{8,9},{9,8},{10,11... | collective-permute-start | bytes 2359304 | tf_op jit(solution)/shard_map/ppermute | solution.py:1545
  583.0 1.0 copy-start.4
  583.0 1.8 copy-start.3
  584.8 52.1 %collective-permute-start.22 = (bf16[2,2,768,768]{3,2,1,0:T(8,128)(2,1)}, bf16[2,2,768,768]{3,2,1,0:T(8,128)(2,1)}, u32[]{:S(2)}, u32[]{:S(2)}) collective-permute-start(bf16[2,2,768,768]{3,2,1,0:T(8,128)(2,1)} %hold.36), channel_id=1, source_target_pairs={{0,4},{4,0},{8,12},{12,8},{16,20},{20,16},{24,28},{28,24},{1,5},{5... | collective-permute-start | bytes 14155784 | tf_op jit(solution)/shard_map/ppermute | solution.py:1545
  584.8 1.0 copy-start.16
  584.8 52.1 %collective-permute-start.21 = (bf16[2,2,768,768]{3,2,1,0:T(8,128)(2,1)}, bf16[2,2,768,768]{3,2,1,0:T(8,128)(2,1)}, u32[]{:S(2)}, u32[]{:S(2)}) collective-permute-start(bf16[2,2,768,768]{3,2,1,0:T(8,128)(2,1)} %hold.35.refs_15_), channel_id=1, source_target_pairs={{0,4},{4,0},{8,12},{12,8},{16,20},{20,16},{24,28},{28,24},{1,5},{5... | collective-permute-start | bytes 14155784 | tf_op jit(solution)/shard_map/ppermute | solution.py:1545
  590.9 37.8 %collective-permute-start.18 = (bf16[1,1,1,1,192,1536]{5,4,3,2,1,0:T(8,128)(2,1)}, bf16[1,1,1,1,192,1536]{5,4,3,2,1,0:T(8,128)(2,1)S(1)}, u32[]{:S(2)}, u32[]{:S(2)}) collective-permute-start(bf16[1,1,1,1,192,1536]{5,4,3,2,1,0:T(8,128)(2,1)} %bitcast.267), channel_id=1, source_target_pairs={{0,16},{4,20},{8,24},{12,28},{16,0},{20,4},{24,8},{28,12},{1,17},{... | collective-permute-start | bytes 1769480 | tf_op jit(solution)/shard_map/ppermute | solution.py:1545
  595.8 41.1 %collective-permute-start.19 = (bf16[1,1,2,1,192,1536]{5,4,2,3,1,0:T(8,128)(2,1)}, bf16[1,1,2,1,192,1536]{5,4,2,3,1,0:T(8,128)(2,1)S(1)}, u32[]{:S(2)}, u32[]{:S(2)}) collective-permute-start(bf16[1,1,2,1,192,1536]{5,4,2,3,1,0:T(8,128)(2,1)} %bitcast.263), channel_id=1, source_target_pairs={{0,8},{4,12},{8,0},{12,4},{16,24},{20,28},{24,16},{28,20},{1,9},{5... | collective-permute-start | bytes 3538952 | tf_op jit(solution)/shard_map/ppermute | solution.py:1545
  602.0 34.9 %collective-permute-start.20 = (bf16[1,1,2,1,192,1536]{5,4,2,3,1,0:T(8,128)(2,1)}, bf16[1,1,2,1,192,1536]{5,4,2,3,1,0:T(8,128)(2,1)S(1)}, u32[]{:S(2)}, u32[]{:S(2)}) collective-permute-start(bf16[1,1,2,1,192,1536]{5,4,2,3,1,0:T(8,128)(2,1)} %bitcast.264), channel_id=1, source_target_pairs={{0,2},{2,0},{1,3},{3,1},{4,6},{6,4},{5,7},{7,5},{8,10},{10,8},{9,1... | collective-permute-start | bytes 3538952 | tf_op jit(solution)/shard_map/ppermute | solution.py:1545
  628.7 8.2 copy-start.12
  636.9 1.0 copy-start.5
  636.9 1.5 copy-start.6
  642.7 1.9 copy-start.14
  642.7 29.5 %collective-permute-start.27 = (f32[130,2,192]{2,0,1:T(8,128)S(1)}, f32[130,2,192]{2,0,1:T(8,128)}, u32[]{:S(2)}, u32[]{:S(2)}) collective-permute-start(f32[130,2,192]{2,0,1:T(8,128)S(1)} %dynamic-slice_bitcast_fusion), channel_id=1, source_target_pairs={{0,1},{1,0},{2,3},{3,2},{4,5},{5,4},{6,7},{7,6},{8,9},{9,8},{10,11... | collective-permute-start | bytes 599048 | tf_op jit(solution)/shard_map/ppermute | solution.py:1545
  653.1 70.5 %collective-permute-start.24 = (bf16[2,1,2,2,192,768]{5,4,3,2,0,1:T(8,128)(2,1)}, bf16[2,1,2,2,192,768]{5,4,3,2,0,1:T(8,128)(2,1)S(1)}, u32[]{:S(2)}, u32[]{:S(2)}) collective-permute-start(bf16[2,1,2,2,192,768]{5,4,3,2,0,1:T(8,128)(2,1)} %bitcast.259), channel_id=1, source_target_pairs={{0,2},{2,0},{1,3},{3,1},{4,6},{6,4},{5,7},{7,5},{8,10},{10,8},{9,1... | collective-permute-start | bytes 7077896 | tf_op jit(solution)/shard_map/ppermute | solution.py:1545
  661.7 61.9 %collective-permute-start.23 = (bf16[1,2,2,2,192,768]{5,4,3,2,1,0:T(8,128)(2,1)}, bf16[1,2,2,2,192,768]{5,4,3,2,1,0:T(8,128)(2,1)}, u32[]{:S(2)}, u32[]{:S(2)}) collective-permute-start(bf16[1,2,2,2,192,768]{5,4,3,2,1,0:T(8,128)(2,1)} %bitcast.260), channel_id=1, source_target_pairs={{0,1},{1,0},{2,3},{3,2},{4,5},{5,4},{6,7},{7,6},{8,9},{9,8},{10,11... | collective-permute-start | bytes 7077896 | tf_op jit(solution)/shard_map/ppermute | solution.py:1545
  665.8 57.8 %collective-permute-start.25 = (bf16[1,1,1,1,192,1536]{5,4,3,2,1,0:T(8,128)(2,1)}, bf16[1,1,1,1,192,1536]{5,4,3,2,1,0:T(8,128)(2,1)S(1)}, u32[]{:S(2)}, u32[]{:S(2)}) collective-permute-start(bf16[1,1,1,1,192,1536]{5,4,3,2,1,0:T(8,128)(2,1)} %bitcast.266), channel_id=1, source_target_pairs={{0,16},{4,20},{8,24},{12,28},{16,0},{20,4},{24,8},{28,12},{1,17},{... | collective-permute-start | bytes 1769480 | tf_op jit(solution)/shard_map/ppermute | solution.py:1545
  665.8 6.5 copy-start.15
  669.4 55.8 %collective-permute-start.26 = (bf16[1,1,1,1,192,1536]{5,4,3,2,1,0:T(8,128)(2,1)}, bf16[1,1,1,1,192,1536]{5,4,3,2,1,0:T(8,128)(2,1)}, u32[]{:S(2)}, u32[]{:S(2)}) collective-permute-start(bf16[1,1,1,1,192,1536]{5,4,3,2,1,0:T(8,128)(2,1)} %bitcast.265), channel_id=1, source_target_pairs={{0,16},{4,20},{8,24},{12,28},{16,0},{20,4},{24,8},{28,12},{1,17},{... | collective-permute-start | bytes 1769480 | tf_op jit(solution)/shard_map/ppermute | solution.py:1545
  673.3 49.3 %collective-permute-start.28 = (f32[130,192]{1,0:T(8,128)S(1)}, f32[130,192]{1,0:T(8,128)S(1)}, u32[]{:S(2)}, u32[]{:S(2)}) collective-permute-start(f32[130,192]{1,0:T(8,128)S(1)} %dynamic-slice_bitcast_fusion.1), channel_id=1, source_target_pairs={{0,2},{2,0},{1,3},{3,1},{4,6},{6,4},{5,7},{7,5},{8,10},{10,8},{9,1... | collective-permute-start | bytes 299528 | tf_op jit(solution)/shard_map/ppermute | solution.py:1545
  723.6 0.8 copy-start.13
  723.6 1.6 copy-start.8
  832.5 4.4 copy-start.26
  832.5 5.3 copy-start.31
  832.5 6.2 copy-start.18
  838.7 2.5 copy-start.10
  841.2 1.8 copy-start.21
  841.2 2.7 copy-start.25
  843.0 1.6 copy-start.24
  843.0 2.4 copy-start.23
  843.0 3.1 copy-start.20
  844.6 2.5 copy-start.1
  (3 other events, 2.0 us)
Sparse Core Ops, SparseCore 0:
  177.2 116.7 all-gather.4
  296.3 83.5 all-gather.6

commit v5 on v4

--- a/solution.py
+++ b/solution.py
@@ -1324,14 +1324,15 @@
     shape = here.shape
     before, after = math.prod(shape[:at]), math.prod(shape[at + 1 : -2])
     view = (before, 2, after) + shape[-2:]
-    block = (1, 1, 1) + shape[-2:]
+    group = 2 if after % 2 == 0 else 1
+    block = (1, 1, group) + shape[-2:]
     keep = pl.BlockSpec(block, lambda a, b, s: (a, s[bit], b, 0, 0))
     send = pl.BlockSpec(block, lambda a, b, s: (a, 1 - s[bit], b, 0, 0))
     out = pl.BlockSpec(block, lambda a, b, s: (a, 0, b, 0, 0))
     out_shape = shaped((before, 1, after) + shape[-2:], BF)
     here, got = here.reshape(view), got.reshape(view)
     results = call(
-        fold_kernel, (before, after),
+        fold_kernel, (before, after // group),
         [(keep, here), (keep, got), (send, here), (send, got)],
         [(out, out_shape)] * 2,
         "fold", here.size * 1.3e-6, scalars=place,

time: 861 us -> 857 us (level)
  transfers between devices with their start and end apart: 31 -> 31, of which waited for: 9 -> 10; matrix products, arithmetic and copies ran while one was open for 2% -> 2% of each run, Pallas kernels for 47% -> 47%
where the time goes in v5:
time: 857 us; the launch traced here: 851 us
  Pallas kernels  668 us (78%)
  waiting for transfers between devices  88.2 us (10%)
  local copies, waits for them, and re-layouts  41.4 us (5%)
  starting transfers between devices  29.4 us (3%)
  between operations  15 us (2%)
  other arithmetic  9.19 us (1%)
    pallas_call x24, Pallas kernels, call(): pl.pallas_call(without_after, **how, out_shape=[shape for _, shape in out...  397 us
    pallas_call x1, Pallas kernels, gather_first(): pl.pallas_call(gather_kernel, in_specs=[anywhere, anywhere] + [vmem] * 5,...  163 us
    pallas_call x1, Pallas kernels, scatter_last(): pl.pallas_call(functools.partial(scatter_kernel, len(queries)), in_specs=...  107 us
    ppermute x29, waiting for transfers between devices, swap(): lax.ppermute(array, axis, [(i, i ^ bit) for i in range(lax.axis_size(axis...  80.5 us
    ppermute x29, starting transfers between devices, swap(): lax.ppermute(array, axis, [(i, i ^ bit) for i in range(lax.axis_size(axis...  29.1 us
    unnamed x84, local copies, waits for them, and re-layouts  20.9 us
  transfers between devices with their start and end apart: 31, of which 10 were waited for; matrix products, arithmetic and copies ran while one was open for 2% of the time, Pallas kernels for 47%

profile of v5, /device:TPU:0, one launch (start us, length us, event | category | flops | bytes accessed | tf_op | source)
XLA Modules:
  0.0 850.7 jit_solution(15576070021584530083)
XLA Ops:
  9.3 1.1 slice_bitcast_fusion.2
  10.5 1.2 copy.144
  13.9 163.1 %gather_first.1 = (bf16[2,2,2,2,192,1152]{5,4,3,2,1,0:T(8,128)(2,1)}, bf16[2,2,2,2,2,192,384]{6,5,4,3,2,1,0:T(8,128)(2,1)}, bf16[2,2,2,2,2,192,384]{6,5,4,3,2,1,...) custom-call(bf16[192,1152]{1,0:T(8,128)(2,1)} %pad_maximum_fusion.3., ...), custom_call_target="tpu_custom_call" | custom-call | tf_op jit(solution)/shard_map/gather_first/pallas_call | solution.py:669
  177.3 1.6 collective-permute-start
  178.9 3.4 collective-permute-start.3
  183.0 3.3 fusion.2
  186.3 1.2 stack.62.refs_0_
  187.5 37.2 %self_forward.1 = (bf16[1024,768]{1,0:T(8,128)(2,1)}, bf16[1024,768]{1,0:T(8,128)(2,1)}, bf16[1024,768]{1,0:T(8,128)(2,1)}, bf16[512,768]{1,0:T(8,128)(2,1)}, bf...) custom-call(s32[7]{0:T(128)} %stack.62.refs_0_, bf16[1024,1536]{1,0:T(8,128)(2,1)} %get-tuple-element.113.refs_1_, ...), custom_call_target="tpu_custom_call" | custom-call | flops 48299999232 | tf_op jit(solution)/shard_map/self_forward/pallas_call | solution.py:439
  224.8 1.1 copy.157.refs_0_
  227.7 1.1 select_bitcast_fusion.3
  228.9 1.2 pad_maximum_fusion.1.refs_0_
  230.9 1.4 reshape.301
  233.5 5.4 cond_forward.1
  238.8 4.0 across.3
  242.8 6.9 collective-permute-done.1.refs_3_.refs_14_.refs_15_.refs_16_
  250.6 26.4 %middle_forward.1 = (f32[512,1536]{1,0:T(8,128)}, bf16[512,1536]{1,0:T(8,128)(2,1)}, bf16[512,1536]{1,0:T(8,128)(2,1)}, bf16[512,1536]{1,0:T(8,128)(2,1)}, f32[5...) custom-call(s32[7]{0:T(128)} %stack.62.refs_0_, bf16[512,1536]{1,0:T(8,128)(2,1)} %get-tuple-element.121.refs_1_.refs_9_, ...), custom_call_target="tpu_custom_call" | custom-call | flops 29899999232 | tf_op jit(solution)/shard_map/middle_forward/pallas_call | solution.py:439
  277.7 17.5 %collective-permute-done.4 = bf16[2,192,1536]{2,1,0:T(8,128)(2,1)S(1)} collective-permute-done((bf16[2,192,1536]{2,1,0:T(8,128)(2,1)}, bf16[2,192,1536]{2,1,0:T(8,128)(2,1)S(1)}, u32[]{:S(2)}, u32[]{:S(2)}) %collective-permute-start.4) | collective-permute-done | bytes 1179680 | tf_op jit(solution)/shard_map/ppermute | solution.py:1546
  295.7 1.6 copy.123
  297.2 3.0 across.4.refs_2_.refs_3_
  300.2 12.1 %collective-permute-done.2.refs_0_.refs_2_ = bf16[512,1536]{1,0:T(8,128)(2,1)} collective-permute-done((bf16[512,1536]{1,0:T(8,128)(2,1)}, bf16[512,1536]{1,0:T(8,128)(2,1)}, u32[]{:S(2)}, u32[]{:S(2)}) %collective-permute-start.2) | collective-permute-done | bytes 1572896 | tf_op jit(solution)/shard_map/ppermute | solution.py:1546
  312.4 3.0 across.5.refs_1_.refs_4_
  315.4 42.3 %feed_forward.3 = (bf16[512,1536]{1,0:T(8,128)(2,1)}, bf16[512,1536]{1,0:T(8,128)(2,1)}, bf16[512,1536]{1,0:T(8,128)(2,1)}, bf16[512,1536]{1,0:T(8,128)(2,1)}, b...) custom-call(s32[7]{0:T(128)} %stack.62.refs_0_, bf16[512,1536]{1,0:T(8,128)(2,1)} %get-tuple-element.131.refs_0_.refs_1_, ...), custom_call_target="tpu_custom_call" | custom-call | flops 41400000512 | tf_op jit(solution)/shard_map/feed_forward/pallas_call | solution.py:439
  357.8 1.6 collective-permute-start.5
  359.4 6.6 collective-permute-done.8
  366.0 6.3 fold.11
  372.3 7.6 all-gather.7.cloned.1.call-done
  379.9 43.7 %feed_forward.4 = (bf16[512,1536]{1,0:T(8,128)(2,1)}, bf16[512,1536]{1,0:T(8,128)(2,1)}, bf16[512,1536]{1,0:T(8,128)(2,1)}, bf16[512,1536]{1,0:T(8,128)(2,1)}, b...) custom-call(s32[7]{0:T(128)} %stack.62.refs_0_, bf16[512,1536]{1,0:T(8,128)(2,1)} %get-tuple-element.131.refs_0_.refs_1_, ...), custom_call_target="tpu_custom_call" | custom-call | flops 41400000512 | tf_op jit(solution)/shard_map/feed_forward/pallas_call | solution.py:439
  424.6 7.3 collective-permute-done.9
  431.9 6.3 fold.12
  438.7 44.5 %feed_forward.5 = (bf16[512,1536]{1,0:T(8,128)(2,1)}, bf16[512,1536]{1,0:T(8,128)(2,1)}, bf16[512,1536]{1,0:T(8,128)(2,1)}, bf16[512,1536]{1,0:T(8,128)(2,1)}, b...) custom-call(s32[7]{0:T(128)} %stack.62.refs_0_, bf16[512,1536]{1,0:T(8,128)(2,1)} %get-tuple-element.131.refs_0_.refs_1_, ...), custom_call_target="tpu_custom_call" | custom-call | flops 41400000512 | tf_op jit(solution)/shard_map/feed_forward/pallas_call | solution.py:439
  483.2 1.4 copy-done.2
  484.9 2.1 collective-permute-start.11
  487.0 4.3 fold.13
  491.3 2.3 collective-permute-start.14
  493.6 7.3 fold.14
  501.0 21.2 %collective-permute-done.11.refs_2_.refs_1_ = bf16[512,1536]{1,0:T(8,128)(2,1)} collective-permute-done((bf16[512,1536]{1,0:T(8,128)(2,1)}, bf16[512,1536]{1,0:T(8,128)(2,1)}, u32[]{:S(2)}, u32[]{:S(2)}) %collective-permute-start.11) | collective-permute-done | bytes 1572896 | tf_op jit(solution)/shard_map/ppermute | solution.py:1546
  522.1 1.7 collective-permute-start.17
  523.9 2.3 collective-permute-start.16
  526.2 34.7 %middle_backward.1 = (f32[512,1536]{1,0:T(8,128)}, bf16[512,1536]{1,0:T(8,128)(2,1)}, bf16[512,1536]{1,0:T(8,128)(2,1)}, bf16[144,1536]{1,0:T(8,128)(2,1)}, bf16...) custom-call(s32[7]{0:T(128)} %stack.62.refs_0_, ...), custom_call_target="tpu_custom_call" | custom-call | flops 46000001024 | tf_op jit(solution)/shard_map/middle_backward/pallas_call | solution.py:439
  561.2 21.5 %middle_weights.1 = (bf16[2,2,768,768]{3,2,1,0:T(8,128)(2,1)}, bf16[2,2,768,768]{3,2,1,0:T(8,128)(2,1)}, bf16[2,2,768,768]{3,2,1,0:T(8,128)(2,1)}, bf16[2,2,768,768]{3,2,1,0:T(8,128)(2,1)}, f32[144,768]{1,0:T(8,128)}) custom-call(s32[7]{0:T(128)} %stack.62.refs_0_, bf16[512,1536]{1,0:T(8,128)(2,1)} %get-tuple-element.163.refs_1_, ...), custom_call_target="tpu_custom_call" | custom-call | flops 5750000128 | tf_op jit(solution)/shard_map/middle_weights/pallas_call | solution.py:439
  587.2 3.4 fold.15
  591.3 4.2 fold.16
  595.5 2.0 collective-permute-start.19
  597.6 4.7 fold.17
  602.2 26.6 %self_backward.2 = (bf16[2,768,384]{2,1,0:T(8,128)(2,1)}, bf16[2,768,384]{2,1,0:T(8,128)(2,1)}, f32[1024,1536]{1,0:T(8,128)}) custom-call(s32[7]{0:T(128)} %stack.62.refs_0_, bf16[1024,768]{1,0:T(8,128)(2,1)} %get-tuple-element.115.refs_1_, bf16[1024,768]{1,0:T(8,128)(2,1)} %get-tuple-element.116.refs_2_, bf16[1024,768]{1,0:T(8,128)(2,1)} %get-tuple-element.117.refs_3_, ...), custom_call_target="tpu_custom_call" | custom-call | flops 29899999232 | tf_op jit(solution)/shard_map/self_backward/pallas_call | solution.py:439
  628.9 7.8 collective-permute-done.19
  636.7 1.0 copy-done.5
  638.1 1.0 slice.32
  639.9 1.9 rev.7
  642.5 1.8 collective-permute-start.27
  644.3 7.0 fold.21
  651.3 6.9 fold.20
  658.9 3.4 fold.19
  662.4 3.6 fold.18
  665.9 2.9 collective-permute-start.26
  668.9 1.0 bitcast_add_fusion
  669.9 2.1 collective-permute-start.28
  672.0 47.3 %self_backward.3 = (bf16[2,768,768]{2,1,0:T(8,128)(2,1)}, bf16[2,768,768]{2,1,0:T(8,128)(2,1)}, bf16[512,1536]{1,0:T(8,128)(2,1)}, bf16[512,1536]{1,0:T(8,128)(2,1)}) custom-call(s32[7]{0:T(128)} %stack.62.refs_0_, bf16[1024,768]{1,0:T(8,128)(2,1)} %get-tuple-element.115.refs_1_, bf16[1024,768]{1,0:T(8,128)(2,1)} %get-tuple-element.116.refs_2_, ...), custom_call_target="tpu_custom_call" | custom-call | flops 59799998464 | tf_op jit(solution)/shard_map/self_backward/pallas_call | solution.py:439
  721.7 107.3 %scatter_last.1 = (bf16[512,1536]{1,0:T(8,128)(2,1)}, f32[512,1536]{1,0:T(8,128)}, f32[192,384]{1,0:T(8,128)}, f32[192,384]{1,0:T(8,128)}, f32[192,384]{1,0:T(8,...) custom-call(bf16[512,1536]{1,0:T(8,128)(2,1)} %hold.42.their_dx_ref,, ...), custom_call_target="tpu_custom_call" | custom-call | tf_op jit(solution)/shard_map/scatter_last/pallas_call | solution.py:1524
  829.1 4.3 reshape.362
  835.3 1.1 copy.184
  836.4 1.3 copy-done.10
  837.8 1.7 copy.185
  842.6 1.0 copy.190
  (183 shorter events, 28.4 us)
Async XLA Ops:
  7.2 218.8 %copy-start = (bf16[2,130,768]{2,0,1:T(2,128)(2,1)S(1)}, bf16[2,130,768]{2,0,1:T(2,128)(2,1)}, u32[]{:S(2)}) copy-start(bf16[2,130,768]{2,0,1:T(2,128)(2,1)} %param.15) | copy-start | bytes 1198084
  7.2 3.3 copy-start.19
  7.2 308.2 %all-gather.5.cloned.1.call-start = ((), (), s32[]{:S(2)}) async-start(), calls=%async_computation | async-start | bytes 10027008 | tf_op jit(solution)/shard_map/all_gather | solution.py:1625
  9.3 2.4 copy-start.30
  10.5 2.6 copy-start.22
  10.5 2.6 copy-start.28
  10.5 2.5 copy-start.29
  12.3 1.7 copy-start.27
  177.0 5.4 copy-start.32
  177.1 202.8 %all-gather.7.cloned.1.call-start = ((), (), s32[]{:S(2)}) async-start(), calls=%async_computation.1 | async-start | bytes 10027008 | tf_op jit(solution)/shard_map/all_gather | solution.py:1625
  177.3 53.0 %collective-permute-start = (bf16[512,1536]{1,0:T(8,128)(2,1)}, bf16[512,1536]{1,0:T(8,128)(2,1)}, u32[]{:S(2)}, u32[]{:S(2)}) collective-permute-start(bf16[512,1536]{1,0:T(8,128)(2,1)} %get-tuple-element.120.refs_5_.refs_3_), channel_id=1, source_target_pairs={{0,1},{1,0},{2,3},{3,2},{4,5},{5,4},{6,7},{7,6},{8,9},{9,8},{10,11... | collective-permute-start | bytes 4718600 | tf_op jit(solution)/shard_map/ppermute | solution.py:1546
  178.9 48.9 %collective-permute-start.3 = (bf16[192,1536]{1,0:T(8,128)(2,1)}, bf16[192,1536]{1,0:T(8,128)(2,1)}, u32[]{:S(2)}, u32[]{:S(2)}) collective-permute-start(bf16[192,1536]{1,0:T(8,128)(2,1)} %hold.25), channel_id=1, source_target_pairs={{0,16},{4,20},{8,24},{12,28},{16,0},{20,4},{24,8},{28,12},{1,17},{... | collective-permute-start | bytes 1769480 | tf_op jit(solution)/shard_map/ppermute | solution.py:1546
  187.5 37.3 %copy-start.17 = (bf16[512,1536]{1,0:T(8,128)(2,1)S(1)}, bf16[512,1536]{1,0:T(8,128)(2,1)}, u32[]{:S(2)}) copy-start(bf16[512,1536]{1,0:T(8,128)(2,1)} %get-tuple-element.120.refs_5_.refs_3_) | copy-start | bytes 4718596
  224.8 2.9 copy-start.11
  230.0 65.2 %collective-permute-start.4 = (bf16[2,192,1536]{2,1,0:T(8,128)(2,1)}, bf16[2,192,1536]{2,1,0:T(8,128)(2,1)S(1)}, u32[]{:S(2)}, u32[]{:S(2)}) collective-permute-start(bf16[2,192,1536]{2,1,0:T(8,128)(2,1)} %hold.26), channel_id=1, source_target_pairs={{0,8},{4,12},{8,0},{12,4},{16,24},{20,28},{24,16},{28,20},{1,9},{5... | collective-permute-start | bytes 3538952 | tf_op jit(solution)/shard_map/ppermute | solution.py:1546
  230.3 19.4 %collective-permute-start.1 = (bf16[512,768]{1,0:T(8,128)(2,1)}, bf16[512,768]{1,0:T(8,128)(2,1)S(1)}, u32[]{:S(2)}, u32[]{:S(2)}) collective-permute-start(bf16[512,768]{1,0:T(8,128)(2,1)} %hold.22.refs_1_.refs_5_), channel_id=1, source_target_pairs={{0,1},{1,0},{2,3},{3,2},{4,5},{5,4},{6,7},{7,6},{8,9},{9,8},{10,11... | collective-permute-start | bytes 2359304 | tf_op jit(solution)/shard_map/ppermute | solution.py:1546
  249.7 0.9 copy-start.9
  250.6 44.7 %copy-start.7 = (bf16[2,192,1536]{2,1,0:T(8,128)(2,1)S(1)}, bf16[2,192,1536]{2,1,0:T(8,128)(2,1)}, u32[]{:S(2)}) copy-start(bf16[2,192,1536]{2,1,0:T(8,128)(2,1)} %hold.26) | copy-start | bytes 3538948
  276.9 35.5 %collective-permute-start.2 = (bf16[512,1536]{1,0:T(8,128)(2,1)}, bf16[512,1536]{1,0:T(8,128)(2,1)}, u32[]{:S(2)}, u32[]{:S(2)}) collective-permute-start(bf16[512,1536]{1,0:T(8,128)(2,1)} %get-tuple-element.131.refs_0_.refs_1_), channel_id=1, source_target_pairs={{0,1},{1,0},{2,3},{3,2},{4,5},{5,4},{6,7},{7,6},{8,9},{9,8},{10,11... | collective-permute-start | bytes 4718600 | tf_op jit(solution)/shard_map/ppermute | solution.py:1546
  357.7 8.3 collective-permute-start.8
  357.8 65.8 %collective-permute-start.5 = (bf16[4,192,1536]{2,1,0:T(8,128)(2,1)}, bf16[4,192,1536]{2,1,0:T(8,128)(2,1)}, u32[]{:S(2)}, u32[]{:S(2)}) collective-permute-start(bf16[4,192,1536]{2,1,0:T(8,128)(2,1)} %hold.28.refs_9_), channel_id=1, source_target_pairs={{0,2},{2,0},{1,3},{3,1},{4,6},{6,4},{5,7},{7,5},{8,10},{10,8},{9,1... | collective-permute-start | bytes 7077896 | tf_op jit(solution)/shard_map/ppermute | solution.py:1546
  423.6 8.3 collective-permute-start.9
  423.9 14.3 %collective-permute-start.6 = (bf16[4,192,1536]{2,1,0:T(8,128)(2,1)}, bf16[4,192,1536]{2,1,0:T(8,128)(2,1)}, u32[]{:S(2)}, u32[]{:S(2)}) collective-permute-start(bf16[4,192,1536]{2,1,0:T(8,128)(2,1)} %hold.28.refs_9_), channel_id=1, source_target_pairs={{0,4},{4,0},{8,12},{12,8},{16,20},{20,16},{24,28},{28,24},{1,5},{5... | collective-permute-start | bytes 7077896 | tf_op jit(solution)/shard_map/ppermute | solution.py:1546
  424.2 14.5 %collective-permute-start.7 = (bf16[4,192,1536]{2,1,0:T(8,128)(2,1)}, bf16[4,192,1536]{2,1,0:T(8,128)(2,1)}, u32[]{:S(2)}, u32[]{:S(2)}) collective-permute-start(bf16[4,192,1536]{2,1,0:T(8,128)(2,1)} %collective-permute-done.5.refs_1_.refs_10_), channel_id=1, source_target_pairs={{0,4},{4,0},{8,12},{12,8},{16,20},{20,16},{24,28},{28,24},{1,5},{5... | collective-permute-start | bytes 7077896 | tf_op jit(solution)/shard_map/ppermute | solution.py:1546
  424.5 58.8 %collective-permute-start.10 = (bf16[1,1,2,2,192,1536]{5,4,3,2,1,0:T(8,128)(2,1)}, bf16[1,1,2,2,192,1536]{5,4,3,2,1,0:T(8,128)(2,1)S(1)}, u32[]{:S(2)}, u32[]{:S(2)}) collective-permute-start(bf16[1,1,2,2,192,1536]{5,4,3,2,1,0:T(8,128)(2,1)} %hold.30), channel_id=1, source_target_pairs={{0,2},{2,0},{1,3},{3,1},{4,6},{6,4},{5,7},{7,5},{8,10},{10,8},{9,1... | collective-permute-start | bytes 7077896 | tf_op jit(solution)/shard_map/ppermute | solution.py:1546
  483.2 1.4 copy-start.2
  484.6 9.0 %collective-permute-start.12 = (bf16[2,768,1536]{2,1,0:T(8,128)(2,1)}, bf16[2,768,1536]{2,1,0:T(8,128)(2,1)}, u32[]{:S(2)}, u32[]{:S(2)}) collective-permute-start(bf16[2,768,1536]{2,1,0:T(8,128)(2,1)} %hold.32), channel_id=1, source_target_pairs={{0,4},{4,0},{8,12},{12,8},{16,20},{20,16},{24,28},{28,24},{1,5},{5... | collective-permute-start | bytes 14155784 | tf_op jit(solution)/shard_map/ppermute | solution.py:1546
  484.9 37.2 %collective-permute-start.11 = (bf16[512,1536]{1,0:T(8,128)(2,1)}, bf16[512,1536]{1,0:T(8,128)(2,1)}, u32[]{:S(2)}, u32[]{:S(2)}) collective-permute-start(bf16[512,1536]{1,0:T(8,128)(2,1)} %hold.31), channel_id=1, source_target_pairs={{0,1},{1,0},{2,3},{3,2},{4,5},{5,4},{6,7},{7,6},{8,9},{9,8},{10,11... | collective-permute-start | bytes 4718600 | tf_op jit(solution)/shard_map/ppermute | solution.py:1546
  491.3 91.4 %collective-permute-start.14 = (bf16[1,1,2,1,192,1536]{5,4,3,2,1,0:T(8,128)(2,1)}, bf16[1,1,2,1,192,1536]{5,4,3,2,1,0:T(8,128)(2,1)S(1)}, u32[]{:S(2)}, u32[]{:S(2)}) collective-permute-start(bf16[1,1,2,1,192,1536]{5,4,3,2,1,0:T(8,128)(2,1)} %bitcast.262), channel_id=1, source_target_pairs={{0,8},{4,12},{8,0},{12,4},{16,24},{20,28},{24,16},{28,20},{1,9},{5... | collective-permute-start | bytes 3538952 | tf_op jit(solution)/shard_map/ppermute | solution.py:1546
  493.6 89.1 %collective-permute-start.15 = (bf16[1,1,2,2,192,1536]{5,4,3,2,1,0:T(8,128)(2,1)}, bf16[1,1,2,2,192,1536]{5,4,3,2,1,0:T(8,128)(2,1)S(1)}, u32[]{:S(2)}, u32[]{:S(2)}) collective-permute-start(bf16[1,1,2,2,192,1536]{5,4,3,2,1,0:T(8,128)(2,1)} %hold.33), channel_id=1, source_target_pairs={{0,2},{2,0},{1,3},{3,1},{4,6},{6,4},{5,7},{7,5},{8,10},{10,8},{9,1... | collective-permute-start | bytes 7077896 | tf_op jit(solution)/shard_map/ppermute | solution.py:1546
  522.1 60.7 %collective-permute-start.17 = (bf16[512,1536]{1,0:T(8,128)(2,1)}, bf16[512,1536]{1,0:T(8,128)(2,1)}, u32[]{:S(2)}, u32[]{:S(2)}) collective-permute-start(bf16[512,1536]{1,0:T(8,128)(2,1)} %hold.34), channel_id=1, source_target_pairs={{0,1},{1,0},{2,3},{3,2},{4,5},{5,4},{6,7},{7,6},{8,9},{9,8},{10,11... | collective-permute-start | bytes 4718600 | tf_op jit(solution)/shard_map/ppermute | solution.py:1546
  523.9 58.9 %collective-permute-start.16 = (bf16[1,2,2,1,192,1536]{5,4,3,2,1,0:T(8,128)(2,1)}, bf16[1,2,2,1,192,1536]{5,4,3,2,1,0:T(8,128)(2,1)}, u32[]{:S(2)}, u32[]{:S(2)}) collective-permute-start(bf16[1,2,2,1,192,1536]{5,4,3,2,1,0:T(8,128)(2,1)} %bitcast.261), channel_id=1, source_target_pairs={{0,8},{4,12},{8,0},{12,4},{16,24},{20,28},{24,16},{28,20},{1,9},{5... | collective-permute-start | bytes 7077896 | tf_op jit(solution)/shard_map/ppermute | solution.py:1546
  560.9 21.9 %collective-permute-start.13 = (bf16[512,768]{1,0:T(8,128)(2,1)}, bf16[512,768]{1,0:T(8,128)(2,1)}, u32[]{:S(2)}, u32[]{:S(2)}) collective-permute-start(bf16[512,768]{1,0:T(8,128)(2,1)} %get-tuple-element.161), channel_id=1, source_target_pairs={{0,1},{1,0},{2,3},{3,2},{4,5},{5,4},{6,7},{7,6},{8,9},{9,8},{10,11... | collective-permute-start | bytes 2359304 | tf_op jit(solution)/shard_map/ppermute | solution.py:1546
  582.8 1.0 copy-start.4
  582.8 1.8 copy-start.3
  584.5 52.1 %collective-permute-start.22 = (bf16[2,2,768,768]{3,2,1,0:T(8,128)(2,1)}, bf16[2,2,768,768]{3,2,1,0:T(8,128)(2,1)}, u32[]{:S(2)}, u32[]{:S(2)}) collective-permute-start(bf16[2,2,768,768]{3,2,1,0:T(8,128)(2,1)} %hold.36), channel_id=1, source_target_pairs={{0,4},{4,0},{8,12},{12,8},{16,20},{20,16},{24,28},{28,24},{1,5},{5... | collective-permute-start | bytes 14155784 | tf_op jit(solution)/shard_map/ppermute | solution.py:1546
  584.6 1.0 copy-start.16
  584.6 52.1 %collective-permute-start.21 = (bf16[2,2,768,768]{3,2,1,0:T(8,128)(2,1)}, bf16[2,2,768,768]{3,2,1,0:T(8,128)(2,1)}, u32[]{:S(2)}, u32[]{:S(2)}) collective-permute-start(bf16[2,2,768,768]{3,2,1,0:T(8,128)(2,1)} %hold.35.refs_15_), channel_id=1, source_target_pairs={{0,4},{4,0},{8,12},{12,8},{16,20},{20,16},{24,28},{28,24},{1,5},{5... | collective-permute-start | bytes 14155784 | tf_op jit(solution)/shard_map/ppermute | solution.py:1546
  590.6 38.3 %collective-permute-start.18 = (bf16[1,1,1,1,192,1536]{5,4,3,2,1,0:T(8,128)(2,1)}, bf16[1,1,1,1,192,1536]{5,4,3,2,1,0:T(8,128)(2,1)S(1)}, u32[]{:S(2)}, u32[]{:S(2)}) collective-permute-start(bf16[1,1,1,1,192,1536]{5,4,3,2,1,0:T(8,128)(2,1)} %bitcast.267), channel_id=1, source_target_pairs={{0,16},{4,20},{8,24},{12,28},{16,0},{20,4},{24,8},{28,12},{1,17},{... | collective-permute-start | bytes 1769480 | tf_op jit(solution)/shard_map/ppermute | solution.py:1546
  595.5 41.1 %collective-permute-start.19 = (bf16[1,1,2,1,192,1536]{5,4,2,3,1,0:T(8,128)(2,1)}, bf16[1,1,2,1,192,1536]{5,4,2,3,1,0:T(8,128)(2,1)S(1)}, u32[]{:S(2)}, u32[]{:S(2)}) collective-permute-start(bf16[1,1,2,1,192,1536]{5,4,2,3,1,0:T(8,128)(2,1)} %bitcast.263), channel_id=1, source_target_pairs={{0,8},{4,12},{8,0},{12,4},{16,24},{20,28},{24,16},{28,20},{1,9},{5... | collective-permute-start | bytes 3538952 | tf_op jit(solution)/shard_map/ppermute | solution.py:1546
  602.2 34.4 %collective-permute-start.20 = (bf16[1,1,2,1,192,1536]{5,4,2,3,1,0:T(8,128)(2,1)}, bf16[1,1,2,1,192,1536]{5,4,2,3,1,0:T(8,128)(2,1)S(1)}, u32[]{:S(2)}, u32[]{:S(2)}) collective-permute-start(bf16[1,1,2,1,192,1536]{5,4,2,3,1,0:T(8,128)(2,1)} %bitcast.264), channel_id=1, source_target_pairs={{0,2},{2,0},{1,3},{3,1},{4,6},{6,4},{5,7},{7,5},{8,10},{10,8},{9,1... | collective-permute-start | bytes 3538952 | tf_op jit(solution)/shard_map/ppermute | solution.py:1546
  628.9 7.8 copy-start.12
  636.7 1.0 copy-start.5
  636.7 1.5 copy-start.6
  642.5 1.9 copy-start.14
  642.5 26.4 %collective-permute-start.27 = (f32[130,2,192]{2,0,1:T(8,128)S(1)}, f32[130,2,192]{2,0,1:T(8,128)}, u32[]{:S(2)}, u32[]{:S(2)}) collective-permute-start(f32[130,2,192]{2,0,1:T(8,128)S(1)} %dynamic-slice_bitcast_fusion), channel_id=1, source_target_pairs={{0,1},{1,0},{2,3},{3,2},{4,5},{5,4},{6,7},{7,6},{8,9},{9,8},{10,11... | collective-permute-start | bytes 599048 | tf_op jit(solution)/shard_map/ppermute | solution.py:1546
  651.3 68.9 %collective-permute-start.24 = (bf16[2,1,2,2,192,768]{5,4,3,2,0,1:T(8,128)(2,1)}, bf16[2,1,2,2,192,768]{5,4,3,2,0,1:T(8,128)(2,1)S(1)}, u32[]{:S(2)}, u32[]{:S(2)}) collective-permute-start(bf16[2,1,2,2,192,768]{5,4,3,2,0,1:T(8,128)(2,1)} %bitcast.259), channel_id=1, source_target_pairs={{0,2},{2,0},{1,3},{3,1},{4,6},{6,4},{5,7},{7,5},{8,10},{10,8},{9,1... | collective-permute-start | bytes 7077896 | tf_op jit(solution)/shard_map/ppermute | solution.py:1546
  658.3 61.9 %collective-permute-start.23 = (bf16[1,2,2,2,192,768]{5,4,3,2,1,0:T(8,128)(2,1)}, bf16[1,2,2,2,192,768]{5,4,3,2,1,0:T(8,128)(2,1)}, u32[]{:S(2)}, u32[]{:S(2)}) collective-permute-start(bf16[1,2,2,2,192,768]{5,4,3,2,1,0:T(8,128)(2,1)} %bitcast.260), channel_id=1, source_target_pairs={{0,1},{1,0},{2,3},{3,2},{4,5},{5,4},{6,7},{7,6},{8,9},{9,8},{10,11... | collective-permute-start | bytes 7077896 | tf_op jit(solution)/shard_map/ppermute | solution.py:1546
  662.4 57.8 %collective-permute-start.25 = (bf16[1,1,1,1,192,1536]{5,4,3,2,1,0:T(8,128)(2,1)}, bf16[1,1,1,1,192,1536]{5,4,3,2,1,0:T(8,128)(2,1)S(1)}, u32[]{:S(2)}, u32[]{:S(2)}) collective-permute-start(bf16[1,1,1,1,192,1536]{5,4,3,2,1,0:T(8,128)(2,1)} %bitcast.266), channel_id=1, source_target_pairs={{0,16},{4,20},{8,24},{12,28},{16,0},{20,4},{24,8},{28,12},{1,17},{... | collective-permute-start | bytes 1769480 | tf_op jit(solution)/shard_map/ppermute | solution.py:1546
  662.4 6.5 copy-start.15
  665.9 55.8 %collective-permute-start.26 = (bf16[1,1,1,1,192,1536]{5,4,3,2,1,0:T(8,128)(2,1)}, bf16[1,1,1,1,192,1536]{5,4,3,2,1,0:T(8,128)(2,1)}, u32[]{:S(2)}, u32[]{:S(2)}) collective-permute-start(bf16[1,1,1,1,192,1536]{5,4,3,2,1,0:T(8,128)(2,1)} %bitcast.265), channel_id=1, source_target_pairs={{0,16},{4,20},{8,24},{12,28},{16,0},{20,4},{24,8},{28,12},{1,17},{... | collective-permute-start | bytes 1769480 | tf_op jit(solution)/shard_map/ppermute | solution.py:1546
  669.9 49.4 %collective-permute-start.28 = (f32[130,192]{1,0:T(8,128)S(1)}, f32[130,192]{1,0:T(8,128)S(1)}, u32[]{:S(2)}, u32[]{:S(2)}) collective-permute-start(f32[130,192]{1,0:T(8,128)S(1)} %dynamic-slice_bitcast_fusion.1), channel_id=1, source_target_pairs={{0,2},{2,0},{1,3},{3,1},{4,6},{6,4},{5,7},{7,5},{8,10},{10,8},{9,1... | collective-permute-start | bytes 299528 | tf_op jit(solution)/shard_map/ppermute | solution.py:1546
  720.2 0.8 copy-start.13
  720.2 1.6 copy-start.8
  829.1 4.4 copy-start.26
  829.1 5.3 copy-start.31
  829.1 6.2 copy-start.18
  835.3 2.5 copy-start.10
  837.7 1.8 copy-start.21
  837.8 2.7 copy-start.25
  839.5 1.6 copy-start.24
  839.5 2.4 copy-start.23
  839.5 3.1 copy-start.20
  841.2 2.5 copy-start.1
  (3 other events, 2.0 us)
Sparse Core Ops, SparseCore 0:
  177.2 116.7 all-gather.4
  296.3 83.5 all-gather.6
